TPU v7x, 32 devices: a whole 2x2x4 slice. The times are simulated.
32 devices in a mesh: ctx: 4 (over y, x), ch: 8 (over z, core).
Axes of the slice: x: 2, y: 2, z: 4, core: 2. Of those that a mesh axis runs over, the one named last changes fastest.
Arguments:
- proj: bfloat16 [3, 4096, 1024], P(None, 'ch', 'ctx'), may hold values from -4 to 4
- scale_exp: int32 [3, 4096, 8], P(None, 'ch', 'ctx'), may hold values from -1 to 1
- filt: bfloat16 [4096, 1024], P('ch'), may hold values from -8 to 8
- reach: int32 [4096], P('ch'), may hold values from 0 to 4
- skip: float32 [4096], P('ch'), may hold values from 0.1 to 1.9
- cotangent: bfloat16 [4096, 1024], P('ch', 'ctx'), may hold values from -6 to 6
Outputs:
- scaled_out: bfloat16 [4096, 1024], P('ch', 'ctx')
- token_max: float32 [1024], P('ctx')
- gradients: bfloat16 [3, 4096, 1024], P(None, 'ch', 'ctx')
- filter_grad: float32 [4096, 1024], P('ch', 'ctx')
All inputs are finite; a program needn't handle non-finite values. Where the computation divides by a largest or mean magnitude, that divisor is 1e-20 or more.
Results may differ from a plain program's by a relative error of at most 0.015.
Values may be sent and summed in bfloat16 or wider, within the bound.
No kernel may reach another device: no remote copies, remote signals or barrier semaphores. Data moves between devices by JAX's collectives and lax.ppermute only.
A program may use at most 64 MiB of HBM per device.

v0:
```python
import math

import jax
import jax.numpy as jnp
from jax import lax
from jax.sharding import PartitionSpec as P

REACH_DIVISORS = (64, 32, 16, 4, 1)


def fourier_basis(span_len):
    freq_index = jnp.arange(span_len, dtype=jnp.int32)
    phase = (2 * freq_index[None, :] + 1) * freq_index[:, None] % (4 * span_len)
    angle = phase.astype(jnp.float32) * (math.pi / (2 * span_len))
    return jnp.concatenate([jnp.cos(angle), -jnp.sin(angle)], axis=1)


def to_spectrum(signal, basis):
    return jnp.einsum("...s,sf->...f", signal, basis, precision=lax.Precision.HIGHEST)


def from_spectrum(spectrum, basis):
    return (
        jnp.einsum("...f,sf->...s", spectrum, basis, precision=lax.Precision.HIGHEST)
        / basis.shape[0]
    )


def blocks_spectrum(signal, basis, channels, blocks_in, span_len):
    shaped = signal.reshape(channels, blocks_in, span_len)
    return jnp.einsum("cks,sf->kcf", shaped, basis, precision=lax.Precision.HIGHEST)


def complex_mul(first_op, second_op):
    half_len = first_op.shape[-1] // 2
    real_a = first_op[..., :half_len]
    imag_a = first_op[..., half_len:]
    real_b = second_op[..., :half_len]
    imag_b = second_op[..., half_len:]
    return jnp.concatenate(
        [real_a * real_b - imag_a * imag_b, real_a * imag_b + imag_a * real_b], axis=-1
    )


def conjugate(spectrum):
    half_len = spectrum.shape[-1] // 2
    return jnp.concatenate([spectrum[..., :half_len], -spectrum[..., half_len:]], axis=-1)


def rotate(spectrum, parity):
    half_len = spectrum.shape[-1] // 2
    return jnp.concatenate(
        [spectrum[..., half_len:] * parity, -spectrum[..., :half_len] * parity], axis=-1
    )


def unrotate(spectrum, parity):
    half_len = spectrum.shape[-1] // 2
    return jnp.concatenate(
        [-spectrum[..., half_len:] * parity, spectrum[..., :half_len] * parity], axis=-1
    )


def body(proj, scale_exp, filt, reach, skip, cotangent):
    groups, channels, span_len = proj.shape
    ctx_count = lax.axis_size("ctx")
    ctx_index = lax.axis_index("ctx")
    seq_len = ctx_count * span_len
    blocks_per = scale_exp.shape[2]
    block_len = span_len // blocks_per
    scaled = jnp.exp2(scale_exp.astype(jnp.float32))
    dequant = (
        proj.astype(jnp.float32).reshape(groups, channels, blocks_per, block_len)
        * scaled[..., None]
    ).reshape(groups, channels, span_len)
    queries = dequant[0]
    keys_deq = dequant[1]
    values_deq = dequant[2]
    mixed_bf = (keys_deq * values_deq).astype(jnp.bfloat16)
    mixed_f = lax.optimization_barrier(mixed_bf).astype(jnp.float32)
    basis = fourier_basis(span_len)
    parity = 1.0 - 2.0 * (jnp.arange(span_len, dtype=jnp.int32) % 2).astype(jnp.float32)
    divisors = jnp.array(REACH_DIVISORS, dtype=jnp.int32)
    class_ids = jnp.arange(len(REACH_DIVISORS), dtype=jnp.int32)
    reach_div = jnp.sum(
        jnp.where(reach[:, None] == class_ids[None, :], divisors[None, :], 0), axis=1
    )
    reach_len = seq_len // reach_div
    fscale = 1.0 / math.sqrt(seq_len)
    tap_index = jnp.arange(seq_len, dtype=jnp.int32)
    kernel = (
        filt.astype(jnp.float32)
        * fscale
        * (tap_index[None, :] < reach_len[:, None]).astype(jnp.float32)
    )
    block_spec = blocks_spectrum(kernel, basis, channels, ctx_count, span_len)
    empty = jnp.zeros((1, channels, 2 * span_len), jnp.float32)
    window = jnp.concatenate([empty, block_spec[:-1]], axis=0) + rotate(block_spec, parity)
    zeros_all = jnp.zeros_like(window)
    ahead_win = lax.dynamic_slice_in_dim(
        jnp.concatenate([zeros_all, window], axis=0), ctx_count - ctx_index, ctx_count, 0
    )
    own_spec = to_spectrum(mixed_f, basis)
    pieces = from_spectrum(unrotate(complex_mul(own_spec[None], ahead_win), parity), basis)
    received = lax.all_to_all(pieces, "ctx", split_axis=0, concat_axis=0, tiled=True)
    conv_out = jnp.sum(received, axis=0) + skip[:, None] * mixed_f
    response = queries * conv_out
    local_peak = jnp.max(jnp.abs(response), axis=0)
    token_max = lax.pmax(local_peak, "ch")
    scaled_out = (response / (token_max + 1e-06)[None, :]).astype(jnp.bfloat16)
    upstream = cotangent.astype(jnp.float32)
    pulled_bf = (upstream * queries).astype(jnp.bfloat16)
    pulled = lax.optimization_barrier(pulled_bf).astype(jnp.float32)
    shard_piece = lax.all_gather(pulled_bf, "ctx", axis=1, tiled=True)
    blocks_in = shard_piece.shape[1] // span_len
    later_spec = blocks_spectrum(
        shard_piece.astype(jnp.float32), basis, channels, blocks_in, span_len
    )
    back_spec = jnp.sum(complex_mul(rotate(later_spec, parity), conjugate(ahead_win)), axis=0)
    grad_mixed = from_spectrum(back_spec, basis) + skip[:, None] * pulled
    gradients = jnp.stack(
        [upstream * conv_out, grad_mixed * values_deq, grad_mixed * keys_deq]
    ).astype(jnp.bfloat16)
    padded_later = jnp.concatenate([later_spec, jnp.zeros_like(later_spec)], axis=0)
    near_spec = lax.dynamic_slice_in_dim(padded_later, ctx_index, ctx_count, 0)
    next_spec = lax.dynamic_slice_in_dim(padded_later, ctx_index + 1, ctx_count, 0)
    near_plus = near_spec + rotate(next_spec, parity)
    tap_spec = complex_mul(conjugate(own_spec)[None], near_plus)
    own_taps = lax.psum_scatter(
        from_spectrum(tap_spec, basis).astype(jnp.bfloat16), "ctx", scatter_dimension=0, tiled=True
    ).astype(jnp.float32)[0]
    own_reach = (ctx_index * span_len + jnp.arange(span_len, dtype=jnp.int32))[None, :] < reach_len[
        :, None
    ]
    filter_grad = own_taps * fscale * own_reach.astype(jnp.float32)
    return (scaled_out, token_max, gradients, filter_grad)


def solution(mesh):
    return jax.shard_map(
        body,
        mesh=mesh,
        in_specs=(
            P(None, "ch", "ctx"),
            P(None, "ch", "ctx"),
            P("ch", None),
            P("ch"),
            P("ch"),
            P("ch", "ctx"),
        ),
        out_specs=(P("ch", "ctx"), P("ctx"), P(None, "ch", "ctx"), P("ch", "ctx")),
        check_vma=False,
    )
```

profile of v0, /device:TPU:0, one launch (start us, length us, event | category | flops | bytes accessed | tf_op | source)
XLA Modules:
  0.0 116.9 jit_solution(12864700281912198398)
XLA Ops:
  7.2 2.0 %reshape.72 = f32[3,512,2,128]{3,2,1,0:T(2,128)S(1)} reshape(bf16[3,512,256]{2,1,0:T(8,128)(2,1)} %param.7) | data formatting | bytes 2359296 | tf_op jit(solution)/shard_map/reshape | solution.py:73
  9.3 0.3 copy.33
  9.6 1.9 %broadcast_multiply_fusion = f32[3,512,2,128]{3,2,1,0:T(2,128)S(1)} fusion(f32[3,512,2,128]{3,2,1,0:T(2,128)S(1)} %reshape.72, f32[3,512,2]{2,1,0:T(8,128)S(1)} %copy.33), kind=kLoop, calls=%fused_computation.43 | loop fusion | flops 393216 | bytes 3158016 | tf_op jit(solution)/shard_map/mul | solution.py:73
  11.7 0.8 copy-done.10
  12.5 0.8 fusion.23
  13.3 1.1 fusion.40
  14.7 1.6 %multiply_select_fusion = f32[512,1024]{1,0:T(8,128)S(1)} fusion(bf16[512,1024]{1,0:T(8,128)(2,1)} %param.9, s32[512]{0:T(512)S(1)} %add_select_fusion.1), kind=kLoop, calls=%fused_computation.36 | loop fusion | flops 2097152 | bytes 3147776 | tf_op jit(solution)/shard_map/mul | solution.py:92
  16.3 3.9 %convolution_bitcast_fusion.1 = f32[4,512,512]{1,2,0:T(8,128)S(1)} fusion(f32[64,4,8,256]{3,2,1,0:T(8,128)S(1)} %bitcast.73, f32[256,256]{0,1:T(8,128)S(1)} %get-tuple-element.30, f32[256,256]{0,1:T(8,128)S(1)} %get-tuple-element.29), kind=kOutput, calls=%fused_computation.17 | convolution fusion | flops 3221356544 | bytes 6815744 | tf_op jit(solution)/shard_map/cks,sf->kcf/dot_general | solution.py:31
  20.2 0.6 fusion.41
  20.9 1.3 %copy-done.1 = f32[4,512,512]{1,2,0:T(8,128)} copy-done((f32[4,512,512]{1,2,0:T(8,128)}, f32[4,512,512]{1,2,0:T(8,128)S(1)}, u32[]{:S(2)}) %copy-start.1) | copy-done | bytes 4194328
  22.3 2.1 %copy-done.2 = f32[4,512,512]{1,2,0:T(8,128)S(1)} copy-done((f32[4,512,512]{1,2,0:T(8,128)S(1)}, f32[4,512,512]{1,2,0:T(8,128)}, u32[]{:S(2)}) %copy-start.2) | copy-done | bytes 4194328
  24.5 0.9 slice_multiply_fusion.1
  25.4 1.0 slice-done
  26.4 3.0 %maximum_add_fusion = f32[4,512,512]{1,2,0:T(8,128)} fusion(f32[4,512,256]{1,2,0:T(8,128)S(1)} %get-tuple-element.15, f32[4,512,256]{1,2,0:T(8,128)S(1)} %get-tuple-element.14, f32[3,512,512]{1,2,0:T(8,128)S(1)} %slice-done), kind=kLoop, calls=%fused_computation.6 | loop fusion | flops 2097152 | bytes 11534336 | tf_op jit(solution)/shard_map/add | solution.py:98
  29.4 1.0 slice_bitcast_fusion.3
  30.4 1.1 slice_bitcast_fusion.1
  31.5 11.2 %all-gather.2.cloned.1.call-done = bf16[512,1024]{1,0:T(8,128)(2,1)} async-done(((bf16[512,256]{1,0:T(8,128)(2,1)}), bf16[512,1024]{1,0:T(8,128)(2,1)}) %all-gather.2.cloned.1.call-update) | async-done | bytes 1048592 | tf_op jit(solution)/shard_map/all_gather | solution.py:114
  42.6 1.5 %copy.37 = bf16[512,1024]{0,1:T(8,128)(2,1)S(1)} copy(bf16[512,1024]{1,0:T(8,128)(2,1)} %all-gather.2.cloned.1.call-done) | data formatting | bytes 2097152 | tf_op jit(solution)/shard_map/all_gather | solution.py:114
  44.1 1.9 %convolution_bitcast_fusion = f32[4,512,512]{1,2,0:T(8,128)S(1)} fusion(bf16[512,4,256]{0,2,1:T(8,128)(2,1)S(1)} %bitcast.81, f32[256,256]{0,1:T(8,128)S(1)} %get-tuple-element.30, f32[256,256]{0,1:T(8,128)S(1)} %get-tuple-element.29), kind=kOutput, calls=%fused_computation.16 | convolution fusion | flops 3221356544 | bytes 5767168 | tf_op jit(solution)/shard_map/cks,sf->kcf/dot_general | solution.py:31
  46.6 3.6 %multiply_subtract_fusion.1 = (f32[4,512,256]{1,2,0:T(8,128)S(1)}, f32[4,512,256]{1,2,0:T(8,128)}, f32[4,512,256]{1,2,0:T(8,128)}, f32[4,512,256]{1,2,0:T(8,128)...) fusion(f32[4,512,512]{1,2,0:T(8,128)S(1)} %convolution_bitcast_fusion, f32[256]{0:T(256)S(1)} %fusion.45, ...), kind=kLoop, calls=%fused_computation.33 | loop fusion | flops 12058624 | bytes 26215436 | tf_op jit(solution)/shard_map/sub | solution.py:41
  50.2 8.5 %fusion.18 = f32[4,512,256]{2,1,0:T(8,128)} fusion(f32[4,512,256]{1,2,0:T(8,128)S(1)} %get-tuple-element.11, f32[4,512,256]{1,2,0:T(8,128)S(1)} %get-tuple-element.12, f32[256,256]{0,1:T(8,128)S(1)} %get-tuple-element.30, f32[256,256]{0,1:T(8,128)S(1)} %get-tuple-element.29), kind=kOutput, calls=%fused_computation.38 | convolution fusion | flops 3222929408 | bytes 6815744 | tf_op jit(solution)/shard_map/...f,sf->...s/dot_general | solution.py:24
  58.6 4.5 %all-to-all-start = ((f32[4,512,256]{2,1,0:T(8,128)}), f32[4,512,256]{2,1,0:T(8,128)}, u32[]{:S(2)}, u32[]{:S(2)}) async-start(f32[4,512,256]{2,1,0:T(8,128)} %fusion.18), calls=%async_computation | async-start | bytes 4194304 | tf_op jit(solution)/shard_map/all_to_all | solution.py:105
  63.2 6.0 %fusion = (f32[4,512,512]{1,2,0:T(8,128)S(1)}, f32[512,512]{0,1:T(8,128)}) fusion(s32[]{:T(128)S(6)} %select_n.60, f32[4,512,512]{1,2,0:T(8,128)} %copy-done, f32[4,512,256]{1,2,0:T(8,128)} %get-tuple-element.13, f32[4,512,256]{1,2,0:T(8,128)} %get-tuple-element.10, f32[4,512,256]{1,2,0:T(8,128)} %get-tuple-element.5, f32[4,512,256]{1,2,0:T(8,128)S(1)} %get-tuple-element.4), kind=kLoop, calls=%fused_computation.5 | loop fusion | flops 3932160 | bytes 17825796 | tf_op jit(solution)/shard_map/add | solution.py:127
  69.2 0.6 multiply_subtract_fusion
  69.8 7.9 %multiply_convert_fusion = bf16[4,512,256]{2,1,0:T(8,128)(2,1)} fusion(f32[4,512,256]{1,2,0:T(8,128)S(1)} %get-tuple-element.9, f32[4,512,256]{1,2,0:T(8,128)S(1)} %get-tuple-element.8, f32[256,256]{0,1:T(8,128)S(1)} %get-tuple-element.30, f32[256,256]{0,1:T(8,128)S(1)} %get-tuple-element.29), kind=kOutput, calls=%fused_computation.29 | convolution fusion | flops 3223453696 | bytes 5767168 | tf_op jit(solution)/shard_map/...f,sf->...s/dot_general | solution.py:24
  77.8 3.5 %fusion.35 = (bf16[1,512,256]{2,1,0:T(8,128)(2,1)S(1)}, bf16[1,512,256]{2,1,0:T(8,128)(2,1)S(1)}) fusion(f32[64,8,2,128]{3,2,1,0:T(2,128)} %bitcast.78, f32[64,8,2,128]{3,2,1,0:T(2,128)} %bitcast.80, bf16[512,256]{1,0:T(8,128)(2,1)} %fusion.23, f32[512]{0:T(512)S(1)} %copy-done.12, f32[512,512]{0,1:T(8,128)} %get-tuple-element.32, ...), kind=kOutput, calls=%fused_computation.76 | convolution fusion | flops 806486016 | bytes 3409920 | tf_op jit(solution)/shard_map/...f,sf->...s/dot_general | solution.py:24
  81.3 9.4 %all-to-all-done = f32[4,512,256]{2,1,0:T(8,128)} async-done(((f32[4,512,256]{2,1,0:T(8,128)}), f32[4,512,256]{2,1,0:T(8,128)}, u32[]{:S(2)}, u32[]{:S(2)}) %all-to-all-start) | async-done | bytes 2097184 | tf_op jit(solution)/shard_map/all_to_all | solution.py:105
  90.6 1.9 %reduce_sum.28 = f32[512,256]{1,0:T(8,128)S(1)} reduce(f32[4,512,256]{2,1,0:T(8,128)} %all-to-all-done, f32[]{:T(128)} %constant.73.clone.1), dimensions={0}, to_apply=%region_1.2 | reduce | flops 393216 | bytes 2621444 | tf_op jit(solution)/shard_map/reduce_sum | solution.py:106
  92.6 13.6 %pmax.7 = f32[256]{0:T(256)S(1)} all-reduce(f32[256]{0:T(256)S(1)} %abs_reduce_fusion), channel_id=1, replica_groups=mesh['ctx'=4,'ch'=8] {'ch'}, use_global_device_ids=true, to_apply=%region_3.4 | all-reduce | flops 256 | bytes 2048 | tf_op jit(solution)/shard_map/pmax | solution.py:109
  106.2 0.9 fusion.36
  107.2 1.0 pad_maximum_fusion
  108.1 1.9 %bitcast_select_fusion = f32[512,256]{1,0:T(8,128)} fusion(bf16[1,512,256]{2,1,0:T(8,128)(2,1)} %reduce-scatter.4.cloned.1.call-done, s32[256]{0:T(256)S(1)} %iota_add_fusion, s32[512]{0:T(512)S(1)} %add_select_fusion.1), kind=kLoop, calls=%fused_computation.61 | loop fusion | flops 524288 | bytes 789504 | tf_op jit(solution)/shard_map/mul | solution.py:135
  (49 shorter events, 1.4 us)
Async XLA Ops:
  7.2 2.1 %copy-start.13 = (s32[3,512,2]{1,2,0:T(2,128)S(1)}, s32[3,512,2]{1,2,0:T(2,128)}, u32[]{:S(2)}) copy-start(s32[3,512,2]{1,2,0:T(2,128)} %param.8) | copy-start | bytes 36868
  7.2 35.4 %all-gather.2.cloned.1.call-start = ((), (), s32[]{:S(2)}) async-start(), calls=%async_computation.2 | async-start | bytes 1310720 | tf_op jit(solution)/shard_map/all_gather | solution.py:114
  11.5 1.0 copy-start.10
  11.5 2.9 %copy-start.15 = (s32[512]{0:T(512)S(1)}, s32[512]{0:T(512)}, u32[]{:S(2)}) copy-start(s32[512]{0:T(512)} %param.10) | copy-start | bytes 6148
  11.5 2.9 %copy-start.16 = (s32[5]{0:T(128)S(1)}, s32[5]{0:T(128)}, u32[]{:S(2)}) copy-start(s32[5]{0:T(128)} %constant.85.clone) | copy-start | bytes 64
  11.7 4.6 %copy-start.4 = (f32[1,512,2,128]{3,2,1,0:T(2,128)}, f32[1,512,2,128]{3,2,1,0:T(2,128)S(1)}, u32[]{:S(2)}) copy-start(f32[1,512,2,128]{3,2,1,0:T(2,128)S(1)} %get-tuple-element.17) | copy-start | bytes 1572868
  11.7 4.6 %copy-start.5 = (f32[1,512,2,128]{3,2,1,0:T(2,128)}, f32[1,512,2,128]{3,2,1,0:T(2,128)S(1)}, u32[]{:S(2)}) copy-start(f32[1,512,2,128]{3,2,1,0:T(2,128)S(1)} %get-tuple-element.18) | copy-start | bytes 1572868
  20.2 1.9 %copy-start.1 = (f32[4,512,512]{1,2,0:T(8,128)}, f32[4,512,512]{1,2,0:T(8,128)S(1)}, u32[]{:S(2)}) copy-start(f32[4,512,512]{1,2,0:T(8,128)S(1)} %convolution_bitcast_fusion.1) | copy-start | bytes 12582916
  22.2 2.3 %copy-start.2 = (f32[4,512,512]{1,2,0:T(8,128)S(1)}, f32[4,512,512]{1,2,0:T(8,128)}, u32[]{:S(2)}) copy-start(f32[4,512,512]{1,2,0:T(8,128)} %copy-done.1) | copy-start | bytes 12582916
  24.5 1.9 %slice-start = ((f32[4,512,512]{1,2,0:T(8,128)}), f32[3,512,512]{1,2,0:T(8,128)S(1)}, s32[]{:S(2)}) async-start(f32[4,512,512]{1,2,0:T(8,128)} %copy-done.1), calls=%async_computation.4 | async-start | bytes 6291456 | tf_op jit(solution)/shard_map/slice | solution.py:98
  44.1 2.2 %copy-start.3 = (f32[4,512,512]{1,2,0:T(8,128)S(1)}, f32[4,512,512]{1,2,0:T(8,128)}, u32[]{:S(2)}) copy-start(f32[4,512,512]{1,2,0:T(8,128)} %maximum_add_fusion) | copy-start | bytes 12582916
  44.1 2.3 %copy-start.8 = (f32[512,256]{0,1:T(8,128)S(1)}, f32[512,256]{0,1:T(8,128)}, u32[]{:S(2)}) copy-start(f32[512,256]{0,1:T(8,128)} %get-tuple-element.23) | copy-start | bytes 1572868
  44.1 2.4 %copy-start.9 = (f32[512,256]{0,1:T(8,128)S(1)}, f32[512,256]{0,1:T(8,128)}, u32[]{:S(2)}) copy-start(f32[512,256]{0,1:T(8,128)} %get-tuple-element.24) | copy-start | bytes 1572868
  46.1 4.1 %copy-start = (f32[4,512,512]{1,2,0:T(8,128)}, f32[4,512,512]{1,2,0:T(8,128)S(1)}, u32[]{:S(2)}) copy-start(f32[4,512,512]{1,2,0:T(8,128)S(1)} %convolution_bitcast_fusion) | copy-start | bytes 12582916
  58.6 32.0 %all-to-all-start = ((f32[4,512,256]{2,1,0:T(8,128)}), f32[4,512,256]{2,1,0:T(8,128)}, u32[]{:S(2)}, u32[]{:S(2)}) async-start(f32[4,512,256]{2,1,0:T(8,128)} %fusion.18), calls=%async_computation | async-start | bytes 4194304 | tf_op jit(solution)/shard_map/all_to_all | solution.py:105
  63.1 45.0 %reduce-scatter.4.cloned.1.call-start = ((), (), s32[]{:S(2)}) async-start(), calls=%async_computation.3 | async-start | bytes 1310720
  63.2 6.0 %copy-start.6 = (f32[512,256]{0,1:T(8,128)S(1)}, f32[512,256]{0,1:T(8,128)}, u32[]{:S(2)}) copy-start(f32[512,256]{0,1:T(8,128)} %get-tuple-element.19) | copy-start | bytes 1572868
  63.2 6.0 %copy-start.7 = (f32[512,256]{0,1:T(8,128)S(1)}, f32[512,256]{0,1:T(8,128)}, u32[]{:S(2)}) copy-start(f32[512,256]{0,1:T(8,128)} %get-tuple-element.20) | copy-start | bytes 1572868
  69.8 8.0 %copy-start.12 = (f32[512]{0:T(512)S(1)}, f32[512]{0:T(512)}, u32[]{:S(2)}) copy-start(f32[512]{0:T(512)} %param.11) | copy-start | bytes 6148
  81.2 25.0 %copy-start.11 = (bf16[512,256]{1,0:T(8,128)(2,1)S(1)}, bf16[512,256]{1,0:T(8,128)(2,1)}, u32[]{:S(2)}) copy-start(bf16[512,256]{1,0:T(8,128)(2,1)} %param.12) | copy-start | bytes 786436
  106.2 3.8 %copy-start.14 = (f32[256]{0:T(256)}, f32[256]{0:T(256)S(1)}, u32[]{:S(2)}) copy-start(f32[256]{0:T(256)S(1)} %pmax.7) | copy-start | bytes 3076
Sparse Core Ops, SparseCore 0:
  13.4 29.1 all-gather.1
  77.9 29.2 reduce-scatter.3
where the time goes:
time: 117 us
  matrix products  26.3 us (22%)
  other arithmetic  25.8 us (22%)
  waiting for transfers between devices  20.5 us (18%)
  between operations  14.4 us (12%)
  blocking collectives  13.6 us (12%)
  local copies, waits for them, and re-layouts  11.7 us (10%)
  starting transfers between devices  4.53 us (4%)
    dot_general x3, matrix products, from_spectrum(): jnp.einsum('...f,sf->...s', spectrum, basis, precision=lax.Precision.HIGH...  19.8 us
    pmax x1, blocking collectives, body(): token_max = lax.pmax(local_peak, 'ch')  13.6 us
    all_gather x1, waiting for transfers between devices, body(): shard_piece = lax.all_gather(pulled_bf, 'ctx', axis=1, tiled=True)  11.2 us
    all_to_all x1, waiting for transfers between devices, body(): lax.all_to_all(pieces, 'ctx', split_axis=0, concat_axis=0, tiled=True)  9.35 us
    add x1, other arithmetic, body(): near_plus = near_spec + rotate(next_spec, parity)  5.98 us
    dot_general x2, matrix products, blocks_spectrum(): jnp.einsum('cks,sf->kcf', shaped, basis, precision=lax.Precision.HIGHEST)  5.82 us
    unnamed x34, local copies, waits for them, and re-layouts  4.78 us
    all_to_all x1, starting transfers between devices, body(): lax.all_to_all(pieces, 'ctx', split_axis=0, concat_axis=0, tiled=True)  4.45 us
  transfers between devices with their start and end apart: 3, of which 2 were waited for; matrix products, arithmetic and copies ran while one was open for 30% of the time, Pallas kernels for 0%

commit v1 on v0

v1 whole, which is shorter than its diff:
```python
import functools
import math

import jax
import jax.numpy as jnp
import ml_dtypes
import numpy as np
from jax import lax
from jax.experimental import pallas as pl
from jax.experimental.pallas import tpu as pltpu
from jax.sharding import PartitionSpec as P

REACH_DIVISORS = (64, 32, 16, 4, 1)
F32 = jnp.float32
BF16 = jnp.bfloat16


def fourier_tables(span):
    freq = np.arange(span)
    time = np.arange(2 * span)
    phase = ((2 * freq[None, :] + 1) * time[:, None]) % (4 * span)
    angle = phase * (math.pi / (2 * span))
    forward = np.concatenate([np.cos(angle), -np.sin(angle)], axis=1)
    high = forward.astype(ml_dtypes.bfloat16)
    low = (forward - high.astype(np.float64)).astype(ml_dtypes.bfloat16)
    inverse = (forward.T / span).astype(ml_dtypes.bfloat16)
    return high, low, inverse


def mm(left, right):
    return lax.dot_general(left, right, (((1,), (0,)), ((), ())), preferred_element_type=F32)


def mm2(left, high, low):
    return mm(left, high) + mm(left, low)


def block_scale(exps, span):
    blocks = exps.shape[0]
    block_len = span // blocks
    col = lax.broadcasted_iota(jnp.int32, (blocks, span), 1)
    row = lax.broadcasted_iota(jnp.int32, (blocks, span), 0)
    onehot = jnp.where(col // block_len == row, 1.0, 0.0).astype(BF16)
    scale = jnp.exp2(exps.astype(F32)).astype(BF16)
    return lax.dot_general(scale, onehot, (((0,), (0,)), ((), ())), preferred_element_type=F32)


def column(row_ref):
    row = row_ref[...]
    return jnp.transpose(jnp.broadcast_to(row, (8, row.shape[1])))[:, 0:1]


def reach_lens(reach_ref, seq_len):
    cls = column(reach_ref)
    out = jnp.zeros_like(cls)
    for index, div in enumerate(REACH_DIVISORS):
        out = jnp.where(cls == index, seq_len // div, out)
    return out


def cmul_parts(first, second, half):
    ar, ai = first[:, :half], first[:, half:]
    br, bi = second[:, :half], second[:, half:]
    return ar, ai, br, bi


def prep_kernel(n, proj_ref, exp_ref, cot_ref, mixed_ref, pulled_ref, *send_refs):
    me = lax.axis_index("ctx")
    span = cot_ref.shape[1]
    exps = exp_ref[...]
    mixed = (
        proj_ref[1].astype(F32) * proj_ref[2].astype(F32) * block_scale(exps[1] + exps[2], span)
    ).astype(BF16)
    pulled = (cot_ref[...].astype(F32) * (proj_ref[0].astype(F32) * block_scale(exps[0], span))).astype(BF16)
    mixed_ref[...] = mixed
    pulled_ref[...] = pulled
    for bit, ref in enumerate(send_refs):
        later = lax.rem(lax.div(me, 2**bit), 2)

        @pl.when(later == 1)
        def _():
            ref[...] = pulled

        @pl.when(later == 0)
        def _():
            ref[...] = mixed


def windows_kernel(
    n, proj_ref, exp_ref, filt_ref, reach_ref, skip_ref, mixed_ref, pulled_ref, high_ref, low_ref,
    recv_ref, query_ref, base_ref, *rest
):
    win_refs, taps = rest[: n - 2], rest[n - 2]
    me = lax.axis_index("ctx")
    rows, seq_len = filt_ref.shape
    span = seq_len // n
    fscale = 1.0 / math.sqrt(seq_len)
    query_ref[...] = (proj_ref[...].astype(F32) * block_scale(exp_ref[...], span)).astype(BF16)
    lens = reach_lens(reach_ref, seq_len)
    taps[0] = jnp.zeros((rows, span), BF16)
    for b in range(n):
        lag = lax.broadcasted_iota(jnp.int32, (rows, span), 1) + b * span
        taps[b + 1] = jnp.where(lag < lens, filt_ref[:, b * span : (b + 1) * span].astype(F32), 0.0).astype(BF16)
    near = mm2(taps[1], high_ref[span:], low_ref[span:])
    near += (column(skip_ref) * (1.0 / fscale)) * high_ref[span : span + 1, :].astype(F32)
    wr, wi = near[:, :span], near[:, span:]
    own = mm2(mixed_ref[...], high_ref[:span], low_ref[:span])
    xr, xi = own[:, :span], own[:, span:]
    base_ref[0, :, :span] = xr * wr - xi * wi
    base_ref[0, :, span:] = xr * wi + xi * wr
    back = mm2(pulled_ref[...], high_ref[span:], low_ref[span:])
    xr, xi = back[:, :span], back[:, span:]
    base_ref[1, :, :span] = xr * wr + xi * wi
    base_ref[1, :, span:] = xi * wr - xr * wi
    for k in range(1, n):
        other = jnp.bitwise_xor(me, k)
        dist = jnp.abs(other - me)
        win = mm2(taps[dist], high_ref[:span], low_ref[:span]) + mm2(
            taps[dist + 1], high_ref[span:], low_ref[span:]
        )
        sign = jnp.where(other < me, 1.0, -1.0).astype(F32)
        wr, wi = win[:, :span], win[:, span:] * sign
        if k > 1:
            win_refs[k - 2][:, :span] = wr.astype(BF16)
            win_refs[k - 2][:, span:] = wi.astype(BF16)
            continue
        later = jnp.where(other > me, 1, 0)
        start = pl.multiple_of(later * span, span)
        spec = mm2(recv_ref[...], high_ref[pl.ds(start, span), :], low_ref[pl.ds(start, span), :])
        xr, xi = spec[:, :span], spec[:, span:]
        base_ref[later, :, :span] += xr * wr - xi * wi
        base_ref[later, :, span:] += xr * wi + xi * wr


def conv_kernel(n, seq_len, *refs):
    recv_refs, win_refs = refs[: n - 2], refs[n - 2 : 2 * n - 4]
    base_ref, query_ref, high_ref, inv_ref = refs[2 * n - 4 : 2 * n]
    resp_ref, conv_ref, back_ref, peak_ref, acc = refs[2 * n :]
    me = lax.axis_index("ctx")
    span = query_ref.shape[1]
    fscale = 1.0 / math.sqrt(seq_len)
    acc[...] = base_ref[...]
    for k in range(2, n):
        later = jnp.where(jnp.bitwise_xor(me, k) > me, 1, 0)
        start = pl.multiple_of(later * span, span)
        spec = mm(recv_refs[k - 2][...], high_ref[pl.ds(start, span), :])
        xr, xi = spec[:, :span], spec[:, span:]
        wr = win_refs[k - 2][:, :span].astype(F32)
        wi = win_refs[k - 2][:, span:].astype(F32)
        acc[later, :, :span] += xr * wr - xi * wi
        acc[later, :, span:] += xr * wi + xi * wr
    conv = mm(acc[0].astype(BF16), inv_ref[:, span:]) * fscale
    response = query_ref[...].astype(F32) * conv
    resp_ref[...] = response
    conv_ref[...] = conv
    back_ref[...] = acc[1].astype(BF16)
    peak = jnp.max(jnp.abs(response), axis=0, keepdims=True)

    @pl.when(pl.program_id(0) == 0)
    def _():
        peak_ref[...] = peak

    @pl.when(pl.program_id(0) > 0)
    def _():
        peak_ref[...] = jnp.maximum(peak_ref[...], peak)


def grad_kernel(seq_len, key_ref, value_ref, exp_ref, cot_ref, conv_ref, back_ref, inv_ref, grad_ref):
    span = cot_ref.shape[1]
    fscale = 1.0 / math.sqrt(seq_len)
    exps = exp_ref[...]
    grad_mixed = mm(back_ref[...], inv_ref[:, :span]) * fscale
    grad_ref[0] = (cot_ref[...].astype(F32) * conv_ref[...]).astype(BF16)
    grad_ref[1] = (grad_mixed * (value_ref[...].astype(F32) * block_scale(exps[2], span))).astype(BF16)
    grad_ref[2] = (grad_mixed * (key_ref[...].astype(F32) * block_scale(exps[1], span))).astype(BF16)


def taps_kernel(n, seq_len, mixed_ref, pulled_ref, reach_ref, high_ref, inv_ref, *refs):
    first_refs, second_refs = refs[: n - 1], refs[n - 1 : 2 * n - 2]
    out_refs, (mbuf, pbuf, mspec, pspec, acc) = refs[2 * n - 1 : 3 * n - 1], refs[3 * n - 1 :]
    me = lax.axis_index("ctx")
    _, rows, span = mbuf.shape
    fscale = 1.0 / math.sqrt(seq_len)
    mbuf[me] = mixed_ref[me]
    pbuf[me] = pulled_ref[me]
    pbuf[n] = jnp.zeros((rows, span), BF16)
    for k in range(1, n):
        other = jnp.bitwise_xor(me, k)

        @pl.when(other < me)
        def _():
            mbuf[other] = first_refs[k - 1][me]
            pbuf[other] = second_refs[k - 1][...]

        @pl.when(other > me)
        def _():
            pbuf[other] = first_refs[k - 1][me]
            mbuf[other] = second_refs[k - 1][...]

    if rows % 16 == 0:
        flat = (n * rows, span)
        mspec[...] = mm(mbuf[...].reshape(flat), high_ref[:span]).reshape(mspec.shape)
        pspec[...] = (
            mm(pbuf[:n].reshape(flat), high_ref[:span]) + mm(pbuf[1:].reshape(flat), high_ref[span:])
        ).reshape(pspec.shape)
    else:
        for b in range(n):
            mspec[b] = mm(mbuf[b], high_ref[:span])
            pspec[b] = mm(pbuf[b], high_ref[:span]) + mm(pbuf[b + 1], high_ref[span:])
    lens = reach_lens(reach_ref.at[me], seq_len)
    for k in range(n):
        lag_block = jnp.bitwise_xor(me, k)
        acc[...] = jnp.zeros_like(acc)
        for b in range(n):

            @pl.when(b + lag_block < n)
            def _():
                ar, ai = mspec[b, :, :span], mspec[b, :, span:]
                near = pspec[b + lag_block]
                br, bi = near[:, :span], near[:, span:]
                acc[:, :span] += ar * br + ai * bi
                acc[:, span:] += ar * bi - ai * br

        lag = lax.broadcasted_iota(jnp.int32, (rows, span), 1) + lag_block * span
        own = mm(acc[...].astype(BF16), inv_ref[:, :span]) * fscale
        out_refs[k][...] = jnp.where(lag < lens, own, 0.0).astype(BF16)


def pick_kernel(k, mixed_ref, pulled_ref, *refs):
    me = lax.axis_index("ctx")
    other = jnp.bitwise_xor(me, k)
    out_ref = refs[-1]

    @pl.when(other > me)
    def _():
        out_ref[...] = pulled_ref[other]

    @pl.when(other < me)
    def _():
        out_ref[...] = mixed_ref[other]


def spread_kernel(n, *refs):
    part_refs, out_ref = refs[:n], refs[n]
    me = lax.axis_index("ctx")
    for k in range(n):
        out_ref[jnp.bitwise_xor(me, k)] = part_refs[k][...].astype(F32)


def scale_kernel(resp_ref, near_ref, far_ref, out_ref, peak_ref):
    peak = jnp.maximum(near_ref[...], far_ref[...])
    peak_ref[...] = peak
    out_ref[...] = (resp_ref[...] / (peak + 1e-06)).astype(BF16)


def params(mib=40):
    return pltpu.CompilerParams(vmem_limit_bytes=mib * 2**20)


def body(proj, scale_exp, filt, reach, skip, cotangent):
    groups, channels, span = proj.shape
    n = lax.axis_size("ctx")
    ch_count = lax.axis_size("ch")
    seq_len = n * span
    blocks = scale_exp.shape[2]
    bits = max(1, (n - 1).bit_length())
    rows = 256 if channels % 256 == 0 else channels
    steps = channels // rows
    high, low, inverse = (jnp.asarray(t) for t in fourier_tables(span))
    exps = jnp.transpose(scale_exp, (0, 2, 1))
    reach_row = reach.reshape(1, channels)
    skip_row = skip.reshape(1, channels)

    tile = pl.BlockSpec((rows, span), lambda i: (i, 0))
    wide = pl.BlockSpec((rows, 2 * span), lambda i: (i, 0))
    line = pl.BlockSpec((1, rows), lambda i: (0, i))
    table = pl.BlockSpec((2 * span, 2 * span), lambda i: (0, 0))
    proj_all = pl.BlockSpec((3, rows, span), lambda i: (0, i, 0))
    exps_all = pl.BlockSpec((3, blocks, rows), lambda i: (0, 0, i))

    def shape(dims, dtype):
        return jax.ShapeDtypeStruct(dims, dtype)

    flat = shape((channels, span), BF16)
    mixed, pulled, *sends = pl.pallas_call(
        functools.partial(prep_kernel, n),
        grid=(steps,),
        in_specs=[proj_all, exps_all, tile],
        out_specs=[tile] * (2 + bits),
        out_shape=[flat] * (2 + bits),
        compiler_params=params(60),
        name="prep",
    )(proj, exps, cotangent)

    first = []
    for k in range(1, n):
        perm = [(j, j ^ k) for j in range(n)]
        first.append(lax.ppermute(sends[k.bit_length() - 1], "ctx", perm))
    me = lax.axis_index("ctx")
    share = channels // n
    shares = (n, share, span)
    part = shape((share, span), BF16)

    def pick(k, *after):
        return pl.pallas_call(
            functools.partial(pick_kernel, k),
            in_specs=[pl.BlockSpec(memory_space=pltpu.VMEM)] * 2 + [pl.BlockSpec(memory_space=pl.ANY)] * len(after),
            out_shape=part,
            compiler_params=params(),
            name="pick",
        )(mixed.reshape(shares), pulled.reshape(shares), *after)

    second = {k: lax.ppermute(pick(k), "ctx", [(j, j ^ k) for j in range(n)]) for k in range(2, n)}

    query, base, *wins = pl.pallas_call(
        functools.partial(windows_kernel, n),
        grid=(steps,),
        in_specs=[
            pl.BlockSpec((None, rows, span), lambda i: (0, i, 0)),
            pl.BlockSpec((None, blocks, rows), lambda i: (0, 0, i)),
            pl.BlockSpec((rows, seq_len), lambda i: (i, 0)),
            line, line, tile, tile, table, table, tile,
        ],
        out_specs=[tile, pl.BlockSpec((2, rows, 2 * span), lambda i: (0, i, 0))] + [wide] * (n - 2),
        out_shape=[flat, shape((2, channels, 2 * span), F32)] + [shape((channels, 2 * span), BF16)] * (n - 2),
        scratch_shapes=[pltpu.VMEM((n + 1, rows, span), BF16)],
        compiler_params=params(),
        name="windows",
    )(proj, exps, filt, reach_row, skip_row, mixed, pulled, high, low, first[0])
    second[1] = lax.ppermute(pick(1, first[0]), "ctx", [(j, j ^ 1) for j in range(n)])

    response, conv, back, peak = pl.pallas_call(
        functools.partial(conv_kernel, n, seq_len),
        grid=(steps,),
        in_specs=[tile] * (n - 2) + [wide] * (n - 2)
        + [pl.BlockSpec((2, rows, 2 * span), lambda i: (0, i, 0)), tile, table, table],
        out_specs=[tile, tile, wide, pl.BlockSpec((1, span), lambda i: (0, 0))],
        out_shape=[shape((channels, span), F32)] * 2
        + [shape((channels, 2 * span), BF16), shape((1, span), F32)],
        scratch_shapes=[pltpu.VMEM((2, rows, 2 * span), F32)],
        compiler_params=params(),
        name="conv",
    )(*first[1:], *wins, base, query, high, inverse)

    far = peak
    hop = 1
    while hop < ch_count:
        peak = jnp.maximum(peak, far)
        far = lax.ppermute(peak, "ch", [(j, j ^ hop) for j in range(ch_count)])
        hop *= 2
    single = pl.BlockSpec((1, span), lambda i: (0, 0))
    scaled_out, peak = pl.pallas_call(
        scale_kernel,
        grid=(steps,),
        in_specs=[tile, single, single],
        out_specs=[tile, single],
        out_shape=[flat, shape((1, span), F32)],
        compiler_params=params(),
        name="scale",
    )(response, peak, far)

    gradients = pl.pallas_call(
        functools.partial(grad_kernel, seq_len),
        grid=(steps,),
        in_specs=[
            pl.BlockSpec((None, rows, span), lambda i: (1, i, 0)),
            pl.BlockSpec((None, rows, span), lambda i: (2, i, 0)),
            exps_all, tile, tile, wide, table,
        ],
        out_specs=proj_all,
        out_shape=shape((3, channels, span), BF16),
        compiler_params=params(),
        name="grads",
    )(proj, proj, exps, cotangent, conv, back, inverse)

    own_part, *parts = pl.pallas_call(
        functools.partial(taps_kernel, n, seq_len),
        in_specs=[pl.BlockSpec(memory_space=pltpu.VMEM)] * (2 * n + 3) + [pl.BlockSpec(memory_space=pl.ANY)],
        out_shape=[part] * n,
        scratch_shapes=[
            pltpu.VMEM(shares, BF16),
            pltpu.VMEM((n + 1, share, span), BF16),
            pltpu.VMEM((n, share, 2 * span), F32),
            pltpu.VMEM((n, share, 2 * span), F32),
            pltpu.VMEM((share, 2 * span), F32),
        ],
        compiler_params=params(),
        name="taps",
    )(
        mixed.reshape(shares), pulled.reshape(shares), reach.reshape(n, 1, share), high, inverse,
        *[x.reshape(shares) for x in first], *[second[k] for k in range(1, n)], peak,
    )
    parts = [
        lax.ppermute(x, "ctx", [(j, j ^ (k + 1)) for j in range(n)]) for k, x in enumerate(parts)
    ]
    filter_grad = pl.pallas_call(
        functools.partial(spread_kernel, n),
        out_shape=shape(shares, F32),
        compiler_params=params(),
        name="spread",
    )(own_part, *parts).reshape(channels, span)
    return (scaled_out, peak.reshape(span), gradients, filter_grad)


def solution(mesh):
    return jax.shard_map(
        body,
        mesh=mesh,
        in_specs=(
            P(None, "ch", "ctx"),
            P(None, "ch", "ctx"),
            P("ch", None),
            P("ch"),
            P("ch"),
            P("ch", "ctx"),
        ),
        out_specs=(P("ch", "ctx"), P("ctx"), P(None, "ch", "ctx"), P("ch", "ctx")),
        check_vma=False,
    )
```

time: 117 us -> 44.2 us (0.38)
  matrix products: 26.3 us -> 0 us
  other arithmetic: 25.8 us -> 0.01 us
  blocking collectives: 13.6 us -> 0 us
  between operations: 14.4 us -> 0.8 us
  starting transfers between devices: 4.53 us -> 17.9 us
  Pallas kernels: 0 us -> 13.2 us
  waiting for transfers between devices: 20.5 us -> 8.44 us
  local copies, waits for them, and re-layouts: 11.7 us -> 3.66 us
    dot_general x6 -> x0, matrix products: 26.3 us -> none  [the longest x3 19.8 us: from_spectrum(): jnp.einsum('...f,sf->...s', spectrum, basis, precision=lax.Precision.HIGH...]
    ppermute x0 -> x12, starting transfers between devices: none -> 17.9 us  [the longest x3 4.46 us: body(): first.append(lax.ppermute(sends[k.bit_length() - 1], 'ctx', perm))]
    pmax x1 -> x0, blocking collectives: 13.6 us -> none  [body(): token_max = lax.pmax(local_peak, 'ch')]
    pallas_call x0 -> x10, Pallas kernels: none -> 13.2 us  [the longest x1 3.86 us: body(): pl.pallas_call(functools.partial(windows_kernel, n), grid=(steps,), in_sp...]
    all_gather x1 -> x0, waiting for transfers between devices: 11.2 us -> none  [body(): shard_piece = lax.all_gather(pulled_bf, 'ctx', axis=1, tiled=True)]
    all_to_all x1 -> x0, waiting for transfers between devices: 9.35 us -> none  [body(): lax.all_to_all(pieces, 'ctx', split_axis=0, concat_axis=0, tiled=True)]
    add x5 -> x0, other arithmetic: 8.97 us -> none  [the longest x1 5.98 us: body(): near_plus = near_spec + rotate(next_spec, parity)]
    ppermute x0 -> x12, waiting for transfers between devices: none -> 8.44 us  [the longest x3 5 us: body(): far = lax.ppermute(peak, 'ch', [(j, j ^ hop) for j in range(ch_count)])]
  transfers between devices with their start and end apart: 3 -> 12, of which waited for: 2 -> 6; matrix products, arithmetic and copies ran while one was open for 30% -> 0% of each run, Pallas kernels for 0% -> 18%
where the time goes in v1:
time: 44.2 us; the launch traced here: 44 us
  starting transfers between devices  17.9 us (40%)
  Pallas kernels  13.2 us (30%)
  waiting for transfers between devices  8.44 us (19%)
  local copies, waits for them, and re-layouts  3.66 us (8%)
  between operations  0.8 us (2%)
    ppermute x3, waiting for transfers between devices, body(): far = lax.ppermute(peak, 'ch', [(j, j ^ hop) for j in range(ch_count)])  5 us
    ppermute x3, starting transfers between devices, body(): first.append(lax.ppermute(sends[k.bit_length() - 1], 'ctx', perm))  4.46 us
    ppermute x3, starting transfers between devices, body(): far = lax.ppermute(peak, 'ch', [(j, j ^ hop) for j in range(ch_count)])  4.24 us
    pallas_call x1, Pallas kernels, body(): pl.pallas_call(functools.partial(windows_kernel, n), grid=(steps,), in_sp...  3.86 us
    unnamed x28, local copies, waits for them, and re-layouts  3.66 us
    ppermute x3, starting transfers between devices, body(): lax.ppermute(x, 'ctx', [(j, j ^ k + 1) for j in range(n)])  3.55 us
    ppermute x2, starting transfers between devices, body(): lax.ppermute(pick(k), 'ctx', [(j, j ^ k) for j in range(n)])  3.55 us
    pallas_call x1, Pallas kernels, body(): pl.pallas_call(functools.partial(prep_kernel, n), grid=(steps,), in_specs...  2.53 us
  transfers between devices with their start and end apart: 12, of which 6 were waited for; matrix products, arithmetic and copies ran while one was open for 0% of the time, Pallas kernels for 18%

profile of v1, /device:TPU:0, one launch (start us, length us, event | category | flops | bytes accessed | tf_op | source)
XLA Modules:
  0.0 44.0 jit_solution(12722200143394186315)
XLA Ops:
  0.7 2.5 %prep.1 = (bf16[512,256]{1,0:T(8,128)(2,1)}, bf16[512,256]{1,0:T(8,128)(2,1)}, bf16[512,256]{1,0:T(8,128)(2,1)}, bf16[512,256]{1,0:T(8,128)(2,1)}) custom-call(bf16[3,512,256]{2,1,0:T(8,128)(2,1)} %value_ref.1, s32[3,2,512]{2,1,0:T(2,128)} %bitcast.22, bf16[512,256]{1,0:T(8,128)(2,1)} %cot_ref.3), custom_call_target="tpu_custom_call" | custom-call | tf_op jit(solution)/shard_map/prep/pallas_call | solution.py:285
  3.2 2.9 %collective-permute-start.2 = (bf16[512,256]{1,0:T(8,128)(2,1)}, bf16[512,256]{1,0:T(8,128)(2,1)S(1)}, u32[]{:S(2)}, u32[]{:S(2)}) collective-permute-start(bf16[512,256]{1,0:T(8,128)(2,1)} %get-tuple-element.25), channel_id=1, source_target_pairs={{0,8},{8,0},{16,24},{24,16},{1,9},{9,1},{17,25},{25,17},{2,10},{10... | collective-permute-start | bytes 786440 | tf_op jit(solution)/shard_map/ppermute | solution.py:298
  6.1 1.5 %collective-permute-start = (bf16[512,256]{1,0:T(8,128)(2,1)}, bf16[512,256]{1,0:T(8,128)(2,1)S(1)}, u32[]{:S(2)}, u32[]{:S(2)}) collective-permute-start(bf16[512,256]{1,0:T(8,128)(2,1)} %get-tuple-element.22), channel_id=1, source_target_pairs={{0,16},{8,24},{16,0},{24,8},{1,17},{9,25},{17,1},{25,9},{2,18},{10... | collective-permute-start | bytes 786440 | tf_op jit(solution)/shard_map/ppermute | solution.py:298
  7.7 0.0 collective-permute-start.1
  7.7 0.9 %copy-done.1 = bf16[512,256]{1,0:T(8,128)(2,1)S(1)} copy-done((bf16[512,256]{1,0:T(8,128)(2,1)S(1)}, bf16[512,256]{1,0:T(8,128)(2,1)}, u32[]{:S(2)}) %copy-start.1) | copy-done | bytes 262168
  8.6 0.9 %copy-done.3 = bf16[512,256]{1,0:T(8,128)(2,1)S(1)} copy-done((bf16[512,256]{1,0:T(8,128)(2,1)S(1)}, bf16[512,256]{1,0:T(8,128)(2,1)}, u32[]{:S(2)}) %copy-start.3) | copy-done | bytes 262168
  9.6 2.1 %collective-permute-start.7 = (bf16[128,256]{1,0:T(8,128)(2,1)S(1)}, bf16[128,256]{1,0:T(8,128)(2,1)S(1)}, u32[]{:S(2)}, u32[]{:S(2)}) collective-permute-start(bf16[128,256]{1,0:T(8,128)(2,1)S(1)} %pick.4), channel_id=1, source_target_pairs={{0,16},{8,24},{16,0},{24,8},{1,17},{9,25},{17,1},{25,9},{2,18},{10... | collective-permute-start | bytes 196616 | tf_op jit(solution)/shard_map/ppermute | solution.py:313
  11.6 1.5 %collective-permute-start.8 = (bf16[128,256]{1,0:T(8,128)(2,1)S(1)}, bf16[128,256]{1,0:T(8,128)(2,1)S(1)}, u32[]{:S(2)}, u32[]{:S(2)}) collective-permute-start(bf16[128,256]{1,0:T(8,128)(2,1)S(1)} %pick.5), channel_id=1, source_target_pairs={{0,24},{8,16},{16,8},{24,0},{1,25},{9,17},{17,9},{25,1},{2,26},{10... | collective-permute-start | bytes 196616 | tf_op jit(solution)/shard_map/ppermute | solution.py:313
  13.1 0.3 collective-permute-done.2.recv_ref.refs_0_
  13.5 2.1 %collective-permute-start.6 = (bf16[128,256]{1,0:T(8,128)(2,1)S(1)}, bf16[128,256]{1,0:T(8,128)(2,1)S(1)}, u32[]{:S(2)}, u32[]{:S(2)}) collective-permute-start(bf16[128,256]{1,0:T(8,128)(2,1)S(1)} %pick.3), channel_id=1, source_target_pairs={{0,8},{8,0},{16,24},{24,16},{1,9},{9,1},{17,25},{25,17},{2,10},{10... | collective-permute-start | bytes 196616 | tf_op jit(solution)/shard_map/ppermute | solution.py:330
  15.6 0.0 copy-start.9
  15.6 1.0 %copy-done.9 = bf16[512,512]{1,0:T(8,128)(2,1)S(1)} copy-done((bf16[512,512]{1,0:T(8,128)(2,1)S(1)}, bf16[512,512]{1,0:T(8,128)(2,1)}, u32[]{:S(2)}) %copy-start.9) | copy-done | bytes 524312
  16.6 3.9 %windows.1 = (bf16[512,256]{1,0:T(8,128)(2,1)S(1)}, f32[2,512,512]{2,1,0:T(8,128)S(1)}, bf16[512,512]{1,0:T(8,128)(2,1)S(1)}, bf16[512,512]{1,0:T(8,128)(2,1)S(1)}) custom-call(bf16[3,512,256]{2,1,0:T(8,128)(2,1)S(1)} %copy-done, s32[3,2,512]{2,1,0:T(2,128)S(1)} %bitcast.23, bf16[512,1024]{1,0:T(8,128)(2,1)S(1)} %copy-done.7, s32[1,512]{1,0:T(1,128)S(1)} %bitcast.25, ...), custom_call_target="tpu_custom_call" | custom-call | tf_op jit(solution)/shard_map/windows/pallas_call | solution.py:315
  20.5 1.3 %collective-permute-done.refs_0_ = bf16[512,256]{1,0:T(8,128)(2,1)S(1)} collective-permute-done((bf16[512,256]{1,0:T(8,128)(2,1)}, bf16[512,256]{1,0:T(8,128)(2,1)S(1)}, u32[]{:S(2)}, u32[]{:S(2)}) %collective-permute-start) | collective-permute-done | bytes 262176 | tf_op jit(solution)/shard_map/ppermute | solution.py:298
  21.8 0.0 copy-start.4
  21.9 1.8 %conv.1 = (f32[512,256]{1,0:T(8,128)S(1)}, f32[512,256]{1,0:T(8,128)S(1)}, bf16[512,512]{1,0:T(8,128)(2,1)S(1)}, f32[1,256]{1,0:T(1,128)S(1)}) custom-call(bf16[512,256]{1,0:T(8,128)(2,1)S(1)} %collective-permute-done.refs_0_, bf16[512,256]{1,0:T(8,128)(2,1)S(1)} %collective-permute-done.1.refs_1_, bf16[512,512]{1,0:T(8,128)(2,1)S(1)} %get-tuple-element.26.refs_2_, ...), custom_call_target="tpu_custom_call" | custom-call | tf_op jit(solution)/shard_map/conv/pallas_call | solution.py:332
  23.7 0.1 collective-permute-start.3
  23.7 1.1 %collective-permute-done.3 = f32[1,256]{1,0:T(1,128)S(1)} collective-permute-done((f32[1,256]{1,0:T(1,128)S(1)}, f32[1,256]{1,0:T(1,128)S(1)}, u32[]{:S(2)}, u32[]{:S(2)}) %collective-permute-start.3) | collective-permute-done | bytes 1056 | tf_op jit(solution)/shard_map/ppermute | solution.py:349
  24.9 1.6 %collective-permute-start.4 = (f32[1,256]{1,0:T(1,128)S(1)}, f32[1,256]{1,0:T(1,128)S(1)}, u32[]{:S(2)}, u32[]{:S(2)}) collective-permute-start(f32[1,256]{1,0:T(1,128)S(1)} %max.7), channel_id=1, source_target_pairs={{0,2},{1,3},{2,0},{3,1},{4,6},{5,7},{6,4},{7,5},{8,10},{9,11},{10,... | collective-permute-start | bytes 3080 | tf_op jit(solution)/shard_map/ppermute | solution.py:349
  26.4 2.0 %collective-permute-done.4 = f32[1,256]{1,0:T(1,128)S(1)} collective-permute-done((f32[1,256]{1,0:T(1,128)S(1)}, f32[1,256]{1,0:T(1,128)S(1)}, u32[]{:S(2)}, u32[]{:S(2)}) %collective-permute-start.4) | collective-permute-done | bytes 1056 | tf_op jit(solution)/shard_map/ppermute | solution.py:349
  28.4 2.6 %collective-permute-start.5 = (f32[1,256]{1,0:T(1,128)S(1)}, f32[1,256]{1,0:T(1,128)S(1)}, u32[]{:S(2)}, u32[]{:S(2)}) collective-permute-start(f32[1,256]{1,0:T(1,128)S(1)} %max.8.near_ref), channel_id=1, source_target_pairs={{0,4},{1,5},{2,6},{3,7},{4,0},{5,1},{6,2},{7,3},{8,12},{9,13},{10,... | collective-permute-start | bytes 3080 | tf_op jit(solution)/shard_map/ppermute | solution.py:349
  31.0 1.9 %collective-permute-done.5.far_ref = f32[1,256]{1,0:T(1,128)S(1)} collective-permute-done((f32[1,256]{1,0:T(1,128)S(1)}, f32[1,256]{1,0:T(1,128)S(1)}, u32[]{:S(2)}, u32[]{:S(2)}) %collective-permute-start.5) | collective-permute-done | bytes 1056 | tf_op jit(solution)/shard_map/ppermute | solution.py:349
  32.9 0.7 %scale.1 = (bf16[512,256]{1,0:T(8,128)(2,1)}, f32[1,256]{1,0:T(1,128)}) custom-call(f32[512,256]{1,0:T(8,128)S(1)} %get-tuple-element.30.resp_ref, f32[1,256]{1,0:T(1,128)S(1)} %max.8.near_ref, f32[1,256]{1,0:T(1,128)S(1)} %collective-permute-done.5.far_ref), custom_call_target="tpu_custom_call" | custom-call | tf_op jit(solution)/shard_map/scale/pallas_call | solution.py:352
  33.7 0.0 copy-start.13
  33.7 0.7 %copy-done.13 = f32[1,256]{1,0:T(1,128)S(1)} copy-done((f32[1,256]{1,0:T(1,128)S(1)}, f32[1,256]{1,0:T(1,128)}, u32[]{:S(2)}) %copy-start.13) | copy-done | bytes 1048
  34.3 2.0 %taps.1 = (bf16[128,256]{1,0:T(8,128)(2,1)S(1)}, bf16[128,256]{1,0:T(8,128)(2,1)S(1)}, bf16[128,256]{1,0:T(8,128)(2,1)S(1)}, bf16[128,256]{1,0:T(8,128)(2,1)S(1)}) custom-call(bf16[4,128,256]{2,1,0:T(8,128)(2,1)S(1)} %bitcast.14, bf16[4,128,256]{2,1,0:T(8,128)(2,1)S(1)} %bitcast.18, s32[4,1,128]{2,1,0:T(1,128)S(1)} %bitcast.26, ...), custom_call_target="tpu_custom_call" | custom-call | tf_op jit(solution)/shard_map/taps/pallas_call | solution.py:376
  36.4 1.6 %collective-permute-start.10 = (bf16[128,256]{1,0:T(8,128)(2,1)S(1)}, bf16[128,256]{1,0:T(8,128)(2,1)S(1)}, u32[]{:S(2)}, u32[]{:S(2)}) collective-permute-start(bf16[128,256]{1,0:T(8,128)(2,1)S(1)} %get-tuple-element.38), channel_id=1, source_target_pairs={{0,16},{8,24},{16,0},{24,8},{1,17},{9,25},{17,1},{25,9},{2,18},{10... | collective-permute-start | bytes 196616 | tf_op jit(solution)/shard_map/ppermute | solution.py:394
  38.0 0.2 collective-permute-start.11
  38.2 1.7 %collective-permute-start.9 = (bf16[128,256]{1,0:T(8,128)(2,1)S(1)}, bf16[128,256]{1,0:T(8,128)(2,1)S(1)}, u32[]{:S(2)}, u32[]{:S(2)}) collective-permute-start(bf16[128,256]{1,0:T(8,128)(2,1)S(1)} %get-tuple-element.37), channel_id=1, source_target_pairs={{0,8},{8,0},{16,24},{24,16},{1,9},{9,1},{17,25},{25,17},{2,10},{10... | collective-permute-start | bytes 196616 | tf_op jit(solution)/shard_map/ppermute | solution.py:394
  39.9 1.4 %grads.1 = bf16[3,512,256]{2,1,0:T(8,128)(2,1)} custom-call(bf16[3,512,256]{2,1,0:T(8,128)(2,1)S(1)} %copy-done, bf16[3,512,256]{2,1,0:T(8,128)(2,1)S(1)} %copy-done, s32[3,2,512]{2,1,0:T(2,128)S(1)} %bitcast.24, bf16[512,256]{1,0:T(8,128)(2,1)S(1)} %copy-done.8, f32[512,256]{1,0:T(8,128)S(1)} %get-tuple-element.34.conv_ref, ...), custom_call_target="tpu_custom_call" | custom-call | tf_op jit(solution)/shard_map/grads/pallas_call | solution.py:362
  41.4 1.8 %collective-permute-done.11.refs_3_ = bf16[128,256]{1,0:T(8,128)(2,1)S(1)} collective-permute-done((bf16[128,256]{1,0:T(8,128)(2,1)S(1)}, bf16[128,256]{1,0:T(8,128)(2,1)S(1)}, u32[]{:S(2)}, u32[]{:S(2)}) %collective-permute-start.11) | collective-permute-done | bytes 65568 | tf_op jit(solution)/shard_map/ppermute | solution.py:394
  43.1 0.8 %spread.1 = f32[4,128,256]{2,1,0:T(8,128)} custom-call(bf16[128,256]{1,0:T(8,128)(2,1)S(1)} %get-tuple-element.36.refs_0_, bf16[128,256]{1,0:T(8,128)(2,1)S(1)} %collective-permute-done.9.refs_1_, bf16[128,256]{1,0:T(8,128)(2,1)S(1)} %collective-permute-done.10.refs_2_, bf16[128,256]{1,0:T(8,128)(2,1)S(1)} %collective-permute-done.11.refs_3_), custom_call_target="tpu_custom_call" | custom-call | tf_op jit(solution)/shard_map/spread/pallas_call | solution.py:396
  (32 shorter events, 0.1 us)
Async XLA Ops:
  0.6 14.9 %copy-start.10 = (s32[3,512,2]{1,2,0:T(2,128)S(1)}, s32[3,512,2]{1,2,0:T(2,128)}, u32[]{:S(2)}) copy-start(s32[3,512,2]{1,2,0:T(2,128)} %param.10) | copy-start | bytes 36868
  0.6 14.9 %copy-start = (bf16[3,512,256]{2,1,0:T(8,128)(2,1)S(1)}, bf16[3,512,256]{2,1,0:T(8,128)(2,1)}, u32[]{:S(2)}) copy-start(bf16[3,512,256]{2,1,0:T(8,128)(2,1)} %value_ref.1) | copy-start | bytes 2359300
  0.7 14.9 %copy-start.11 = (s32[512]{0:T(512)S(1)}, s32[512]{0:T(512)}, u32[]{:S(2)}) copy-start(s32[512]{0:T(512)} %param.12) | copy-start | bytes 6148
  0.7 14.9 %copy-start.12 = (f32[512]{0:T(512)S(1)}, f32[512]{0:T(512)}, u32[]{:S(2)}) copy-start(f32[512]{0:T(512)} %param.13) | copy-start | bytes 6148
  3.2 10.3 %collective-permute-start.2 = (bf16[512,256]{1,0:T(8,128)(2,1)}, bf16[512,256]{1,0:T(8,128)(2,1)S(1)}, u32[]{:S(2)}, u32[]{:S(2)}) collective-permute-start(bf16[512,256]{1,0:T(8,128)(2,1)} %get-tuple-element.25), channel_id=1, source_target_pairs={{0,8},{8,0},{16,24},{24,16},{1,9},{9,1},{17,25},{25,17},{2,10},{10... | collective-permute-start | bytes 786440 | tf_op jit(solution)/shard_map/ppermute | solution.py:298
  6.1 15.7 %collective-permute-start = (bf16[512,256]{1,0:T(8,128)(2,1)}, bf16[512,256]{1,0:T(8,128)(2,1)S(1)}, u32[]{:S(2)}, u32[]{:S(2)}) collective-permute-start(bf16[512,256]{1,0:T(8,128)(2,1)} %get-tuple-element.22), channel_id=1, source_target_pairs={{0,16},{8,24},{16,0},{24,8},{1,17},{9,25},{17,1},{25,9},{2,18},{10... | collective-permute-start | bytes 786440 | tf_op jit(solution)/shard_map/ppermute | solution.py:298
  7.7 14.2 %collective-permute-start.1 = (bf16[512,256]{1,0:T(8,128)(2,1)}, bf16[512,256]{1,0:T(8,128)(2,1)S(1)}, u32[]{:S(2)}, u32[]{:S(2)}) collective-permute-start(bf16[512,256]{1,0:T(8,128)(2,1)} %get-tuple-element.22), channel_id=1, source_target_pairs={{0,24},{8,16},{16,8},{24,0},{1,25},{9,17},{17,9},{25,1},{2,26},{10... | collective-permute-start | bytes 786440 | tf_op jit(solution)/shard_map/ppermute | solution.py:298
  7.7 0.9 %copy-start.1 = (bf16[512,256]{1,0:T(8,128)(2,1)S(1)}, bf16[512,256]{1,0:T(8,128)(2,1)}, u32[]{:S(2)}) copy-start(bf16[512,256]{1,0:T(8,128)(2,1)} %get-tuple-element.23.mixed_ref) | copy-start | bytes 786436
  8.6 0.9 %copy-start.3 = (bf16[512,256]{1,0:T(8,128)(2,1)S(1)}, bf16[512,256]{1,0:T(8,128)(2,1)}, u32[]{:S(2)}) copy-start(bf16[512,256]{1,0:T(8,128)(2,1)} %get-tuple-element.24.pulled_ref) | copy-start | bytes 786436
  9.6 6.0 %copy-start.6 = (bf16[512,512]{1,0:T(8,128)(2,1)S(1)}, bf16[512,512]{1,0:T(8,128)(2,1)}, u32[]{:S(2)}) copy-start(bf16[512,512]{1,0:T(8,128)(2,1)} %constant.6.clone.high_ref.refs_6_) | copy-start | bytes 1572868
  9.6 6.0 %copy-start.7 = (bf16[512,1024]{1,0:T(8,128)(2,1)S(1)}, bf16[512,1024]{1,0:T(8,128)(2,1)}, u32[]{:S(2)}) copy-start(bf16[512,1024]{1,0:T(8,128)(2,1)} %filt_ref.1) | copy-start | bytes 3145732
  9.6 24.1 %collective-permute-start.7 = (bf16[128,256]{1,0:T(8,128)(2,1)S(1)}, bf16[128,256]{1,0:T(8,128)(2,1)S(1)}, u32[]{:S(2)}, u32[]{:S(2)}) collective-permute-start(bf16[128,256]{1,0:T(8,128)(2,1)S(1)} %pick.4), channel_id=1, source_target_pairs={{0,16},{8,24},{16,0},{24,8},{1,17},{9,25},{17,1},{25,9},{2,18},{10... | collective-permute-start | bytes 196616 | tf_op jit(solution)/shard_map/ppermute | solution.py:313
  11.6 10.2 %copy-start.5 = (bf16[512,512]{1,0:T(8,128)(2,1)S(1)}, bf16[512,512]{1,0:T(8,128)(2,1)}, u32[]{:S(2)}) copy-start(bf16[512,512]{1,0:T(8,128)(2,1)} %constant.8.clone.refs_7_.inv_ref) | copy-start | bytes 1572868
  11.6 22.0 %collective-permute-start.8 = (bf16[128,256]{1,0:T(8,128)(2,1)S(1)}, bf16[128,256]{1,0:T(8,128)(2,1)S(1)}, u32[]{:S(2)}, u32[]{:S(2)}) collective-permute-start(bf16[128,256]{1,0:T(8,128)(2,1)S(1)} %pick.5), channel_id=1, source_target_pairs={{0,24},{8,16},{16,8},{24,0},{1,25},{9,17},{17,9},{25,1},{2,26},{10... | collective-permute-start | bytes 196616 | tf_op jit(solution)/shard_map/ppermute | solution.py:313
  13.5 20.2 %collective-permute-start.6 = (bf16[128,256]{1,0:T(8,128)(2,1)S(1)}, bf16[128,256]{1,0:T(8,128)(2,1)S(1)}, u32[]{:S(2)}, u32[]{:S(2)}) collective-permute-start(bf16[128,256]{1,0:T(8,128)(2,1)S(1)} %pick.3), channel_id=1, source_target_pairs={{0,8},{8,0},{16,24},{24,16},{1,9},{9,1},{17,25},{25,17},{2,10},{10... | collective-permute-start | bytes 196616 | tf_op jit(solution)/shard_map/ppermute | solution.py:330
  15.6 1.0 %copy-start.9 = (bf16[512,512]{1,0:T(8,128)(2,1)S(1)}, bf16[512,512]{1,0:T(8,128)(2,1)}, u32[]{:S(2)}) copy-start(bf16[512,512]{1,0:T(8,128)(2,1)} %constant.7.clone.low_ref) | copy-start | bytes 1572868
  21.8 11.8 %copy-start.2 = (bf16[512,256]{1,0:T(8,128)(2,1)S(1)}, bf16[512,256]{1,0:T(8,128)(2,1)}, u32[]{:S(2)}) copy-start(bf16[512,256]{1,0:T(8,128)(2,1)} %get-tuple-element.23.mixed_ref) | copy-start | bytes 786436
  21.8 11.8 %copy-start.4 = (bf16[512,256]{1,0:T(8,128)(2,1)S(1)}, bf16[512,256]{1,0:T(8,128)(2,1)}, u32[]{:S(2)}) copy-start(bf16[512,256]{1,0:T(8,128)(2,1)} %get-tuple-element.24.pulled_ref) | copy-start | bytes 786436
  23.6 16.3 %copy-start.8 = (bf16[512,256]{1,0:T(8,128)(2,1)S(1)}, bf16[512,256]{1,0:T(8,128)(2,1)}, u32[]{:S(2)}) copy-start(bf16[512,256]{1,0:T(8,128)(2,1)} %cot_ref.3) | copy-start | bytes 786436
  23.7 1.2 %collective-permute-start.3 = (f32[1,256]{1,0:T(1,128)S(1)}, f32[1,256]{1,0:T(1,128)S(1)}, u32[]{:S(2)}, u32[]{:S(2)}) collective-permute-start(f32[1,256]{1,0:T(1,128)S(1)} %get-tuple-element.31), channel_id=1, source_target_pairs={{0,1},{1,0},{2,3},{3,2},{4,5},{5,4},{6,7},{7,6},{8,9},{9,8},{10,11... | collective-permute-start | bytes 3080 | tf_op jit(solution)/shard_map/ppermute | solution.py:349
  24.9 3.6 %collective-permute-start.4 = (f32[1,256]{1,0:T(1,128)S(1)}, f32[1,256]{1,0:T(1,128)S(1)}, u32[]{:S(2)}, u32[]{:S(2)}) collective-permute-start(f32[1,256]{1,0:T(1,128)S(1)} %max.7), channel_id=1, source_target_pairs={{0,2},{1,3},{2,0},{3,1},{4,6},{5,7},{6,4},{7,5},{8,10},{9,11},{10,... | collective-permute-start | bytes 3080 | tf_op jit(solution)/shard_map/ppermute | solution.py:349
  28.4 4.5 %collective-permute-start.5 = (f32[1,256]{1,0:T(1,128)S(1)}, f32[1,256]{1,0:T(1,128)S(1)}, u32[]{:S(2)}, u32[]{:S(2)}) collective-permute-start(f32[1,256]{1,0:T(1,128)S(1)} %max.8.near_ref), channel_id=1, source_target_pairs={{0,4},{1,5},{2,6},{3,7},{4,0},{5,1},{6,2},{7,3},{8,12},{9,13},{10,... | collective-permute-start | bytes 3080 | tf_op jit(solution)/shard_map/ppermute | solution.py:349
  33.7 0.7 %copy-start.13 = (f32[1,256]{1,0:T(1,128)S(1)}, f32[1,256]{1,0:T(1,128)}, u32[]{:S(2)}) copy-start(f32[1,256]{1,0:T(1,128)} %get-tuple-element.33.refs_6_) | copy-start | bytes 3076
  36.4 5.0 %collective-permute-start.10 = (bf16[128,256]{1,0:T(8,128)(2,1)S(1)}, bf16[128,256]{1,0:T(8,128)(2,1)S(1)}, u32[]{:S(2)}, u32[]{:S(2)}) collective-permute-start(bf16[128,256]{1,0:T(8,128)(2,1)S(1)} %get-tuple-element.38), channel_id=1, source_target_pairs={{0,16},{8,24},{16,0},{24,8},{1,17},{9,25},{17,1},{25,9},{2,18},{10... | collective-permute-start | bytes 196616 | tf_op jit(solution)/shard_map/ppermute | solution.py:394
  38.0 5.2 %collective-permute-start.11 = (bf16[128,256]{1,0:T(8,128)(2,1)S(1)}, bf16[128,256]{1,0:T(8,128)(2,1)S(1)}, u32[]{:S(2)}, u32[]{:S(2)}) collective-permute-start(bf16[128,256]{1,0:T(8,128)(2,1)S(1)} %get-tuple-element.39), channel_id=1, source_target_pairs={{0,24},{8,16},{16,8},{24,0},{1,25},{9,17},{17,9},{25,1},{2,26},{10... | collective-permute-start | bytes 196616 | tf_op jit(solution)/shard_map/ppermute | solution.py:394
  38.2 4.9 %collective-permute-start.9 = (bf16[128,256]{1,0:T(8,128)(2,1)S(1)}, bf16[128,256]{1,0:T(8,128)(2,1)S(1)}, u32[]{:S(2)}, u32[]{:S(2)}) collective-permute-start(bf16[128,256]{1,0:T(8,128)(2,1)S(1)} %get-tuple-element.37), channel_id=1, source_target_pairs={{0,8},{8,0},{16,24},{24,16},{1,9},{9,1},{17,25},{25,17},{2,10},{10... | collective-permute-start | bytes 196616 | tf_op jit(solution)/shard_map/ppermute | solution.py:394

commit v2 on v1

v2 whole, which is shorter than its diff:
```python
import functools
import math

import jax
import jax.numpy as jnp
import ml_dtypes
import numpy as np
from jax import lax
from jax.experimental import pallas as pl
from jax.experimental.pallas import tpu as pltpu
from jax.sharding import PartitionSpec as P

REACH_DIVISORS = (64, 32, 16, 4, 1)
F32 = jnp.float32
BF16 = jnp.bfloat16


def fourier_tables(span):
    freq = np.arange(span)
    time = np.arange(2 * span)
    phase = ((2 * freq[None, :] + 1) * time[:, None]) % (4 * span)
    angle = phase * (math.pi / (2 * span))
    forward = np.concatenate([np.cos(angle), -np.sin(angle)], axis=1)
    high = forward.astype(ml_dtypes.bfloat16)
    low = (forward - high.astype(np.float64)).astype(ml_dtypes.bfloat16)
    inverse = (forward.T / span).astype(ml_dtypes.bfloat16)
    return high, low, inverse


def mm(left, right):
    return lax.dot_general(left, right, (((1,), (0,)), ((), ())), preferred_element_type=F32)


def mm2(left, high, low):
    return mm(left, high) + mm(left, low)


def block_scale(exps, span):
    blocks = exps.shape[0]
    block_len = span // blocks
    col = lax.broadcasted_iota(jnp.int32, (blocks, span), 1)
    row = lax.broadcasted_iota(jnp.int32, (blocks, span), 0)
    onehot = jnp.where(col // block_len == row, 1.0, 0.0).astype(BF16)
    scale = jnp.exp2(exps.astype(F32)).astype(BF16)
    return lax.dot_general(scale, onehot, (((0,), (0,)), ((), ())), preferred_element_type=F32)


def column(row_ref):
    row = row_ref[...]
    return jnp.transpose(jnp.broadcast_to(row, (8, row.shape[1])))[:, 0:1]


def reach_lens(reach_ref, seq_len):
    cls = column(reach_ref)
    out = jnp.zeros_like(cls)
    for index, div in enumerate(REACH_DIVISORS):
        out = jnp.where(cls == index, seq_len // div, out)
    return out


def cmul_parts(first, second, half):
    ar, ai = first[:, :half], first[:, half:]
    br, bi = second[:, :half], second[:, half:]
    return ar, ai, br, bi


def row_loop(total, step):
    def run(step_fn):
        if total <= step:
            step_fn(slice(0, total))
            return

        def one(i, carry):
            step_fn(pl.ds(pl.multiple_of(i * step, step), step))
            return carry

        lax.fori_loop(0, total // step, one, 0)

    return run


def top_bit(n):
    return lax.div(lax.axis_index("ctx"), (n + 1) // 2)


def prep_kernel(parts, n, proj_hbm, exp_hbm, cot_hbm, main_ref, rest_ref, *refs):
    send_refs, (proj, exp, cot, exp_sem, key_sem, query_sem) = refs[:-6], refs[-6:]
    me = lax.axis_index("ctx")
    upper = top_bit(n)
    channels, span = cot.shape
    rows = channels // parts
    exp_copy = pltpu.make_async_copy(exp_hbm, exp, exp_sem)
    exp_copy.start()
    copies = []
    for part in range(parts):
        block = pl.ds(part * rows, rows)
        copies.append(
            (
                pltpu.make_async_copy(proj_hbm.at[1, block], proj.at[1, block], key_sem.at[part, 0]),
                pltpu.make_async_copy(proj_hbm.at[2, block], proj.at[2, block], key_sem.at[part, 1]),
                pltpu.make_async_copy(proj_hbm.at[0, block], proj.at[0, block], query_sem.at[part, 0]),
                pltpu.make_async_copy(cot_hbm.at[block], cot.at[block], query_sem.at[part, 1]),
            )
        )
        for copy in copies[-1]:
            copy.start()
    exp_copy.wait()
    exps = exp[...]
    for part in range(parts):
        block = pl.ds(part * rows, rows)
        key_scale = block_scale(exps[1, :, part * rows : (part + 1) * rows] + exps[2, :, part * rows : (part + 1) * rows], span)
        query_scale = block_scale(exps[0, :, part * rows : (part + 1) * rows], span)
        for copy in copies[part]:
            copy.wait()
        mixed = (proj[1, block].astype(F32) * proj[2, block].astype(F32) * key_scale).astype(BF16)
        pulled = (cot[block].astype(F32) * (proj[0, block].astype(F32) * query_scale)).astype(BF16)
        lows = [lax.rem(lax.div(me, 2**bit), 2) for bit in range(len(send_refs))]
        for ref, later in [(main_ref, upper), (rest_ref, 1 - upper), *zip(send_refs, lows)]:

            @pl.when(later == 1)
            def _():
                ref[block] = pulled

            @pl.when(later == 0)
            def _():
                ref[block] = mixed


def windows_kernel(
    n, rows, proj_ref, exp_ref, filt_ref, reach_ref, skip_ref, main_ref, rest_ref, high_ref, low_ref,
    recv_ref, query_ref, base_ref, *rest
):
    win_refs, (taps, lens, gain) = rest[: n - 2], rest[n - 2 :]
    me = lax.axis_index("ctx")
    channels, seq_len = filt_ref.shape
    span = seq_len // n
    fscale = 1.0 / math.sqrt(seq_len)
    query_ref[...] = (proj_ref[0].astype(F32) * block_scale(exp_ref[0], span)).astype(BF16)
    upper = top_bit(n)
    lens[...] = reach_lens(reach_ref, seq_len)
    gain[...] = column(skip_ref) * (1.0 / fscale)

    @row_loop(channels, rows)
    def _(block):
        count = min(rows, channels)
        taps[0] = jnp.zeros((count, span), BF16)
        for b in range(n):
            lag = lax.broadcasted_iota(jnp.int32, (count, span), 1) + b * span
            taps[b + 1] = jnp.where(
                lag < lens[block], filt_ref[block, b * span : (b + 1) * span].astype(F32), 0.0
            ).astype(BF16)
        near = mm2(taps[1], high_ref[span:], low_ref[span:])
        near += gain[block] * high_ref[span : span + 1, :].astype(F32)
        wr, wi = near[:, :span], near[:, span:]
        for ref, later in ((main_ref, upper), (rest_ref, 1 - upper)):
            start = pl.multiple_of(later * span, span)
            spec = mm2(ref[block], high_ref[pl.ds(start, span), :], low_ref[pl.ds(start, span), :])
            xr, xi = spec[:, :span], spec[:, span:]
            turned = wi * (1 - 2 * later).astype(F32)
            base_ref[later, block, :span] = xr * wr - xi * turned
            base_ref[later, block, span:] = xr * turned + xi * wr
        for k in range(1, n):
            other = jnp.bitwise_xor(me, k)
            dist = jnp.abs(other - me)
            win = mm2(taps[dist], high_ref[:span], low_ref[:span]) + mm2(
                taps[dist + 1], high_ref[span:], low_ref[span:]
            )
            sign = jnp.where(other < me, 1.0, -1.0).astype(F32)
            wr, wi = win[:, :span], win[:, span:] * sign
            if k > 1:
                win_refs[k - 2][block, :span] = wr.astype(BF16)
                win_refs[k - 2][block, span:] = wi.astype(BF16)
                continue
            later = jnp.where(other > me, 1, 0)
            start = pl.multiple_of(later * span, span)
            spec = mm2(recv_ref[block], high_ref[pl.ds(start, span), :], low_ref[pl.ds(start, span), :])
            xr, xi = spec[:, :span], spec[:, span:]
            base_ref[later, block, :span] += xr * wr - xi * wi
            base_ref[later, block, span:] += xr * wi + xi * wr


def conv_kernel(n, seq_len, rows, *refs):
    recv_refs, win_refs = refs[: n - 2], refs[n - 2 : 2 * n - 4]
    _, query_ref, high_ref, inv_ref = refs[2 * n - 4 : 2 * n]
    acc, resp_ref, conv_ref, peak_ref = refs[2 * n :]
    me = lax.axis_index("ctx")
    channels, span = query_ref.shape
    fscale = 1.0 / math.sqrt(seq_len)
    peak_ref[...] = jnp.zeros_like(peak_ref)

    @row_loop(channels, rows)
    def _(block):
        for k in range(2, n):
            later = jnp.where(jnp.bitwise_xor(me, k) > me, 1, 0)
            start = pl.multiple_of(later * span, span)
            spec = mm(recv_refs[k - 2][block], high_ref[pl.ds(start, span), :])
            xr, xi = spec[:, :span], spec[:, span:]
            wr = win_refs[k - 2][block, :span].astype(F32)
            wi = win_refs[k - 2][block, span:].astype(F32)
            acc[later, block, :span] += xr * wr - xi * wi
            acc[later, block, span:] += xr * wi + xi * wr
        conv = mm(acc[0, block].astype(BF16), inv_ref[:, span:]) * fscale
        response = query_ref[block].astype(F32) * conv
        resp_ref[block] = response
        conv_ref[block] = conv
        peak_ref[...] = jnp.maximum(peak_ref[...], jnp.max(jnp.abs(response), axis=0, keepdims=True))


def grad_kernel(seq_len, rows, proj_ref, exp_ref, cot_ref, conv_ref, acc_ref, inv_ref, grad_ref):
    channels, span = cot_ref.shape
    fscale = 1.0 / math.sqrt(seq_len)
    exps = exp_ref[...]
    grad_mixed = mm(acc_ref[1].astype(BF16), inv_ref[:, :span]) * fscale
    grad_ref[0] = (cot_ref[...].astype(F32) * conv_ref[...]).astype(BF16)
    grad_ref[1] = (grad_mixed * (proj_ref[2].astype(F32) * block_scale(exps[2], span))).astype(BF16)
    grad_ref[2] = (grad_mixed * (proj_ref[1].astype(F32) * block_scale(exps[1], span))).astype(BF16)


def taps_kernel(n, seq_len, main_ref, rest_ref, reach_ref, high_ref, inv_ref, *refs):
    first_refs, second_refs, refs = refs[: n - 1], refs[n - 1 : 2 * n - 2], refs[2 * n - 2 :]
    peak_ref, out_refs, top_ref = refs[0], refs[1 : n + 1], refs[n + 1]
    mbuf, pbuf, mspec, pspec, acc = refs[n + 2 :]
    top_ref[...] = peak_ref[...]
    me = lax.axis_index("ctx")
    _, rows, span = mbuf.shape
    fscale = 1.0 / math.sqrt(seq_len)
    upper = top_bit(n)

    @pl.when(upper == 0)
    def _():
        mbuf[me] = main_ref[me]
        pbuf[me] = rest_ref[me]

    @pl.when(upper == 1)
    def _():
        mbuf[me] = rest_ref[me]
        pbuf[me] = main_ref[me]

    pbuf[n] = jnp.zeros((rows, span), BF16)
    for k in range(1, n):
        other = jnp.bitwise_xor(me, k)

        @pl.when(other < me)
        def _():
            mbuf[other] = first_refs[k - 1][me]
            pbuf[other] = second_refs[k - 1][...]

        @pl.when(other > me)
        def _():
            pbuf[other] = first_refs[k - 1][me]
            mbuf[other] = second_refs[k - 1][...]

    if rows % 16 == 0:
        flat = (n * rows, span)
        mspec[...] = mm(mbuf[...].reshape(flat), high_ref[:span]).reshape(mspec.shape)
        pspec[...] = (
            mm(pbuf[:n].reshape(flat), high_ref[:span]) + mm(pbuf[1:].reshape(flat), high_ref[span:])
        ).reshape(pspec.shape)
    else:
        for b in range(n):
            mspec[b] = mm(mbuf[b], high_ref[:span])
            pspec[b] = mm(pbuf[b], high_ref[:span]) + mm(pbuf[b + 1], high_ref[span:])
    lens = reach_lens(reach_ref.at[me], seq_len)
    for k in range(n):
        lag_block = jnp.bitwise_xor(me, k)
        acc[...] = jnp.zeros_like(acc)
        for b in range(n):

            @pl.when(b + lag_block < n)
            def _():
                ar, ai = mspec[b, :, :span], mspec[b, :, span:]
                near = pspec[b + lag_block]
                br, bi = near[:, :span], near[:, span:]
                acc[:, :span] += ar * br + ai * bi
                acc[:, span:] += ar * bi - ai * br

        lag = lax.broadcasted_iota(jnp.int32, (rows, span), 1) + lag_block * span
        own = mm(acc[...].astype(BF16), inv_ref[:, :span]) * fscale
        out_refs[k][...] = jnp.where(lag < lens, own, 0.0).astype(BF16)


def pick_kernel(k, n, main_ref, rest_ref, *refs):
    me = lax.axis_index("ctx")
    other = jnp.bitwise_xor(me, k)
    out_ref = refs[-1]

    wanted = jnp.where(other > me, 1, 0)

    @pl.when(wanted == top_bit(n))
    def _():
        out_ref[...] = main_ref[other]

    @pl.when(wanted != top_bit(n))
    def _():
        out_ref[...] = rest_ref[other]


def spread_kernel(n, *refs):
    part_refs, out_ref = refs[:n], refs[n]
    me = lax.axis_index("ctx")
    for k in range(n):
        out_ref[jnp.bitwise_xor(me, k)] = part_refs[k][...].astype(F32)


def scale_kernel(resp_ref, near_ref, far_ref, out_ref, peak_ref):
    peak = jnp.maximum(near_ref[...], far_ref[...])
    peak_ref[...] = peak
    out_ref[...] = (resp_ref[...] / (peak + 1e-06)).astype(BF16)


def params(mib=32):
    return pltpu.CompilerParams(vmem_limit_bytes=mib * 2**20)


def body(proj, scale_exp, filt, reach, skip, cotangent):
    groups, channels, span = proj.shape
    n = lax.axis_size("ctx")
    ch_count = lax.axis_size("ch")
    seq_len = n * span
    blocks = scale_exp.shape[2]
    bits = max(1, (n - 1).bit_length())
    rows = 256 if channels % 256 == 0 else channels
    parts = 2 if channels % 256 == 0 else 1
    share = channels // n
    shares = (n, share, span)
    high, low, inverse = (jnp.asarray(t) for t in fourier_tables(span))
    exps = jnp.transpose(scale_exp, (0, 2, 1))
    reach_row = reach.reshape(1, channels)
    skip_row = skip.reshape(1, channels)
    vmem = pl.BlockSpec(memory_space=pltpu.VMEM)
    hbm = pl.BlockSpec(memory_space=pltpu.HBM)
    remote = pl.BlockSpec(memory_space=pl.ANY)

    def shape(dims, dtype):
        return jax.ShapeDtypeStruct(dims, dtype)

    def call(kernel, name, ins, outs, mib=32, **options):
        return pl.pallas_call(
            kernel,
            in_specs=ins,
            out_specs=[vmem] * len(outs),
            out_shape=outs,
            compiler_params=params(mib),
            name=name,
            **options,
        )

    def swap(value, axis, k):
        return lax.ppermute(value, axis, [(j, j ^ k) for j in range(lax.axis_size(axis))])

    flat = shape((channels, span), BF16)
    part = shape((share, span), BF16)
    line = shape((1, span), F32)
    main, rest, *sends = call(
        functools.partial(prep_kernel, parts, n),
        "prep",
        [hbm] * 3,
        [flat] * (1 + bits),
        mib=53,
        scratch_shapes=[
            pltpu.VMEM((3, channels, span), BF16),
            pltpu.VMEM((3, blocks, channels), jnp.int32),
            pltpu.VMEM((channels, span), BF16),
            pltpu.SemaphoreType.DMA,
            pltpu.SemaphoreType.DMA((parts, 2)),
            pltpu.SemaphoreType.DMA((parts, 2)),
        ],
    )(proj, exps, cotangent)

    sends.append(main)
    first = [swap(sends[k.bit_length() - 1], "ctx", k) for k in range(1, n)]

    def pick(k, *after):
        return call(functools.partial(pick_kernel, k, n), "pick", [vmem] * 2 + [remote] * len(after), [part])(
            main.reshape(shares), rest.reshape(shares), *after
        )[0]

    second = {k: swap(pick(k), "ctx", k) for k in range(2, n)}

    wide = shape((channels, 2 * span), BF16)
    query, base, *wins = call(
        functools.partial(windows_kernel, n, rows),
        "windows",
        [vmem] * 10,
        [flat, shape((2, channels, 2 * span), F32)] + [wide] * (n - 2),
        scratch_shapes=[
            pltpu.VMEM((n + 1, rows, span), BF16),
            pltpu.VMEM((channels, 1), jnp.int32),
            pltpu.VMEM((channels, 1), F32),
        ],
    )(proj, exps, filt, reach_row, skip_row, main, rest, high, low, first[0])
    second[1] = swap(pick(1, first[0]), "ctx", 1)

    acc, response, conv, peak = call(
        functools.partial(conv_kernel, n, seq_len, rows),
        "conv",
        [vmem] * (2 * n),
        [shape((2, channels, 2 * span), F32)] + [shape((channels, span), F32)] * 2 + [line],
        input_output_aliases={2 * n - 4: 0},
    )(*first[1:], *wins, base, query, high, inverse)

    far = swap(peak, "ch", 1)
    own_part, *parts_out, peak = call(
        functools.partial(taps_kernel, n, seq_len),
        "taps",
        [vmem] * (2 * n + 4),
        [part] * n + [line],
        scratch_shapes=[
            pltpu.VMEM(shares, BF16),
            pltpu.VMEM((n + 1, share, span), BF16),
            pltpu.VMEM((n, share, 2 * span), F32),
            pltpu.VMEM((n, share, 2 * span), F32),
            pltpu.VMEM((share, 2 * span), F32),
        ],
    )(
        main.reshape(shares), rest.reshape(shares), reach.reshape(n, 1, share), high, inverse,
        *[x.reshape(shares) for x in first], *[second[k] for k in range(1, n)], peak,
    )
    hop = 2
    while hop < ch_count:
        peak = jnp.maximum(peak, far)
        far = swap(peak, "ch", hop)
        hop *= 2
    scaled_out, peak = call(scale_kernel, "scale", [vmem] * 3, [flat, line])(response, peak, far)

    (gradients,) = call(
        functools.partial(grad_kernel, seq_len, rows),
        "grads",
        [vmem] * 6,
        [shape((3, channels, span), BF16)],
        cost_estimate=pl.CostEstimate(flops=10**9, bytes_accessed=10**6, transcendentals=0),
    )(proj, exps, cotangent, conv, acc, inverse)

    parts_out = [swap(x, "ctx", k + 1) for k, x in enumerate(parts_out)]
    (filter_grad,) = call(functools.partial(spread_kernel, n), "spread", [vmem] * n, [shape(shares, F32)])(
        own_part, *parts_out
    )
    return (scaled_out, peak.reshape(span), gradients, filter_grad.reshape(channels, span))


def solution(mesh):
    return jax.shard_map(
        body,
        mesh=mesh,
        in_specs=(
            P(None, "ch", "ctx"),
            P(None, "ch", "ctx"),
            P("ch", None),
            P("ch"),
            P("ch"),
            P("ch", "ctx"),
        ),
        out_specs=(P("ch", "ctx"), P("ctx"), P(None, "ch", "ctx"), P("ch", "ctx")),
        check_vma=False,
    )
```

time: 44.2 us -> 37 us (0.84)
  waiting for transfers between devices: 8.44 us -> 5.19 us
  local copies, waits for them, and re-layouts: 3.66 us -> 0.89 us
  Pallas kernels: 13.2 us -> 12 us
    ppermute x12, waiting for transfers between devices: 8.44 us -> 5.19 us  [swap(): lax.ppermute(value, axis, [(j, j ^ k) for j in range(lax.axis_size(axis))])]
    unnamed x28 -> x18, local copies, waits for them, and re-layouts: 3.66 us -> 0.89 us
    pallas_call x10, Pallas kernels: 13.2 us -> 12 us  [the longest x1 3.61 us: body(): call(functools.partial(windows_kernel, n, rows), 'windows', [vmem] * 10,...]
  transfers between devices with their start and end apart: 12 -> 12, of which waited for: 6 -> 3; matrix products, arithmetic and copies ran while one was open for 0% -> 0% of each run, Pallas kernels for 18% -> 25%
where the time goes in v2:
time: 37 us; the launch traced here: 36.8 us
  starting transfers between devices  17.9 us (48%)
  Pallas kernels  12 us (32%)
  waiting for transfers between devices  5.19 us (14%)
  local copies, waits for them, and re-layouts  0.89 us (2%)
  between operations  0.8 us (2%)
    ppermute x12, starting transfers between devices, swap(): lax.ppermute(value, axis, [(j, j ^ k) for j in range(lax.axis_size(axis))])  17.9 us
    ppermute x12, waiting for transfers between devices, swap(): lax.ppermute(value, axis, [(j, j ^ k) for j in range(lax.axis_size(axis))])  5.19 us
    pallas_call x1, Pallas kernels, body(): call(functools.partial(windows_kernel, n, rows), 'windows', [vmem] * 10,...  3.61 us
    pallas_call x1, Pallas kernels, body(): call(functools.partial(taps_kernel, n, seq_len), 'taps', [vmem] * (2 * n...  2.04 us
    pallas_call x1, Pallas kernels, body(): call(functools.partial(prep_kernel, parts, n), 'prep', [hbm] * 3, [flat]...  1.85 us
    pallas_call x1, Pallas kernels, body(): call(functools.partial(conv_kernel, n, seq_len, rows), 'conv', [vmem] * (...  1.48 us
    pallas_call x1, Pallas kernels, body(): call(functools.partial(grad_kernel, seq_len, rows), 'grads', [vmem] * 6,...  1.46 us
    unnamed x18, local copies, waits for them, and re-layouts  0.89 us
  transfers between devices with their start and end apart: 12, of which 3 were waited for; matrix products, arithmetic and copies ran while one was open for 0% of the time, Pallas kernels for 25%

profile of v2, /device:TPU:0, one launch (start us, length us, event | category | flops | bytes accessed | tf_op | source)
XLA Modules:
  0.0 36.8 jit_solution(13115319957083026598)
XLA Ops:
  0.6 0.0 copy-start.1
  0.6 0.0 copy-start.5
  0.7 0.8 %copy-done.6 = s32[3,512,2]{1,2,0:T(2,128)S(1)} copy-done((s32[3,512,2]{1,2,0:T(2,128)S(1)}, s32[3,512,2]{1,2,0:T(2,128)}, u32[]{:S(2)}) %copy-start.6) | copy-done | bytes 12312
  1.5 1.8 %prep.1 = (bf16[512,256]{1,0:T(8,128)(2,1)S(1)}, bf16[512,256]{1,0:T(8,128)(2,1)S(1)}, bf16[512,256]{1,0:T(8,128)(2,1)S(1)}) custom-call(bf16[3,512,256]{2,1,0:T(8,128)(2,1)} %proj_ref.3, s32[3,2,512]{2,1,0:T(2,128)S(1)} %bitcast.22, bf16[512,256]{1,0:T(8,128)(2,1)} %cot_ref.1), custom_call_target="tpu_custom_call" | custom-call | tf_op jit(solution)/shard_map/prep/pallas_call | solution.py:354
  3.4 3.0 %collective-permute-start.2 = (bf16[512,256]{1,0:T(8,128)(2,1)S(1)}, bf16[512,256]{1,0:T(8,128)(2,1)S(1)}, u32[]{:S(2)}, u32[]{:S(2)}) collective-permute-start(bf16[512,256]{1,0:T(8,128)(2,1)S(1)} %get-tuple-element.24), channel_id=1, source_target_pairs={{0,8},{8,0},{16,24},{24,16},{1,9},{9,1},{17,25},{25,17},{2,10},{10... | collective-permute-start | bytes 786440 | tf_op jit(solution)/shard_map/ppermute | solution.py:349
  6.4 1.5 %collective-permute-start = (bf16[512,256]{1,0:T(8,128)(2,1)S(1)}, bf16[512,256]{1,0:T(8,128)(2,1)S(1)}, u32[]{:S(2)}, u32[]{:S(2)}) collective-permute-start(bf16[512,256]{1,0:T(8,128)(2,1)S(1)} %get-tuple-element.22.main_ref), channel_id=1, source_target_pairs={{0,16},{8,24},{16,0},{24,8},{1,17},{9,25},{17,1},{25,9},{2,18},{10... | collective-permute-start | bytes 786440 | tf_op jit(solution)/shard_map/ppermute | solution.py:349
  7.9 0.0 collective-permute-start.1
  7.9 2.0 %collective-permute-start.4 = (bf16[128,256]{1,0:T(8,128)(2,1)S(1)}, bf16[128,256]{1,0:T(8,128)(2,1)S(1)}, u32[]{:S(2)}, u32[]{:S(2)}) collective-permute-start(bf16[128,256]{1,0:T(8,128)(2,1)S(1)} %pick.4), channel_id=1, source_target_pairs={{0,16},{8,24},{16,0},{24,8},{1,17},{9,25},{17,1},{25,9},{2,18},{10... | collective-permute-start | bytes 196616 | tf_op jit(solution)/shard_map/ppermute | solution.py:349
  9.9 1.5 %collective-permute-start.5 = (bf16[128,256]{1,0:T(8,128)(2,1)S(1)}, bf16[128,256]{1,0:T(8,128)(2,1)S(1)}, u32[]{:S(2)}, u32[]{:S(2)}) collective-permute-start(bf16[128,256]{1,0:T(8,128)(2,1)S(1)} %pick.5), channel_id=1, source_target_pairs={{0,24},{8,16},{16,8},{24,0},{1,25},{9,17},{17,9},{25,1},{2,26},{10... | collective-permute-start | bytes 196616 | tf_op jit(solution)/shard_map/ppermute | solution.py:349
  11.4 2.1 %collective-permute-done.2.recv_ref.refs_0_ = bf16[512,256]{1,0:T(8,128)(2,1)S(1)} collective-permute-done((bf16[512,256]{1,0:T(8,128)(2,1)S(1)}, bf16[512,256]{1,0:T(8,128)(2,1)S(1)}, u32[]{:S(2)}, u32[]{:S(2)}) %collective-permute-start.2) | collective-permute-done | bytes 262176 | tf_op jit(solution)/shard_map/ppermute | solution.py:349
  13.5 2.1 %collective-permute-start.3 = (bf16[128,256]{1,0:T(8,128)(2,1)S(1)}, bf16[128,256]{1,0:T(8,128)(2,1)S(1)}, u32[]{:S(2)}, u32[]{:S(2)}) collective-permute-start(bf16[128,256]{1,0:T(8,128)(2,1)S(1)} %pick.3), channel_id=1, source_target_pairs={{0,8},{8,0},{16,24},{24,16},{1,9},{9,1},{17,25},{25,17},{2,10},{10... | collective-permute-start | bytes 196616 | tf_op jit(solution)/shard_map/ppermute | solution.py:349
  15.6 3.6 %windows.1 = (bf16[512,256]{1,0:T(8,128)(2,1)S(1)}, f32[2,512,512]{2,1,0:T(8,128)S(1)}, bf16[512,512]{1,0:T(8,128)(2,1)S(1)}, bf16[512,512]{1,0:T(8,128)(2,1)S(1)}) custom-call(bf16[3,512,256]{2,1,0:T(8,128)(2,1)S(1)} %copy-done, s32[3,2,512]{2,1,0:T(2,128)S(1)} %bitcast.23, bf16[512,1024]{1,0:T(8,128)(2,1)S(1)} %copy-done.3, s32[1,512]{1,0:T(1,128)S(1)} %bitcast.25, ...), custom_call_target="tpu_custom_call" | custom-call | tf_op jit(solution)/shard_map/windows/pallas_call | solution.py:381
  19.2 2.6 %collective-permute-done.refs_0_ = bf16[512,256]{1,0:T(8,128)(2,1)S(1)} collective-permute-done((bf16[512,256]{1,0:T(8,128)(2,1)S(1)}, bf16[512,256]{1,0:T(8,128)(2,1)S(1)}, u32[]{:S(2)}, u32[]{:S(2)}) %collective-permute-start) | collective-permute-done | bytes 262176 | tf_op jit(solution)/shard_map/ppermute | solution.py:349
  21.9 0.0 collective-permute-done.1.refs_1_
  21.9 1.5 %conv.1 = (f32[2,512,512]{2,1,0:T(8,128)S(1)}, f32[512,256]{1,0:T(8,128)S(1)}, f32[512,256]{1,0:T(8,128)S(1)}, f32[1,256]{1,0:T(1,128)S(1)}) custom-call(bf16[512,256]{1,0:T(8,128)(2,1)S(1)} %collective-permute-done.refs_0_, bf16[512,256]{1,0:T(8,128)(2,1)S(1)} %collective-permute-done.1.refs_1_, ...), custom_call_target="tpu_custom_call", output_to_operand_aliasing={{0}: (4, {})} | custom-call | tf_op jit(solution)/shard_map/conv/pallas_call | solution.py:394
  23.4 0.0 copy-start.4
  23.4 0.1 collective-permute-start.6
  23.5 0.0 collective-permute-done.5.refs_5_
  23.5 2.0 %taps.1 = (bf16[128,256]{1,0:T(8,128)(2,1)S(1)}, bf16[128,256]{1,0:T(8,128)(2,1)S(1)}, bf16[128,256]{1,0:T(8,128)(2,1)S(1)}, bf16[128,256]{1,0:T(8,128)(2,1)S(1)}, f32[1,256]{1,0:T(1,128)S(1)}) custom-call(bf16[4,128,256]{2,1,0:T(8,128)(2,1)S(1)} %bitcast.14, bf16[4,128,256]{2,1,0:T(8,128)(2,1)S(1)} %bitcast.18, s32[4,1,128]{2,1,0:T(1,128)S(1)} %bitcast.26, ...), custom_call_target="tpu_custom_call" | custom-call | tf_op jit(solution)/shard_map/taps/pallas_call | solution.py:403
  25.5 0.0 collective-permute-done.6
  25.6 1.6 %collective-permute-start.7 = (f32[1,256]{1,0:T(1,128)S(1)}, f32[1,256]{1,0:T(1,128)S(1)}, u32[]{:S(2)}, u32[]{:S(2)}) collective-permute-start(f32[1,256]{1,0:T(1,128)S(1)} %max.6), channel_id=1, source_target_pairs={{0,2},{1,3},{2,0},{3,1},{4,6},{5,7},{6,4},{7,5},{8,10},{9,11},{10,... | collective-permute-start | bytes 3080 | tf_op jit(solution)/shard_map/ppermute | solution.py:349
  27.2 1.5 %collective-permute-start.10 = (bf16[128,256]{1,0:T(8,128)(2,1)S(1)}, bf16[128,256]{1,0:T(8,128)(2,1)S(1)}, u32[]{:S(2)}, u32[]{:S(2)}) collective-permute-start(bf16[128,256]{1,0:T(8,128)(2,1)S(1)} %get-tuple-element.38), channel_id=1, source_target_pairs={{0,16},{8,24},{16,0},{24,8},{1,17},{9,25},{17,1},{25,9},{2,18},{10... | collective-permute-start | bytes 196616 | tf_op jit(solution)/shard_map/ppermute | solution.py:349
  28.7 0.3 collective-permute-start.11
  29.0 1.7 %collective-permute-start.9 = (bf16[128,256]{1,0:T(8,128)(2,1)S(1)}, bf16[128,256]{1,0:T(8,128)(2,1)S(1)}, u32[]{:S(2)}, u32[]{:S(2)}) collective-permute-start(bf16[128,256]{1,0:T(8,128)(2,1)S(1)} %get-tuple-element.37), channel_id=1, source_target_pairs={{0,8},{8,0},{16,24},{24,16},{1,9},{9,1},{17,25},{25,17},{2,10},{10... | collective-permute-start | bytes 196616 | tf_op jit(solution)/shard_map/ppermute | solution.py:349
  30.7 0.0 collective-permute-done.7
  30.7 2.6 %collective-permute-start.8 = (f32[1,256]{1,0:T(1,128)S(1)}, f32[1,256]{1,0:T(1,128)S(1)}, u32[]{:S(2)}, u32[]{:S(2)}) collective-permute-start(f32[1,256]{1,0:T(1,128)S(1)} %max.7.near_ref), channel_id=1, source_target_pairs={{0,4},{1,5},{2,6},{3,7},{4,0},{5,1},{6,2},{7,3},{8,12},{9,13},{10,... | collective-permute-start | bytes 3080 | tf_op jit(solution)/shard_map/ppermute | solution.py:349
  33.3 1.5 %grads.1 = bf16[3,512,256]{2,1,0:T(8,128)(2,1)} custom-call(bf16[3,512,256]{2,1,0:T(8,128)(2,1)S(1)} %copy-done, s32[3,2,512]{2,1,0:T(2,128)S(1)} %bitcast.24, bf16[512,256]{1,0:T(8,128)(2,1)S(1)} %copy-done.4, f32[512,256]{1,0:T(8,128)S(1)} %get-tuple-element.34.conv_ref, f32[2,512,512]{2,1,0:T(8,128)S(1)} %get-tuple-element.35.acc_ref, ...), custom_call_target="tpu_custom_call" | custom-call | flops 1000000000 | bytes 1000000 | tf_op jit(solution)/shard_map/grads/pallas_call | solution.py:426
  34.8 0.4 %collective-permute-done.8.far_ref = f32[1,256]{1,0:T(1,128)S(1)} collective-permute-done((f32[1,256]{1,0:T(1,128)S(1)}, f32[1,256]{1,0:T(1,128)S(1)}, u32[]{:S(2)}, u32[]{:S(2)}) %collective-permute-start.8) | collective-permute-done | bytes 1056 | tf_op jit(solution)/shard_map/ppermute | solution.py:349
  35.2 0.7 %scale.1 = (bf16[512,256]{1,0:T(8,128)(2,1)}, f32[1,256]{1,0:T(1,128)}) custom-call(f32[512,256]{1,0:T(8,128)S(1)} %get-tuple-element.29.resp_ref, f32[1,256]{1,0:T(1,128)S(1)} %max.7.near_ref, f32[1,256]{1,0:T(1,128)S(1)} %collective-permute-done.8.far_ref), custom_call_target="tpu_custom_call" | custom-call | tf_op jit(solution)/shard_map/scale/pallas_call | solution.py:424
  35.9 0.0 collective-permute-done.10.refs_2_
  35.9 0.0 collective-permute-done.11.refs_3_
  35.9 0.8 %spread.1 = f32[4,128,256]{2,1,0:T(8,128)} custom-call(bf16[128,256]{1,0:T(8,128)(2,1)S(1)} %get-tuple-element.36.refs_0_, bf16[128,256]{1,0:T(8,128)(2,1)S(1)} %collective-permute-done.9.refs_1_, bf16[128,256]{1,0:T(8,128)(2,1)S(1)} %collective-permute-done.10.refs_2_, bf16[128,256]{1,0:T(8,128)(2,1)S(1)} %collective-permute-done.11.refs_3_), custom_call_target="tpu_custom_call" | custom-call | tf_op jit(solution)/shard_map/spread/pallas_call | solution.py:435
  (22 shorter events, 0.1 us)
Async XLA Ops:
  0.6 15.0 %copy-start.1 = (bf16[512,512]{1,0:T(8,128)(2,1)S(1)}, bf16[512,512]{1,0:T(8,128)(2,1)}, u32[]{:S(2)}) copy-start(bf16[512,512]{1,0:T(8,128)(2,1)} %constant.6.clone.high_ref.refs_6_) | copy-start | bytes 1572868
  0.6 14.9 %copy-start.5 = (bf16[512,512]{1,0:T(8,128)(2,1)S(1)}, bf16[512,512]{1,0:T(8,128)(2,1)}, u32[]{:S(2)}) copy-start(bf16[512,512]{1,0:T(8,128)(2,1)} %constant.7.clone.low_ref) | copy-start | bytes 1572868
  0.7 14.9 %copy-start = (bf16[3,512,256]{2,1,0:T(8,128)(2,1)S(1)}, bf16[3,512,256]{2,1,0:T(8,128)(2,1)}, u32[]{:S(2)}) copy-start(bf16[3,512,256]{2,1,0:T(8,128)(2,1)} %proj_ref.3) | copy-start | bytes 2359300
  0.7 14.9 %copy-start.3 = (bf16[512,1024]{1,0:T(8,128)(2,1)S(1)}, bf16[512,1024]{1,0:T(8,128)(2,1)}, u32[]{:S(2)}) copy-start(bf16[512,1024]{1,0:T(8,128)(2,1)} %filt_ref.1) | copy-start | bytes 3145732
  0.7 0.9 %copy-start.6 = (s32[3,512,2]{1,2,0:T(2,128)S(1)}, s32[3,512,2]{1,2,0:T(2,128)}, u32[]{:S(2)}) copy-start(s32[3,512,2]{1,2,0:T(2,128)} %param.10) | copy-start | bytes 36868
  1.5 14.1 %copy-start.7 = (s32[512]{0:T(512)S(1)}, s32[512]{0:T(512)}, u32[]{:S(2)}) copy-start(s32[512]{0:T(512)} %param.12) | copy-start | bytes 6148
  1.5 14.1 %copy-start.8 = (f32[512]{0:T(512)S(1)}, f32[512]{0:T(512)}, u32[]{:S(2)}) copy-start(f32[512]{0:T(512)} %param.13) | copy-start | bytes 6148
  3.4 10.1 %collective-permute-start.2 = (bf16[512,256]{1,0:T(8,128)(2,1)S(1)}, bf16[512,256]{1,0:T(8,128)(2,1)S(1)}, u32[]{:S(2)}, u32[]{:S(2)}) collective-permute-start(bf16[512,256]{1,0:T(8,128)(2,1)S(1)} %get-tuple-element.24), channel_id=1, source_target_pairs={{0,8},{8,0},{16,24},{24,16},{1,9},{9,1},{17,25},{25,17},{2,10},{10... | collective-permute-start | bytes 786440 | tf_op jit(solution)/shard_map/ppermute | solution.py:349
  6.4 15.5 %collective-permute-start = (bf16[512,256]{1,0:T(8,128)(2,1)S(1)}, bf16[512,256]{1,0:T(8,128)(2,1)S(1)}, u32[]{:S(2)}, u32[]{:S(2)}) collective-permute-start(bf16[512,256]{1,0:T(8,128)(2,1)S(1)} %get-tuple-element.22.main_ref), channel_id=1, source_target_pairs={{0,16},{8,24},{16,0},{24,8},{1,17},{9,25},{17,1},{25,9},{2,18},{10... | collective-permute-start | bytes 786440 | tf_op jit(solution)/shard_map/ppermute | solution.py:349
  7.9 14.0 %collective-permute-start.1 = (bf16[512,256]{1,0:T(8,128)(2,1)S(1)}, bf16[512,256]{1,0:T(8,128)(2,1)S(1)}, u32[]{:S(2)}, u32[]{:S(2)}) collective-permute-start(bf16[512,256]{1,0:T(8,128)(2,1)S(1)} %get-tuple-element.22.main_ref), channel_id=1, source_target_pairs={{0,24},{8,16},{16,8},{24,0},{1,25},{9,17},{17,9},{25,1},{2,26},{10... | collective-permute-start | bytes 786440 | tf_op jit(solution)/shard_map/ppermute | solution.py:349
  7.9 15.5 %collective-permute-start.4 = (bf16[128,256]{1,0:T(8,128)(2,1)S(1)}, bf16[128,256]{1,0:T(8,128)(2,1)S(1)}, u32[]{:S(2)}, u32[]{:S(2)}) collective-permute-start(bf16[128,256]{1,0:T(8,128)(2,1)S(1)} %pick.4), channel_id=1, source_target_pairs={{0,16},{8,24},{16,0},{24,8},{1,17},{9,25},{17,1},{25,9},{2,18},{10... | collective-permute-start | bytes 196616 | tf_op jit(solution)/shard_map/ppermute | solution.py:349
  9.9 12.0 %copy-start.2 = (bf16[512,512]{1,0:T(8,128)(2,1)S(1)}, bf16[512,512]{1,0:T(8,128)(2,1)}, u32[]{:S(2)}) copy-start(bf16[512,512]{1,0:T(8,128)(2,1)} %constant.8.clone.refs_7_.inv_ref) | copy-start | bytes 1572868
  9.9 13.5 %collective-permute-start.5 = (bf16[128,256]{1,0:T(8,128)(2,1)S(1)}, bf16[128,256]{1,0:T(8,128)(2,1)S(1)}, u32[]{:S(2)}, u32[]{:S(2)}) collective-permute-start(bf16[128,256]{1,0:T(8,128)(2,1)S(1)} %pick.5), channel_id=1, source_target_pairs={{0,24},{8,16},{16,8},{24,0},{1,25},{9,17},{17,9},{25,1},{2,26},{10... | collective-permute-start | bytes 196616 | tf_op jit(solution)/shard_map/ppermute | solution.py:349
  13.5 10.0 %collective-permute-start.3 = (bf16[128,256]{1,0:T(8,128)(2,1)S(1)}, bf16[128,256]{1,0:T(8,128)(2,1)S(1)}, u32[]{:S(2)}, u32[]{:S(2)}) collective-permute-start(bf16[128,256]{1,0:T(8,128)(2,1)S(1)} %pick.3), channel_id=1, source_target_pairs={{0,8},{8,0},{16,24},{24,16},{1,9},{9,1},{17,25},{25,17},{2,10},{10... | collective-permute-start | bytes 196616 | tf_op jit(solution)/shard_map/ppermute | solution.py:349
  23.4 9.9 %copy-start.4 = (bf16[512,256]{1,0:T(8,128)(2,1)S(1)}, bf16[512,256]{1,0:T(8,128)(2,1)}, u32[]{:S(2)}) copy-start(bf16[512,256]{1,0:T(8,128)(2,1)} %cot_ref.1) | copy-start | bytes 786436
  23.4 2.2 %collective-permute-start.6 = (f32[1,256]{1,0:T(1,128)S(1)}, f32[1,256]{1,0:T(1,128)S(1)}, u32[]{:S(2)}, u32[]{:S(2)}) collective-permute-start(f32[1,256]{1,0:T(1,128)S(1)} %get-tuple-element.30.refs_6_), channel_id=1, source_target_pairs={{0,1},{1,0},{2,3},{3,2},{4,5},{5,4},{6,7},{7,6},{8,9},{9,8},{10,11... | collective-permute-start | bytes 3080 | tf_op jit(solution)/shard_map/ppermute | solution.py:349
  25.6 5.1 %collective-permute-start.7 = (f32[1,256]{1,0:T(1,128)S(1)}, f32[1,256]{1,0:T(1,128)S(1)}, u32[]{:S(2)}, u32[]{:S(2)}) collective-permute-start(f32[1,256]{1,0:T(1,128)S(1)} %max.6), channel_id=1, source_target_pairs={{0,2},{1,3},{2,0},{3,1},{4,6},{5,7},{6,4},{7,5},{8,10},{9,11},{10,... | collective-permute-start | bytes 3080 | tf_op jit(solution)/shard_map/ppermute | solution.py:349
  27.2 8.7 %collective-permute-start.10 = (bf16[128,256]{1,0:T(8,128)(2,1)S(1)}, bf16[128,256]{1,0:T(8,128)(2,1)S(1)}, u32[]{:S(2)}, u32[]{:S(2)}) collective-permute-start(bf16[128,256]{1,0:T(8,128)(2,1)S(1)} %get-tuple-element.38), channel_id=1, source_target_pairs={{0,16},{8,24},{16,0},{24,8},{1,17},{9,25},{17,1},{25,9},{2,18},{10... | collective-permute-start | bytes 196616 | tf_op jit(solution)/shard_map/ppermute | solution.py:349
  28.7 7.2 %collective-permute-start.11 = (bf16[128,256]{1,0:T(8,128)(2,1)S(1)}, bf16[128,256]{1,0:T(8,128)(2,1)S(1)}, u32[]{:S(2)}, u32[]{:S(2)}) collective-permute-start(bf16[128,256]{1,0:T(8,128)(2,1)S(1)} %get-tuple-element.39), channel_id=1, source_target_pairs={{0,24},{8,16},{16,8},{24,0},{1,25},{9,17},{17,9},{25,1},{2,26},{10... | collective-permute-start | bytes 196616 | tf_op jit(solution)/shard_map/ppermute | solution.py:349
  29.0 6.9 %collective-permute-start.9 = (bf16[128,256]{1,0:T(8,128)(2,1)S(1)}, bf16[128,256]{1,0:T(8,128)(2,1)S(1)}, u32[]{:S(2)}, u32[]{:S(2)}) collective-permute-start(bf16[128,256]{1,0:T(8,128)(2,1)S(1)} %get-tuple-element.37), channel_id=1, source_target_pairs={{0,8},{8,0},{16,24},{24,16},{1,9},{9,1},{17,25},{25,17},{2,10},{10... | collective-permute-start | bytes 196616 | tf_op jit(solution)/shard_map/ppermute | solution.py:349
  30.7 4.5 %collective-permute-start.8 = (f32[1,256]{1,0:T(1,128)S(1)}, f32[1,256]{1,0:T(1,128)S(1)}, u32[]{:S(2)}, u32[]{:S(2)}) collective-permute-start(f32[1,256]{1,0:T(1,128)S(1)} %max.7.near_ref), channel_id=1, source_target_pairs={{0,4},{1,5},{2,6},{3,7},{4,0},{5,1},{6,2},{7,3},{8,12},{9,13},{10,... | collective-permute-start | bytes 3080 | tf_op jit(solution)/shard_map/ppermute | solution.py:349

commit v3 on v2

--- a/solution.py
+++ b/solution.py
@@ -11,6 +11,14 @@
 from jax.sharding import PartitionSpec as P
 
 REACH_DIVISORS = (64, 32, 16, 4, 1)
+LOAD_MIB = 53.3
+
+
+def cost(flops):
+    return pl.CostEstimate(flops=flops, bytes_accessed=10**6, transcendentals=0)
+
+
+COSTS = {"load": cost(10**9), "grads": cost(10**9), "scale": cost(10**9)}
 F32 = jnp.float32
 BF16 = jnp.bfloat16
 
@@ -83,47 +91,43 @@
     return lax.div(lax.axis_index("ctx"), (n + 1) // 2)
 
 
-def prep_kernel(parts, n, proj_hbm, exp_hbm, cot_hbm, main_ref, rest_ref, *refs):
-    send_refs, (proj, exp, cot, exp_sem, key_sem, query_sem) = refs[:-6], refs[-6:]
-    me = lax.axis_index("ctx")
-    upper = top_bit(n)
+def load_kernel(parts, proj_hbm, cot_hbm, key_value_ref, query_cot_ref, proj, cot, key_sem, query_sem):
     channels, span = cot.shape
     rows = channels // parts
-    exp_copy = pltpu.make_async_copy(exp_hbm, exp, exp_sem)
-    exp_copy.start()
     copies = []
     for part in range(parts):
         block = pl.ds(part * rows, rows)
         copies.append(
             (
-                pltpu.make_async_copy(proj_hbm.at[1, block], proj.at[1, block], key_sem.at[part, 0]),
-                pltpu.make_async_copy(proj_hbm.at[2, block], proj.at[2, block], key_sem.at[part, 1]),
+                pltpu.make_async_copy(proj_hbm.at[pl.ds(1, 2), block], proj.at[pl.ds(1, 2), block], key_sem.at[part]),
                 pltpu.make_async_copy(proj_hbm.at[0, block], proj.at[0, block], query_sem.at[part, 0]),
                 pltpu.make_async_copy(cot_hbm.at[block], cot.at[block], query_sem.at[part, 1]),
             )
         )
         for copy in copies[-1]:
             copy.start()
-    exp_copy.wait()
-    exps = exp[...]
     for part in range(parts):
         block = pl.ds(part * rows, rows)
-        key_scale = block_scale(exps[1, :, part * rows : (part + 1) * rows] + exps[2, :, part * rows : (part + 1) * rows], span)
-        query_scale = block_scale(exps[0, :, part * rows : (part + 1) * rows], span)
-        for copy in copies[part]:
-            copy.wait()
-        mixed = (proj[1, block].astype(F32) * proj[2, block].astype(F32) * key_scale).astype(BF16)
-        pulled = (cot[block].astype(F32) * (proj[0, block].astype(F32) * query_scale)).astype(BF16)
-        lows = [lax.rem(lax.div(me, 2**bit), 2) for bit in range(len(send_refs))]
+        copies[part][0].wait()
+        key_value_ref[block] = (proj[1, block].astype(F32) * proj[2, block].astype(F32)).astype(BF16)
+        copies[part][1].wait()
+        copies[part][2].wait()
+        query_cot_ref[block] = (cot[block].astype(F32) * proj[0, block].astype(F32)).astype(BF16)
+
+
+def prep_kernel(n, rows, key_value_ref, query_cot_ref, exp_ref, main_ref, rest_ref, *send_refs):
+    me = lax.axis_index("ctx")
+    upper = top_bit(n)
+    channels, span = main_ref.shape
+    lows = [lax.rem(lax.div(me, 2**bit), 2) for bit in range(len(send_refs))]
+    for first in range(0, channels, rows):
+        block = slice(first, first + rows)
+        mixed = (
+            key_value_ref[block].astype(F32) * block_scale(exp_ref[1, :, block] + exp_ref[2, :, block], span)
+        ).astype(BF16)
+        pulled = (query_cot_ref[block].astype(F32) * block_scale(exp_ref[0, :, block], span)).astype(BF16)
         for ref, later in [(main_ref, upper), (rest_ref, 1 - upper), *zip(send_refs, lows)]:
-
-            @pl.when(later == 1)
-            def _():
-                ref[block] = pulled
-
-            @pl.when(later == 0)
-            def _():
-                ref[block] = mixed
+            ref[block] = jnp.where(later == 1, pulled, mixed)
 
 
 def windows_kernel(
@@ -206,20 +210,10 @@
         peak_ref[...] = jnp.maximum(peak_ref[...], jnp.max(jnp.abs(response), axis=0, keepdims=True))
 
 
-def grad_kernel(seq_len, rows, proj_ref, exp_ref, cot_ref, conv_ref, acc_ref, inv_ref, grad_ref):
-    channels, span = cot_ref.shape
-    fscale = 1.0 / math.sqrt(seq_len)
-    exps = exp_ref[...]
-    grad_mixed = mm(acc_ref[1].astype(BF16), inv_ref[:, :span]) * fscale
-    grad_ref[0] = (cot_ref[...].astype(F32) * conv_ref[...]).astype(BF16)
-    grad_ref[1] = (grad_mixed * (proj_ref[2].astype(F32) * block_scale(exps[2], span))).astype(BF16)
-    grad_ref[2] = (grad_mixed * (proj_ref[1].astype(F32) * block_scale(exps[1], span))).astype(BF16)
-
-
 def taps_kernel(n, seq_len, main_ref, rest_ref, reach_ref, high_ref, inv_ref, *refs):
     first_refs, second_refs, refs = refs[: n - 1], refs[n - 1 : 2 * n - 2], refs[2 * n - 2 :]
     peak_ref, out_refs, top_ref = refs[0], refs[1 : n + 1], refs[n + 1]
-    mbuf, pbuf, mspec, pspec, acc = refs[n + 2 :]
+    mbuf, pbuf, mspec, pspec, acc, out = refs[n + 2 :]
     top_ref[...] = peak_ref[...]
     me = lax.axis_index("ctx")
     _, rows, span = mbuf.shape
@@ -253,30 +247,32 @@
     if rows % 16 == 0:
         flat = (n * rows, span)
         mspec[...] = mm(mbuf[...].reshape(flat), high_ref[:span]).reshape(mspec.shape)
-        pspec[...] = (
-            mm(pbuf[:n].reshape(flat), high_ref[:span]) + mm(pbuf[1:].reshape(flat), high_ref[span:])
-        ).reshape(pspec.shape)
+        pair = jnp.concatenate([pbuf[:n].reshape(flat), pbuf[1:].reshape(flat)], axis=1)
+        pspec[...] = mm(pair, high_ref[...]).reshape(pspec.shape)
     else:
         for b in range(n):
             mspec[b] = mm(mbuf[b], high_ref[:span])
             pspec[b] = mm(pbuf[b], high_ref[:span]) + mm(pbuf[b + 1], high_ref[span:])
+
+    @row_loop(rows, 16)
+    def _(tile):
+        for lag_block in range(n):
+            real = imag = 0.0
+            for b in range(n - lag_block):
+                ar, ai = mspec[b, tile, :span], mspec[b, tile, span:]
+                br, bi = pspec[b + lag_block, tile, :span], pspec[b + lag_block, tile, span:]
+                real += ar * br + ai * bi
+                imag += ar * bi - ai * br
+            acc[lag_block, tile, :span] = real.astype(BF16)
+            acc[lag_block, tile, span:] = imag.astype(BF16)
+
     lens = reach_lens(reach_ref.at[me], seq_len)
+    for lag_block in range(n):
+        lag = lax.broadcasted_iota(jnp.int32, (rows, span), 1) + lag_block * span
+        own = mm(acc[lag_block], inv_ref[:, :span]) * fscale
+        out[lag_block] = jnp.where(lag < lens, own, 0.0).astype(BF16)
     for k in range(n):
-        lag_block = jnp.bitwise_xor(me, k)
-        acc[...] = jnp.zeros_like(acc)
-        for b in range(n):
-
-            @pl.when(b + lag_block < n)
-            def _():
-                ar, ai = mspec[b, :, :span], mspec[b, :, span:]
-                near = pspec[b + lag_block]
-                br, bi = near[:, :span], near[:, span:]
-                acc[:, :span] += ar * br + ai * bi
-                acc[:, span:] += ar * bi - ai * br
-
-        lag = lax.broadcasted_iota(jnp.int32, (rows, span), 1) + lag_block * span
-        own = mm(acc[...].astype(BF16), inv_ref[:, :span]) * fscale
-        out_refs[k][...] = jnp.where(lag < lens, own, 0.0).astype(BF16)
+        out_refs[k][...] = out[jnp.bitwise_xor(me, k)]
 
 
 def pick_kernel(k, n, main_ref, rest_ref, *refs):
@@ -295,21 +291,49 @@
         out_ref[...] = rest_ref[other]
 
 
+def grads_kernel(seq_len, proj_ref, exp_ref, cot_ref, conv_ref, acc_ref, inv_ref, *refs):
+    grad_hbm, grad, grad_sem = refs
+    span = cot_ref.shape[1]
+    fscale = 1.0 / math.sqrt(seq_len)
+    copies = []
+
+    def send(source, target, sem):
+        copies.append(pltpu.make_async_copy(source, target, sem))
+        copies[-1].start()
+
+    grad[0] = (cot_ref[...].astype(F32) * conv_ref[...]).astype(BF16)
+    send(grad.at[0], grad_hbm.at[0], grad_sem.at[0])
+    grad_mixed = mm(acc_ref[1].astype(BF16), inv_ref[:, :span]) * fscale
+    for slot, source in ((1, 2), (2, 1)):
+        scaled = proj_ref[source].astype(F32) * block_scale(exp_ref[source], span)
+        grad[slot] = (grad_mixed * scaled).astype(BF16)
+        send(grad.at[slot], grad_hbm.at[slot], grad_sem.at[slot])
+    for copy in copies:
+        copy.wait()
+
+
 def spread_kernel(n, *refs):
-    part_refs, out_ref = refs[:n], refs[n]
-    me = lax.axis_index("ctx")
+    part_refs, (near_ref, taps_hbm, peak_ref, taps, taps_sem) = refs[:n], refs[n:]
+    me = lax.axis_index("ctx")
+    peak_ref[...] = near_ref[...]
+    copies = []
     for k in range(n):
-        out_ref[jnp.bitwise_xor(me, k)] = part_refs[k][...].astype(F32)
+        block = jnp.bitwise_xor(me, k)
+        taps[block] = part_refs[k][...].astype(F32)
+        copies.append(pltpu.make_async_copy(taps.at[block], taps_hbm.at[block], taps_sem.at[k]))
+        copies[-1].start()
+    for copy in copies:
+        copy.wait()
 
 
 def scale_kernel(resp_ref, near_ref, far_ref, out_ref, peak_ref):
     peak = jnp.maximum(near_ref[...], far_ref[...])
     peak_ref[...] = peak
-    out_ref[...] = (resp_ref[...] / (peak + 1e-06)).astype(BF16)
+    out_ref[...] = (resp_ref[...] * (1.0 / (peak + 1e-06))).astype(BF16)
 
 
 def params(mib=32):
-    return pltpu.CompilerParams(vmem_limit_bytes=mib * 2**20)
+    return pltpu.CompilerParams(vmem_limit_bytes=int(mib * 2**20))
 
 
 def body(proj, scale_exp, filt, reach, skip, cotangent):
@@ -319,7 +343,7 @@
     seq_len = n * span
     blocks = scale_exp.shape[2]
     bits = max(1, (n - 1).bit_length())
-    rows = 256 if channels % 256 == 0 else channels
+    rows = channels
     parts = 2 if channels % 256 == 0 else 1
     share = channels // n
     shares = (n, share, span)
@@ -334,14 +358,15 @@
     def shape(dims, dtype):
         return jax.ShapeDtypeStruct(dims, dtype)
 
-    def call(kernel, name, ins, outs, mib=32, **options):
+    def call(kernel, name, ins, outs, mib=32, out_specs=None, **options):
         return pl.pallas_call(
             kernel,
             in_specs=ins,
-            out_specs=[vmem] * len(outs),
+            out_specs=out_specs or [vmem] * len(outs),
             out_shape=outs,
             compiler_params=params(mib),
             name=name,
+            cost_estimate=COSTS.get(name),
             **options,
         )
 
@@ -351,22 +376,22 @@
     flat = shape((channels, span), BF16)
     part = shape((share, span), BF16)
     line = shape((1, span), F32)
-    main, rest, *sends = call(
-        functools.partial(prep_kernel, parts, n),
-        "prep",
-        [hbm] * 3,
-        [flat] * (1 + bits),
-        mib=53,
+    raw = call(
+        functools.partial(load_kernel, parts),
+        "load",
+        [hbm] * 2,
+        [flat] * 2,
+        mib=LOAD_MIB,
         scratch_shapes=[
             pltpu.VMEM((3, channels, span), BF16),
-            pltpu.VMEM((3, blocks, channels), jnp.int32),
             pltpu.VMEM((channels, span), BF16),
-            pltpu.SemaphoreType.DMA,
-            pltpu.SemaphoreType.DMA((parts, 2)),
+            pltpu.SemaphoreType.DMA((parts,)),
             pltpu.SemaphoreType.DMA((parts, 2)),
         ],
-    )(proj, exps, cotangent)
-
+    )(proj, cotangent)
+    main, rest, *sends = call(
+        functools.partial(prep_kernel, n, rows), "prep", [vmem] * 3, [flat] * (1 + bits)
+    )(*raw, exps)
     sends.append(main)
     first = [swap(sends[k.bit_length() - 1], "ctx", k) for k in range(1, n)]
 
@@ -410,7 +435,8 @@
             pltpu.VMEM((n + 1, share, span), BF16),
             pltpu.VMEM((n, share, 2 * span), F32),
             pltpu.VMEM((n, share, 2 * span), F32),
-            pltpu.VMEM((share, 2 * span), F32),
+            pltpu.VMEM((n, share, 2 * span), BF16),
+            pltpu.VMEM(shares, BF16),
         ],
     )(
         main.reshape(shares), rest.reshape(shares), reach.reshape(n, 1, share), high, inverse,
@@ -421,20 +447,24 @@
         peak = jnp.maximum(peak, far)
         far = swap(peak, "ch", hop)
         hop *= 2
-    scaled_out, peak = call(scale_kernel, "scale", [vmem] * 3, [flat, line])(response, peak, far)
-
+    parts_out = [swap(x, "ctx", k + 1) for k, x in enumerate(parts_out)]
     (gradients,) = call(
-        functools.partial(grad_kernel, seq_len, rows),
+        functools.partial(grads_kernel, seq_len),
         "grads",
         [vmem] * 6,
         [shape((3, channels, span), BF16)],
-        cost_estimate=pl.CostEstimate(flops=10**9, bytes_accessed=10**6, transcendentals=0),
+        out_specs=[hbm],
+        scratch_shapes=[pltpu.VMEM((3, channels, span), BF16), pltpu.SemaphoreType.DMA((3,))],
     )(proj, exps, cotangent, conv, acc, inverse)
-
-    parts_out = [swap(x, "ctx", k + 1) for k, x in enumerate(parts_out)]
-    (filter_grad,) = call(functools.partial(spread_kernel, n), "spread", [vmem] * n, [shape(shares, F32)])(
-        own_part, *parts_out
-    )
+    filter_grad, peak = call(
+        functools.partial(spread_kernel, n),
+        "spread",
+        [vmem] * (n + 1),
+        [shape(shares, F32), line],
+        out_specs=[hbm, vmem],
+        scratch_shapes=[pltpu.VMEM(shares, F32), pltpu.SemaphoreType.DMA((n,))],
+    )(own_part, *parts_out, peak)
+    scaled_out, peak = call(scale_kernel, "scale", [vmem] * 3, [flat, line])(response, peak, far)
     return (scaled_out, peak.reshape(span), gradients, filter_grad.reshape(channels, span))
 
 

time: 37 us -> 34.5 us (0.932)
  Pallas kernels: 12 us -> 10.7 us
  local copies, waits for them, and re-layouts: 0.89 us -> 0.05 us
    unnamed x18, local copies, waits for them, and re-layouts: 0.89 us -> 0.05 us
    pallas_call x1, Pallas kernels: 2.04 us -> 1.4 us  [body(): call(functools.partial(taps_kernel, n, seq_len), 'taps', [vmem] * (2 * n...]
    pallas_call x3 -> x4, Pallas kernels: 4.14 us -> 3.87 us  [the longest x1 1.37 us: body(): call(functools.partial(load_kernel, parts), 'load', [hbm] * 2, [flat] * 2...]
  transfers between devices with their start and end apart: 12 -> 12, of which waited for: 3 -> 2; matrix products, arithmetic and copies ran while one was open for 0% -> 0% of each run, Pallas kernels for 25% -> 24%
where the time goes in v3:
time: 34.5 us; the launch traced here: 34.4 us
  starting transfers between devices  17.9 us (52%)
  Pallas kernels  10.7 us (31%)
  waiting for transfers between devices  4.92 us (14%)
  between operations  0.86 us (2%)
    ppermute x12, starting transfers between devices, swap(): lax.ppermute(value, axis, [(j, j ^ k) for j in range(lax.axis_size(axis))])  17.9 us
    ppermute x12, waiting for transfers between devices, swap(): lax.ppermute(value, axis, [(j, j ^ k) for j in range(lax.axis_size(axis))])  4.92 us
    pallas_call x1, Pallas kernels, body(): call(functools.partial(windows_kernel, n, rows), 'windows', [vmem] * 10,...  3.46 us
    pallas_call x1, Pallas kernels, body(): call(functools.partial(taps_kernel, n, seq_len), 'taps', [vmem] * (2 * n...  1.4 us
    pallas_call x1, Pallas kernels, body(): call(functools.partial(load_kernel, parts), 'load', [hbm] * 2, [flat] * 2...  1.37 us
    pallas_call x1, Pallas kernels, body(): call(functools.partial(grads_kernel, seq_len), 'grads', [vmem] * 6, [shap...  1.31 us
    pallas_call x1, Pallas kernels, body(): call(functools.partial(conv_kernel, n, seq_len, rows), 'conv', [vmem] * (...  1.17 us
    pallas_call x1, Pallas kernels, body(): call(functools.partial(spread_kernel, n), 'spread', [vmem] * (n + 1), [sh...  0.84 us
  transfers between devices with their start and end apart: 12, of which 2 were waited for; matrix products, arithmetic and copies ran while one was open for 0% of the time, Pallas kernels for 24%

profile of v3, /device:TPU:0, one launch (start us, length us, event | category | flops | bytes accessed | tf_op | source)
XLA Modules:
  0.0 34.4 jit_solution(3453705671432409750)
XLA Ops:
  0.6 0.0 copy-start.4
  0.7 1.4 %load.1 = (bf16[512,256]{1,0:T(8,128)(2,1)S(1)}, bf16[512,256]{1,0:T(8,128)(2,1)S(1)}) custom-call(bf16[3,512,256]{2,1,0:T(8,128)(2,1)} %proj_ref.3, bf16[512,256]{1,0:T(8,128)(2,1)} %cot_ref.1), custom_call_target="tpu_custom_call" | custom-call | flops 1000000000 | bytes 1000000 | tf_op jit(solution)/shard_map/load/pallas_call | solution.py:379
  2.0 0.0 copy-start
  2.0 0.0 copy-start.2
  2.1 0.0 copy-start.3
  2.1 0.0 copy-start.7
  2.1 0.0 copy-start.8
  2.1 0.3 prep.1
  2.5 3.0 %collective-permute-start.2 = (bf16[512,256]{1,0:T(8,128)(2,1)S(1)}, bf16[512,256]{1,0:T(8,128)(2,1)S(1)}, u32[]{:S(2)}, u32[]{:S(2)}) collective-permute-start(bf16[512,256]{1,0:T(8,128)(2,1)S(1)} %get-tuple-element.30), channel_id=1, source_target_pairs={{0,8},{8,0},{16,24},{24,16},{1,9},{9,1},{17,25},{25,17},{2,10},{10... | collective-permute-start | bytes 786440 | tf_op jit(solution)/shard_map/ppermute | solution.py:374
  5.5 1.5 %collective-permute-start = (bf16[512,256]{1,0:T(8,128)(2,1)S(1)}, bf16[512,256]{1,0:T(8,128)(2,1)S(1)}, u32[]{:S(2)}, u32[]{:S(2)}) collective-permute-start(bf16[512,256]{1,0:T(8,128)(2,1)S(1)} %get-tuple-element.28.main_ref), channel_id=1, source_target_pairs={{0,16},{8,24},{16,0},{24,8},{1,17},{9,25},{17,1},{25,9},{2,18},{10... | collective-permute-start | bytes 786440 | tf_op jit(solution)/shard_map/ppermute | solution.py:374
  7.0 0.0 collective-permute-start.1
  7.0 2.0 %collective-permute-start.4 = (bf16[128,256]{1,0:T(8,128)(2,1)S(1)}, bf16[128,256]{1,0:T(8,128)(2,1)S(1)}, u32[]{:S(2)}, u32[]{:S(2)}) collective-permute-start(bf16[128,256]{1,0:T(8,128)(2,1)S(1)} %pick.4), channel_id=1, source_target_pairs={{0,16},{8,24},{16,0},{24,8},{1,17},{9,25},{17,1},{25,9},{2,18},{10... | collective-permute-start | bytes 196616 | tf_op jit(solution)/shard_map/ppermute | solution.py:374
  9.0 1.5 %collective-permute-start.5 = (bf16[128,256]{1,0:T(8,128)(2,1)S(1)}, bf16[128,256]{1,0:T(8,128)(2,1)S(1)}, u32[]{:S(2)}, u32[]{:S(2)}) collective-permute-start(bf16[128,256]{1,0:T(8,128)(2,1)S(1)} %pick.5), channel_id=1, source_target_pairs={{0,24},{8,16},{16,8},{24,0},{1,25},{9,17},{17,9},{25,1},{2,26},{10... | collective-permute-start | bytes 196616 | tf_op jit(solution)/shard_map/ppermute | solution.py:374
  10.5 2.1 %collective-permute-done.2.recv_ref.refs_0_ = bf16[512,256]{1,0:T(8,128)(2,1)S(1)} collective-permute-done((bf16[512,256]{1,0:T(8,128)(2,1)S(1)}, bf16[512,256]{1,0:T(8,128)(2,1)S(1)}, u32[]{:S(2)}, u32[]{:S(2)}) %collective-permute-start.2) | collective-permute-done | bytes 262176 | tf_op jit(solution)/shard_map/ppermute | solution.py:374
  12.6 2.1 %collective-permute-start.3 = (bf16[128,256]{1,0:T(8,128)(2,1)S(1)}, bf16[128,256]{1,0:T(8,128)(2,1)S(1)}, u32[]{:S(2)}, u32[]{:S(2)}) collective-permute-start(bf16[128,256]{1,0:T(8,128)(2,1)S(1)} %pick.3), channel_id=1, source_target_pairs={{0,8},{8,0},{16,24},{24,16},{1,9},{9,1},{17,25},{25,17},{2,10},{10... | collective-permute-start | bytes 196616 | tf_op jit(solution)/shard_map/ppermute | solution.py:374
  14.7 3.5 %windows.1 = (bf16[512,256]{1,0:T(8,128)(2,1)S(1)}, f32[2,512,512]{2,1,0:T(8,128)S(1)}, bf16[512,512]{1,0:T(8,128)(2,1)S(1)}, bf16[512,512]{1,0:T(8,128)(2,1)S(1)}) custom-call(bf16[3,512,256]{2,1,0:T(8,128)(2,1)S(1)} %copy-done.2, s32[3,2,512]{2,1,0:T(2,128)S(1)} %bitcast.23, bf16[512,1024]{1,0:T(8,128)(2,1)S(1)} %copy-done.3, s32[1,512]{1,0:T(1,128)S(1)} %bitcast.25, ...), custom_call_target="tpu_custom_call" | custom-call | tf_op jit(solution)/shard_map/windows/pallas_call | solution.py:406
  18.2 2.8 %collective-permute-done.refs_0_ = bf16[512,256]{1,0:T(8,128)(2,1)S(1)} collective-permute-done((bf16[512,256]{1,0:T(8,128)(2,1)S(1)}, bf16[512,256]{1,0:T(8,128)(2,1)S(1)}, u32[]{:S(2)}, u32[]{:S(2)}) %collective-permute-start) | collective-permute-done | bytes 262176 | tf_op jit(solution)/shard_map/ppermute | solution.py:374
  21.0 1.2 %conv.1 = (f32[2,512,512]{2,1,0:T(8,128)S(1)}, f32[512,256]{1,0:T(8,128)S(1)}, f32[512,256]{1,0:T(8,128)S(1)}, f32[1,256]{1,0:T(1,128)S(1)}) custom-call(bf16[512,256]{1,0:T(8,128)(2,1)S(1)} %collective-permute-done.refs_0_, bf16[512,256]{1,0:T(8,128)(2,1)S(1)} %collective-permute-done.1.refs_1_, ...), custom_call_target="tpu_custom_call", output_to_operand_aliasing={{0}: (4, {})} | custom-call | tf_op jit(solution)/shard_map/conv/pallas_call | solution.py:419
  22.1 0.0 copy-start.5
  22.1 0.1 collective-permute-start.9
  22.2 0.0 collective-permute-done.4.refs_4_
  22.2 0.0 collective-permute-done.5.refs_5_
  22.3 1.4 %taps.1 = (bf16[128,256]{1,0:T(8,128)(2,1)S(1)}, bf16[128,256]{1,0:T(8,128)(2,1)S(1)}, bf16[128,256]{1,0:T(8,128)(2,1)S(1)}, bf16[128,256]{1,0:T(8,128)(2,1)S(1)}, f32[1,256]{1,0:T(1,128)S(1)}) custom-call(bf16[4,128,256]{2,1,0:T(8,128)(2,1)S(1)} %bitcast.14, bf16[4,128,256]{2,1,0:T(8,128)(2,1)S(1)} %bitcast.18, s32[4,1,128]{2,1,0:T(1,128)S(1)} %bitcast.26, ...), custom_call_target="tpu_custom_call" | custom-call | tf_op jit(solution)/shard_map/taps/pallas_call | solution.py:428
  23.7 0.0 collective-permute-done.9
  23.7 1.6 %collective-permute-start.10 = (f32[1,256]{1,0:T(1,128)S(1)}, f32[1,256]{1,0:T(1,128)S(1)}, u32[]{:S(2)}, u32[]{:S(2)}) collective-permute-start(f32[1,256]{1,0:T(1,128)S(1)} %max.6), channel_id=1, source_target_pairs={{0,2},{1,3},{2,0},{3,1},{4,6},{5,7},{6,4},{7,5},{8,10},{9,11},{10,... | collective-permute-start | bytes 3080 | tf_op jit(solution)/shard_map/ppermute | solution.py:374
  25.3 0.3 collective-permute-start.6
  25.6 1.8 %collective-permute-start.7 = (bf16[128,256]{1,0:T(8,128)(2,1)S(1)}, bf16[128,256]{1,0:T(8,128)(2,1)S(1)}, u32[]{:S(2)}, u32[]{:S(2)}) collective-permute-start(bf16[128,256]{1,0:T(8,128)(2,1)S(1)} %get-tuple-element.39), channel_id=1, source_target_pairs={{0,16},{8,24},{16,0},{24,8},{1,17},{9,25},{17,1},{25,9},{2,18},{10... | collective-permute-start | bytes 196616 | tf_op jit(solution)/shard_map/ppermute | solution.py:374
  27.4 1.4 %collective-permute-start.8 = (bf16[128,256]{1,0:T(8,128)(2,1)S(1)}, bf16[128,256]{1,0:T(8,128)(2,1)S(1)}, u32[]{:S(2)}, u32[]{:S(2)}) collective-permute-start(bf16[128,256]{1,0:T(8,128)(2,1)S(1)} %get-tuple-element.40), channel_id=1, source_target_pairs={{0,24},{8,16},{16,8},{24,0},{1,25},{9,17},{17,9},{25,1},{2,26},{10... | collective-permute-start | bytes 196616 | tf_op jit(solution)/shard_map/ppermute | solution.py:374
  28.8 2.6 %collective-permute-start.11 = (f32[1,256]{1,0:T(1,128)S(1)}, f32[1,256]{1,0:T(1,128)S(1)}, u32[]{:S(2)}, u32[]{:S(2)}) collective-permute-start(f32[1,256]{1,0:T(1,128)S(1)} %max.7.refs_4_), channel_id=1, source_target_pairs={{0,4},{1,5},{2,6},{3,7},{4,0},{5,1},{6,2},{7,3},{8,12},{9,13},{10,... | collective-permute-start | bytes 3080 | tf_op jit(solution)/shard_map/ppermute | solution.py:374
  31.4 1.3 %grads.1 = bf16[3,512,256]{2,1,0:T(8,128)(2,1)} custom-call(bf16[3,512,256]{2,1,0:T(8,128)(2,1)S(1)} %copy-done.2, s32[3,2,512]{2,1,0:T(2,128)S(1)} %bitcast.24, bf16[512,256]{1,0:T(8,128)(2,1)S(1)} %copy-done.5, f32[512,256]{1,0:T(8,128)S(1)} %get-tuple-element.45.conv_ref, f32[2,512,512]{2,1,0:T(8,128)S(1)} %get-tuple-element.46.acc_ref, ...), custom_call_target="tpu_custom_call" | custom-call | flops 1000000000 | bytes 1000000 | tf_op jit(solution)/shard_map/grads/pallas_call | solution.py:451
  32.8 0.8 %spread.1 = (f32[4,128,256]{2,1,0:T(8,128)}, f32[1,256]{1,0:T(1,128)S(1)}) custom-call(bf16[128,256]{1,0:T(8,128)(2,1)S(1)} %get-tuple-element.37.refs_0_, bf16[128,256]{1,0:T(8,128)(2,1)S(1)} %collective-permute-done.6.refs_1_, bf16[128,256]{1,0:T(8,128)(2,1)S(1)} %collective-permute-done.7.refs_2_, bf16[128,256]{1,0:T(8,128)(2,1)S(1)} %collective-permute-done.8.refs_3_, ...), custom_call_target="tpu_custom_call" | custom-call | tf_op jit(solution)/shard_map/spread/pallas_call | solution.py:459
  33.6 0.7 %scale.1 = (bf16[512,256]{1,0:T(8,128)(2,1)}, f32[1,256]{1,0:T(1,128)}) custom-call(f32[512,256]{1,0:T(8,128)S(1)} %get-tuple-element.35.resp_ref, f32[1,256]{1,0:T(1,128)S(1)} %get-tuple-element.42.near_ref, f32[1,256]{1,0:T(1,128)S(1)} %collective-permute-done.11.far_ref), custom_call_target="tpu_custom_call" | custom-call | flops 1000000000 | bytes 1000000 | tf_op jit(solution)/shard_map/scale/pallas_call | solution.py:467
  (23 shorter events, 0.1 us)
Async XLA Ops:
  0.6 1.5 %copy-start.6 = (s32[3,512,2]{1,2,0:T(2,128)S(1)}, s32[3,512,2]{1,2,0:T(2,128)}, u32[]{:S(2)}) copy-start(s32[3,512,2]{1,2,0:T(2,128)} %param.10) | copy-start | bytes 36868
  0.6 14.0 %copy-start.4 = (bf16[512,512]{1,0:T(8,128)(2,1)S(1)}, bf16[512,512]{1,0:T(8,128)(2,1)}, u32[]{:S(2)}) copy-start(bf16[512,512]{1,0:T(8,128)(2,1)} %constant.7.clone.low_ref) | copy-start | bytes 1572868
  2.0 12.6 %copy-start = (bf16[512,512]{1,0:T(8,128)(2,1)S(1)}, bf16[512,512]{1,0:T(8,128)(2,1)}, u32[]{:S(2)}) copy-start(bf16[512,512]{1,0:T(8,128)(2,1)} %constant.6.clone.high_ref.refs_6_) | copy-start | bytes 1572868
  2.0 12.6 %copy-start.2 = (bf16[3,512,256]{2,1,0:T(8,128)(2,1)S(1)}, bf16[3,512,256]{2,1,0:T(8,128)(2,1)}, u32[]{:S(2)}) copy-start(bf16[3,512,256]{2,1,0:T(8,128)(2,1)} %proj_ref.3) | copy-start | bytes 2359300
  2.1 12.6 %copy-start.3 = (bf16[512,1024]{1,0:T(8,128)(2,1)S(1)}, bf16[512,1024]{1,0:T(8,128)(2,1)}, u32[]{:S(2)}) copy-start(bf16[512,1024]{1,0:T(8,128)(2,1)} %filt_ref.1) | copy-start | bytes 3145732
  2.1 12.6 %copy-start.7 = (s32[512]{0:T(512)S(1)}, s32[512]{0:T(512)}, u32[]{:S(2)}) copy-start(s32[512]{0:T(512)} %param.12) | copy-start | bytes 6148
  2.1 12.6 %copy-start.8 = (f32[512]{0:T(512)S(1)}, f32[512]{0:T(512)}, u32[]{:S(2)}) copy-start(f32[512]{0:T(512)} %param.13) | copy-start | bytes 6148
  2.5 10.1 %collective-permute-start.2 = (bf16[512,256]{1,0:T(8,128)(2,1)S(1)}, bf16[512,256]{1,0:T(8,128)(2,1)S(1)}, u32[]{:S(2)}, u32[]{:S(2)}) collective-permute-start(bf16[512,256]{1,0:T(8,128)(2,1)S(1)} %get-tuple-element.30), channel_id=1, source_target_pairs={{0,8},{8,0},{16,24},{24,16},{1,9},{9,1},{17,25},{25,17},{2,10},{10... | collective-permute-start | bytes 786440 | tf_op jit(solution)/shard_map/ppermute | solution.py:374
  5.5 15.5 %collective-permute-start = (bf16[512,256]{1,0:T(8,128)(2,1)S(1)}, bf16[512,256]{1,0:T(8,128)(2,1)S(1)}, u32[]{:S(2)}, u32[]{:S(2)}) collective-permute-start(bf16[512,256]{1,0:T(8,128)(2,1)S(1)} %get-tuple-element.28.main_ref), channel_id=1, source_target_pairs={{0,16},{8,24},{16,0},{24,8},{1,17},{9,25},{17,1},{25,9},{2,18},{10... | collective-permute-start | bytes 786440 | tf_op jit(solution)/shard_map/ppermute | solution.py:374
  7.0 14.0 %collective-permute-start.1 = (bf16[512,256]{1,0:T(8,128)(2,1)S(1)}, bf16[512,256]{1,0:T(8,128)(2,1)S(1)}, u32[]{:S(2)}, u32[]{:S(2)}) collective-permute-start(bf16[512,256]{1,0:T(8,128)(2,1)S(1)} %get-tuple-element.28.main_ref), channel_id=1, source_target_pairs={{0,24},{8,16},{16,8},{24,0},{1,25},{9,17},{17,9},{25,1},{2,26},{10... | collective-permute-start | bytes 786440 | tf_op jit(solution)/shard_map/ppermute | solution.py:374
  7.0 15.2 %collective-permute-start.4 = (bf16[128,256]{1,0:T(8,128)(2,1)S(1)}, bf16[128,256]{1,0:T(8,128)(2,1)S(1)}, u32[]{:S(2)}, u32[]{:S(2)}) collective-permute-start(bf16[128,256]{1,0:T(8,128)(2,1)S(1)} %pick.4), channel_id=1, source_target_pairs={{0,16},{8,24},{16,0},{24,8},{1,17},{9,25},{17,1},{25,9},{2,18},{10... | collective-permute-start | bytes 196616 | tf_op jit(solution)/shard_map/ppermute | solution.py:374
  9.0 12.0 %copy-start.1 = (bf16[512,512]{1,0:T(8,128)(2,1)S(1)}, bf16[512,512]{1,0:T(8,128)(2,1)}, u32[]{:S(2)}) copy-start(bf16[512,512]{1,0:T(8,128)(2,1)} %constant.8.clone.refs_7_.inv_ref) | copy-start | bytes 1572868
  9.0 13.2 %collective-permute-start.5 = (bf16[128,256]{1,0:T(8,128)(2,1)S(1)}, bf16[128,256]{1,0:T(8,128)(2,1)S(1)}, u32[]{:S(2)}, u32[]{:S(2)}) collective-permute-start(bf16[128,256]{1,0:T(8,128)(2,1)S(1)} %pick.5), channel_id=1, source_target_pairs={{0,24},{8,16},{16,8},{24,0},{1,25},{9,17},{17,9},{25,1},{2,26},{10... | collective-permute-start | bytes 196616 | tf_op jit(solution)/shard_map/ppermute | solution.py:374
  12.6 9.6 %collective-permute-start.3 = (bf16[128,256]{1,0:T(8,128)(2,1)S(1)}, bf16[128,256]{1,0:T(8,128)(2,1)S(1)}, u32[]{:S(2)}, u32[]{:S(2)}) collective-permute-start(bf16[128,256]{1,0:T(8,128)(2,1)S(1)} %pick.3), channel_id=1, source_target_pairs={{0,8},{8,0},{16,24},{24,16},{1,9},{9,1},{17,25},{25,17},{2,10},{10... | collective-permute-start | bytes 196616 | tf_op jit(solution)/shard_map/ppermute | solution.py:374
  22.1 9.3 %copy-start.5 = (bf16[512,256]{1,0:T(8,128)(2,1)S(1)}, bf16[512,256]{1,0:T(8,128)(2,1)}, u32[]{:S(2)}) copy-start(bf16[512,256]{1,0:T(8,128)(2,1)} %cot_ref.1) | copy-start | bytes 786436
  22.1 1.5 %collective-permute-start.9 = (f32[1,256]{1,0:T(1,128)S(1)}, f32[1,256]{1,0:T(1,128)S(1)}, u32[]{:S(2)}, u32[]{:S(2)}) collective-permute-start(f32[1,256]{1,0:T(1,128)S(1)} %get-tuple-element.36.refs_6_), channel_id=1, source_target_pairs={{0,1},{1,0},{2,3},{3,2},{4,5},{5,4},{6,7},{7,6},{8,9},{9,8},{10,11... | collective-permute-start | bytes 3080 | tf_op jit(solution)/shard_map/ppermute | solution.py:374
  23.7 5.1 %collective-permute-start.10 = (f32[1,256]{1,0:T(1,128)S(1)}, f32[1,256]{1,0:T(1,128)S(1)}, u32[]{:S(2)}, u32[]{:S(2)}) collective-permute-start(f32[1,256]{1,0:T(1,128)S(1)} %max.6), channel_id=1, source_target_pairs={{0,2},{1,3},{2,0},{3,1},{4,6},{5,7},{6,4},{7,5},{8,10},{9,11},{10,... | collective-permute-start | bytes 3080 | tf_op jit(solution)/shard_map/ppermute | solution.py:374
  25.3 7.4 %collective-permute-start.6 = (bf16[128,256]{1,0:T(8,128)(2,1)S(1)}, bf16[128,256]{1,0:T(8,128)(2,1)S(1)}, u32[]{:S(2)}, u32[]{:S(2)}) collective-permute-start(bf16[128,256]{1,0:T(8,128)(2,1)S(1)} %get-tuple-element.38), channel_id=1, source_target_pairs={{0,8},{8,0},{16,24},{24,16},{1,9},{9,1},{17,25},{25,17},{2,10},{10... | collective-permute-start | bytes 196616 | tf_op jit(solution)/shard_map/ppermute | solution.py:374
  25.6 7.1 %collective-permute-start.7 = (bf16[128,256]{1,0:T(8,128)(2,1)S(1)}, bf16[128,256]{1,0:T(8,128)(2,1)S(1)}, u32[]{:S(2)}, u32[]{:S(2)}) collective-permute-start(bf16[128,256]{1,0:T(8,128)(2,1)S(1)} %get-tuple-element.39), channel_id=1, source_target_pairs={{0,16},{8,24},{16,0},{24,8},{1,17},{9,25},{17,1},{25,9},{2,18},{10... | collective-permute-start | bytes 196616 | tf_op jit(solution)/shard_map/ppermute | solution.py:374
  27.4 5.4 %collective-permute-start.8 = (bf16[128,256]{1,0:T(8,128)(2,1)S(1)}, bf16[128,256]{1,0:T(8,128)(2,1)S(1)}, u32[]{:S(2)}, u32[]{:S(2)}) collective-permute-start(bf16[128,256]{1,0:T(8,128)(2,1)S(1)} %get-tuple-element.40), channel_id=1, source_target_pairs={{0,24},{8,16},{16,8},{24,0},{1,25},{9,17},{17,9},{25,1},{2,26},{10... | collective-permute-start | bytes 196616 | tf_op jit(solution)/shard_map/ppermute | solution.py:374
  28.8 4.8 %collective-permute-start.11 = (f32[1,256]{1,0:T(1,128)S(1)}, f32[1,256]{1,0:T(1,128)S(1)}, u32[]{:S(2)}, u32[]{:S(2)}) collective-permute-start(f32[1,256]{1,0:T(1,128)S(1)} %max.7.refs_4_), channel_id=1, source_target_pairs={{0,4},{1,5},{2,6},{3,7},{4,0},{5,1},{6,2},{7,3},{8,12},{9,13},{10,... | collective-permute-start | bytes 3080 | tf_op jit(solution)/shard_map/ppermute | solution.py:374

commit v4 on v3

--- a/solution.py
+++ b/solution.py
@@ -132,14 +132,15 @@
 
 def windows_kernel(
     n, rows, proj_ref, exp_ref, filt_ref, reach_ref, skip_ref, main_ref, rest_ref, high_ref, low_ref,
-    recv_ref, query_ref, base_ref, *rest
+    recv_ref, deq_ref, base_ref, *rest
 ):
     win_refs, (taps, lens, gain) = rest[: n - 2], rest[n - 2 :]
     me = lax.axis_index("ctx")
     channels, seq_len = filt_ref.shape
     span = seq_len // n
     fscale = 1.0 / math.sqrt(seq_len)
-    query_ref[...] = (proj_ref[0].astype(F32) * block_scale(exp_ref[0], span)).astype(BF16)
+    for group in range(3):
+        deq_ref[group] = (proj_ref[group].astype(F32) * block_scale(exp_ref[group], span)).astype(BF16)
     upper = top_bit(n)
     lens[...] = reach_lens(reach_ref, seq_len)
     gain[...] = column(skip_ref) * (1.0 / fscale)
@@ -184,30 +185,38 @@
 
 
 def conv_kernel(n, seq_len, rows, *refs):
-    recv_refs, win_refs = refs[: n - 2], refs[n - 2 : 2 * n - 4]
-    _, query_ref, high_ref, inv_ref = refs[2 * n - 4 : 2 * n]
-    acc, resp_ref, conv_ref, peak_ref = refs[2 * n :]
-    me = lax.axis_index("ctx")
-    channels, span = query_ref.shape
+    recv_refs, win_refs, refs = refs[: n - 2], refs[n - 2 : 2 * n - 4], refs[2 * n - 4 :]
+    base_ref, deq_ref, high_ref, inv_ref, back_ref, resp_ref, conv_ref, peak_ref = refs
+    me = lax.axis_index("ctx")
+    channels, span = resp_ref.shape
     fscale = 1.0 / math.sqrt(seq_len)
-    peak_ref[...] = jnp.zeros_like(peak_ref)
-
-    @row_loop(channels, rows)
-    def _(block):
-        for k in range(2, n):
-            later = jnp.where(jnp.bitwise_xor(me, k) > me, 1, 0)
-            start = pl.multiple_of(later * span, span)
-            spec = mm(recv_refs[k - 2][block], high_ref[pl.ds(start, span), :])
-            xr, xi = spec[:, :span], spec[:, span:]
-            wr = win_refs[k - 2][block, :span].astype(F32)
-            wi = win_refs[k - 2][block, span:].astype(F32)
-            acc[later, block, :span] += xr * wr - xi * wi
-            acc[later, block, span:] += xr * wi + xi * wr
-        conv = mm(acc[0, block].astype(BF16), inv_ref[:, span:]) * fscale
-        response = query_ref[block].astype(F32) * conv
-        resp_ref[block] = response
-        conv_ref[block] = conv
-        peak_ref[...] = jnp.maximum(peak_ref[...], jnp.max(jnp.abs(response), axis=0, keepdims=True))
+    uppers = [lax.rem(lax.div(me, 2**bit), 2) for bit in range((n - 1).bit_length())]
+    starts = [pl.multiple_of((1 - upper) * span, span) for upper in uppers]
+    peaks = []
+    for first in range(0, channels, rows):
+        tile = slice(first, first + rows)
+        fr, fi = base_ref[0, tile, :span], base_ref[0, tile, span:]
+        br, bi = base_ref[1, tile, :span], base_ref[1, tile, span:]
+        for bit in range(1, len(uppers)):
+            real = imag = 0.0
+            for k in range(2**bit, min(2 ** (bit + 1), n)):
+                spec = mm(recv_refs[k - 2][tile], high_ref[pl.ds(starts[bit], span), :])
+                xr, xi = spec[:, :span], spec[:, span:]
+                wr = win_refs[k - 2][tile, :span].astype(F32)
+                wi = win_refs[k - 2][tile, span:].astype(F32)
+                real += xr * wr - xi * wi
+                imag += xr * wi + xi * wr
+            here = uppers[bit] == 1
+            fr, br = jnp.where(here, fr + real, fr), jnp.where(here, br, br + real)
+            fi, bi = jnp.where(here, fi + imag, fi), jnp.where(here, bi, bi + imag)
+        back_ref[tile, :span], back_ref[tile, span:] = br.astype(BF16), bi.astype(BF16)
+        front = jnp.concatenate([fr.astype(BF16), fi.astype(BF16)], axis=1)
+        conv = mm(front, inv_ref[:, span:]) * fscale
+        response = deq_ref[0, tile].astype(F32) * conv
+        resp_ref[tile] = response
+        conv_ref[tile] = conv
+        peaks.append(jnp.max(jnp.abs(response), axis=0, keepdims=True))
+    peak_ref[...] = functools.reduce(jnp.maximum, peaks)
 
 
 def taps_kernel(n, seq_len, main_ref, rest_ref, reach_ref, high_ref, inv_ref, *refs):
@@ -254,7 +263,7 @@
             mspec[b] = mm(mbuf[b], high_ref[:span])
             pspec[b] = mm(pbuf[b], high_ref[:span]) + mm(pbuf[b + 1], high_ref[span:])
 
-    @row_loop(rows, 16)
+    @row_loop(rows, rows)
     def _(tile):
         for lag_block in range(n):
             real = imag = 0.0
@@ -291,23 +300,20 @@
         out_ref[...] = rest_ref[other]
 
 
-def grads_kernel(seq_len, proj_ref, exp_ref, cot_ref, conv_ref, acc_ref, inv_ref, *refs):
-    grad_hbm, grad, grad_sem = refs
+def grads_kernel(seq_len, deq_ref, cot_ref, conv_ref, back_ref, inv_ref, grad_hbm, grad, grad_sem):
     span = cot_ref.shape[1]
     fscale = 1.0 / math.sqrt(seq_len)
     copies = []
 
-    def send(source, target, sem):
-        copies.append(pltpu.make_async_copy(source, target, sem))
+    def send(slot, value):
+        grad[slot] = value.astype(BF16)
+        copies.append(pltpu.make_async_copy(grad.at[slot], grad_hbm.at[slot], grad_sem.at[slot]))
         copies[-1].start()
 
-    grad[0] = (cot_ref[...].astype(F32) * conv_ref[...]).astype(BF16)
-    send(grad.at[0], grad_hbm.at[0], grad_sem.at[0])
-    grad_mixed = mm(acc_ref[1].astype(BF16), inv_ref[:, :span]) * fscale
-    for slot, source in ((1, 2), (2, 1)):
-        scaled = proj_ref[source].astype(F32) * block_scale(exp_ref[source], span)
-        grad[slot] = (grad_mixed * scaled).astype(BF16)
-        send(grad.at[slot], grad_hbm.at[slot], grad_sem.at[slot])
+    send(0, cot_ref[...].astype(F32) * conv_ref[...])
+    grad_mixed = mm(back_ref[...], inv_ref[:, :span]) * fscale
+    send(1, grad_mixed * deq_ref[2].astype(F32))
+    send(2, grad_mixed * deq_ref[1].astype(F32))
     for copy in copies:
         copy.wait()
 
@@ -403,11 +409,11 @@
     second = {k: swap(pick(k), "ctx", k) for k in range(2, n)}
 
     wide = shape((channels, 2 * span), BF16)
-    query, base, *wins = call(
+    deq, base, *wins = call(
         functools.partial(windows_kernel, n, rows),
         "windows",
         [vmem] * 10,
-        [flat, shape((2, channels, 2 * span), F32)] + [wide] * (n - 2),
+        [shape((3, channels, span), BF16), shape((2, channels, 2 * span), F32)] + [wide] * (n - 2),
         scratch_shapes=[
             pltpu.VMEM((n + 1, rows, span), BF16),
             pltpu.VMEM((channels, 1), jnp.int32),
@@ -416,13 +422,12 @@
     )(proj, exps, filt, reach_row, skip_row, main, rest, high, low, first[0])
     second[1] = swap(pick(1, first[0]), "ctx", 1)
 
-    acc, response, conv, peak = call(
-        functools.partial(conv_kernel, n, seq_len, rows),
+    back, response, conv, peak = call(
+        functools.partial(conv_kernel, n, seq_len, channels),
         "conv",
         [vmem] * (2 * n),
-        [shape((2, channels, 2 * span), F32)] + [shape((channels, span), F32)] * 2 + [line],
-        input_output_aliases={2 * n - 4: 0},
-    )(*first[1:], *wins, base, query, high, inverse)
+        [wide] + [shape((channels, span), F32)] * 2 + [line],
+    )(*first[1:], *wins, base, deq, high, inverse)
 
     far = swap(peak, "ch", 1)
     own_part, *parts_out, peak = call(
@@ -451,11 +456,11 @@
     (gradients,) = call(
         functools.partial(grads_kernel, seq_len),
         "grads",
-        [vmem] * 6,
+        [vmem] * 5,
         [shape((3, channels, span), BF16)],
         out_specs=[hbm],
         scratch_shapes=[pltpu.VMEM((3, channels, span), BF16), pltpu.SemaphoreType.DMA((3,))],
-    )(proj, exps, cotangent, conv, acc, inverse)
+    )(deq, cotangent, conv, back, inverse)
     filter_grad, peak = call(
         functools.partial(spread_kernel, n),
         "spread",

time: 34.5 us -> 34.2 us (level)
  transfers between devices with their start and end apart: 12 -> 12, of which waited for: 2 -> 2; matrix products, arithmetic and copies ran while one was open for 0% -> 0% of each run, Pallas kernels for 24% -> 23%
where the time goes in v4:
time: 34.2 us; the launch traced here: 34 us
  starting transfers between devices  17.9 us (52%)
  Pallas kernels  10.4 us (30%)
  waiting for transfers between devices  4.78 us (14%)
  between operations  0.86 us (3%)
    ppermute x12, starting transfers between devices, swap(): lax.ppermute(value, axis, [(j, j ^ k) for j in range(lax.axis_size(axis))])  17.9 us
    ppermute x12, waiting for transfers between devices, swap(): lax.ppermute(value, axis, [(j, j ^ k) for j in range(lax.axis_size(axis))])  4.78 us
    pallas_call x1, Pallas kernels, body(): call(functools.partial(windows_kernel, n, rows), 'windows', [vmem] * 10,...  3.6 us
    pallas_call x1, Pallas kernels, body(): call(functools.partial(load_kernel, parts), 'load', [hbm] * 2, [flat] * 2...  1.37 us
    pallas_call x1, Pallas kernels, body(): call(functools.partial(conv_kernel, n, seq_len, channels), 'conv', [vmem]...  1.26 us
    pallas_call x1, Pallas kernels, body(): call(functools.partial(grads_kernel, seq_len), 'grads', [vmem] * 5, [shap...  1.15 us
    pallas_call x1, Pallas kernels, body(): call(functools.partial(taps_kernel, n, seq_len), 'taps', [vmem] * (2 * n...  1.12 us
    pallas_call x1, Pallas kernels, body(): call(functools.partial(spread_kernel, n), 'spread', [vmem] * (n + 1), [sh...  0.84 us
  transfers between devices with their start and end apart: 12, of which 2 were waited for; matrix products, arithmetic and copies ran while one was open for 0% of the time, Pallas kernels for 23%

profile of v4, /device:TPU:0, one launch (start us, length us, event | category | flops | bytes accessed | tf_op | source)
XLA Modules:
  0.0 34.0 jit_solution(522261982991176612)
XLA Ops:
  0.6 0.0 copy-start.4
  0.7 1.4 %load.1 = (bf16[512,256]{1,0:T(8,128)(2,1)S(1)}, bf16[512,256]{1,0:T(8,128)(2,1)S(1)}) custom-call(bf16[3,512,256]{2,1,0:T(8,128)(2,1)} %proj_ref.1, bf16[512,256]{1,0:T(8,128)(2,1)} %cot_ref.1), custom_call_target="tpu_custom_call" | custom-call | flops 1000000000 | bytes 1000000 | tf_op jit(solution)/shard_map/load/pallas_call | solution.py:385
  2.0 0.0 copy-start
  2.0 0.0 copy-start.2
  2.1 0.0 copy-start.3
  2.1 0.0 copy-start.6
  2.1 0.0 copy-start.7
  2.1 0.3 %prep.1 = (bf16[512,256]{1,0:T(8,128)(2,1)S(1)}, bf16[512,256]{1,0:T(8,128)(2,1)S(1)}, bf16[512,256]{1,0:T(8,128)(2,1)S(1)}) custom-call(bf16[512,256]{1,0:T(8,128)(2,1)S(1)} %get-tuple-element.26.key_value_ref, bf16[512,256]{1,0:T(8,128)(2,1)S(1)} %get-tuple-element.27.query_cot_ref, s32[3,2,512]{2,1,0:T(2,128)S(1)} %bitcast.22), custom_call_target="tpu_custom_call" | custom-call | tf_op jit(solution)/shard_map/prep/pallas_call | solution.py:398
  2.5 3.0 %collective-permute-start.2 = (bf16[512,256]{1,0:T(8,128)(2,1)S(1)}, bf16[512,256]{1,0:T(8,128)(2,1)S(1)}, u32[]{:S(2)}, u32[]{:S(2)}) collective-permute-start(bf16[512,256]{1,0:T(8,128)(2,1)S(1)} %get-tuple-element.30), channel_id=1, source_target_pairs={{0,8},{8,0},{16,24},{24,16},{1,9},{9,1},{17,25},{25,17},{2,10},{10... | collective-permute-start | bytes 786440 | tf_op jit(solution)/shard_map/ppermute | solution.py:380
  5.5 1.5 %collective-permute-start = (bf16[512,256]{1,0:T(8,128)(2,1)S(1)}, bf16[512,256]{1,0:T(8,128)(2,1)S(1)}, u32[]{:S(2)}, u32[]{:S(2)}) collective-permute-start(bf16[512,256]{1,0:T(8,128)(2,1)S(1)} %get-tuple-element.28.main_ref), channel_id=1, source_target_pairs={{0,16},{8,24},{16,0},{24,8},{1,17},{9,25},{17,1},{25,9},{2,18},{10... | collective-permute-start | bytes 786440 | tf_op jit(solution)/shard_map/ppermute | solution.py:380
  7.0 0.0 collective-permute-start.1
  7.0 2.0 %collective-permute-start.4 = (bf16[128,256]{1,0:T(8,128)(2,1)S(1)}, bf16[128,256]{1,0:T(8,128)(2,1)S(1)}, u32[]{:S(2)}, u32[]{:S(2)}) collective-permute-start(bf16[128,256]{1,0:T(8,128)(2,1)S(1)} %pick.4), channel_id=1, source_target_pairs={{0,16},{8,24},{16,0},{24,8},{1,17},{9,25},{17,1},{25,9},{2,18},{10... | collective-permute-start | bytes 196616 | tf_op jit(solution)/shard_map/ppermute | solution.py:380
  9.0 1.5 %collective-permute-start.5 = (bf16[128,256]{1,0:T(8,128)(2,1)S(1)}, bf16[128,256]{1,0:T(8,128)(2,1)S(1)}, u32[]{:S(2)}, u32[]{:S(2)}) collective-permute-start(bf16[128,256]{1,0:T(8,128)(2,1)S(1)} %pick.5), channel_id=1, source_target_pairs={{0,24},{8,16},{16,8},{24,0},{1,25},{9,17},{17,9},{25,1},{2,26},{10... | collective-permute-start | bytes 196616 | tf_op jit(solution)/shard_map/ppermute | solution.py:380
  10.5 2.1 %collective-permute-done.2.recv_ref.refs_0_ = bf16[512,256]{1,0:T(8,128)(2,1)S(1)} collective-permute-done((bf16[512,256]{1,0:T(8,128)(2,1)S(1)}, bf16[512,256]{1,0:T(8,128)(2,1)S(1)}, u32[]{:S(2)}, u32[]{:S(2)}) %collective-permute-start.2) | collective-permute-done | bytes 262176 | tf_op jit(solution)/shard_map/ppermute | solution.py:380
  12.6 2.1 %collective-permute-start.3 = (bf16[128,256]{1,0:T(8,128)(2,1)S(1)}, bf16[128,256]{1,0:T(8,128)(2,1)S(1)}, u32[]{:S(2)}, u32[]{:S(2)}) collective-permute-start(bf16[128,256]{1,0:T(8,128)(2,1)S(1)} %pick.3), channel_id=1, source_target_pairs={{0,8},{8,0},{16,24},{24,16},{1,9},{9,1},{17,25},{25,17},{2,10},{10... | collective-permute-start | bytes 196616 | tf_op jit(solution)/shard_map/ppermute | solution.py:380
  14.7 3.6 %windows.1 = (bf16[3,512,256]{2,1,0:T(8,128)(2,1)S(1)}, f32[2,512,512]{2,1,0:T(8,128)S(1)}, bf16[512,512]{1,0:T(8,128)(2,1)S(1)}, bf16[512,512]{1,0:T(8,128)(2,1)S(1)}) custom-call(bf16[3,512,256]{2,1,0:T(8,128)(2,1)S(1)} %copy-done.3, s32[3,2,512]{2,1,0:T(2,128)S(1)} %bitcast.23, bf16[512,1024]{1,0:T(8,128)(2,1)S(1)} %copy-done.2, s32[1,512]{1,0:T(1,128)S(1)} %bitcast.24, ...), custom_call_target="tpu_custom_call" | custom-call | tf_op jit(solution)/shard_map/windows/pallas_call | solution.py:412
  18.3 2.6 %collective-permute-done.refs_0_ = bf16[512,256]{1,0:T(8,128)(2,1)S(1)} collective-permute-done((bf16[512,256]{1,0:T(8,128)(2,1)S(1)}, bf16[512,256]{1,0:T(8,128)(2,1)S(1)}, u32[]{:S(2)}, u32[]{:S(2)}) %collective-permute-start) | collective-permute-done | bytes 262176 | tf_op jit(solution)/shard_map/ppermute | solution.py:380
  21.0 1.3 %conv.1 = (bf16[512,512]{1,0:T(8,128)(2,1)S(1)}, f32[512,256]{1,0:T(8,128)S(1)}, f32[512,256]{1,0:T(8,128)S(1)}, f32[1,256]{1,0:T(1,128)S(1)}) custom-call(bf16[512,256]{1,0:T(8,128)(2,1)S(1)} %collective-permute-done.refs_0_, bf16[512,256]{1,0:T(8,128)(2,1)S(1)} %collective-permute-done.1.refs_1_, bf16[512,512]{1,0:T(8,128)(2,1)S(1)} %get-tuple-element.31.refs_2_, ...), custom_call_target="tpu_custom_call" | custom-call | tf_op jit(solution)/shard_map/conv/pallas_call | solution.py:425
  22.2 0.0 copy-start.8
  22.2 0.1 collective-permute-start.9
  22.3 0.0 collective-permute-done.4.refs_4_
  22.3 0.0 collective-permute-done.5.refs_5_
  22.3 1.1 %taps.1 = (bf16[128,256]{1,0:T(8,128)(2,1)S(1)}, bf16[128,256]{1,0:T(8,128)(2,1)S(1)}, bf16[128,256]{1,0:T(8,128)(2,1)S(1)}, bf16[128,256]{1,0:T(8,128)(2,1)S(1)}, f32[1,256]{1,0:T(1,128)S(1)}) custom-call(bf16[4,128,256]{2,1,0:T(8,128)(2,1)S(1)} %bitcast.14, bf16[4,128,256]{2,1,0:T(8,128)(2,1)S(1)} %bitcast.18, s32[4,1,128]{2,1,0:T(1,128)S(1)} %bitcast.25, ...), custom_call_target="tpu_custom_call" | custom-call | tf_op jit(solution)/shard_map/taps/pallas_call | solution.py:433
  23.5 0.0 collective-permute-done.9
  23.5 1.6 %collective-permute-start.10 = (f32[1,256]{1,0:T(1,128)S(1)}, f32[1,256]{1,0:T(1,128)S(1)}, u32[]{:S(2)}, u32[]{:S(2)}) collective-permute-start(f32[1,256]{1,0:T(1,128)S(1)} %max.6), channel_id=1, source_target_pairs={{0,2},{1,3},{2,0},{3,1},{4,6},{5,7},{6,4},{7,5},{8,10},{9,11},{10,... | collective-permute-start | bytes 3080 | tf_op jit(solution)/shard_map/ppermute | solution.py:380
  25.1 0.3 collective-permute-start.6
  25.4 1.8 %collective-permute-start.7 = (bf16[128,256]{1,0:T(8,128)(2,1)S(1)}, bf16[128,256]{1,0:T(8,128)(2,1)S(1)}, u32[]{:S(2)}, u32[]{:S(2)}) collective-permute-start(bf16[128,256]{1,0:T(8,128)(2,1)S(1)} %get-tuple-element.39), channel_id=1, source_target_pairs={{0,16},{8,24},{16,0},{24,8},{1,17},{9,25},{17,1},{25,9},{2,18},{10... | collective-permute-start | bytes 196616 | tf_op jit(solution)/shard_map/ppermute | solution.py:380
  27.2 1.4 %collective-permute-start.8 = (bf16[128,256]{1,0:T(8,128)(2,1)S(1)}, bf16[128,256]{1,0:T(8,128)(2,1)S(1)}, u32[]{:S(2)}, u32[]{:S(2)}) collective-permute-start(bf16[128,256]{1,0:T(8,128)(2,1)S(1)} %get-tuple-element.40), channel_id=1, source_target_pairs={{0,24},{8,16},{16,8},{24,0},{1,25},{9,17},{17,9},{25,1},{2,26},{10... | collective-permute-start | bytes 196616 | tf_op jit(solution)/shard_map/ppermute | solution.py:380
  28.6 2.6 %collective-permute-start.11 = (f32[1,256]{1,0:T(1,128)S(1)}, f32[1,256]{1,0:T(1,128)S(1)}, u32[]{:S(2)}, u32[]{:S(2)}) collective-permute-start(f32[1,256]{1,0:T(1,128)S(1)} %max.7.refs_4_), channel_id=1, source_target_pairs={{0,4},{1,5},{2,6},{3,7},{4,0},{5,1},{6,2},{7,3},{8,12},{9,13},{10,... | collective-permute-start | bytes 3080 | tf_op jit(solution)/shard_map/ppermute | solution.py:380
  31.2 1.1 %grads.1 = bf16[3,512,256]{2,1,0:T(8,128)(2,1)} custom-call(bf16[3,512,256]{2,1,0:T(8,128)(2,1)S(1)} %get-tuple-element.34.refs_5_.deq_ref, bf16[512,256]{1,0:T(8,128)(2,1)S(1)} %copy-done.8, f32[512,256]{1,0:T(8,128)S(1)} %get-tuple-element.45.conv_ref, bf16[512,512]{1,0:T(8,128)(2,1)S(1)} %get-tuple-element.46.back_ref, bf16[512,512]{1,0:T(8,128)(2,1)S(1)} %copy-done.1), custom_call_target="tpu_custom_call" | custom-call | flops 1000000000 | bytes 1000000 | tf_op jit(solution)/shard_map/grads/pallas_call | solution.py:456
  32.4 0.8 %spread.1 = (f32[4,128,256]{2,1,0:T(8,128)}, f32[1,256]{1,0:T(1,128)S(1)}) custom-call(bf16[128,256]{1,0:T(8,128)(2,1)S(1)} %get-tuple-element.37.refs_0_, bf16[128,256]{1,0:T(8,128)(2,1)S(1)} %collective-permute-done.6.refs_1_, bf16[128,256]{1,0:T(8,128)(2,1)S(1)} %collective-permute-done.7.refs_2_, bf16[128,256]{1,0:T(8,128)(2,1)S(1)} %collective-permute-done.8.refs_3_, ...), custom_call_target="tpu_custom_call" | custom-call | tf_op jit(solution)/shard_map/spread/pallas_call | solution.py:464
  33.3 0.7 %scale.1 = (bf16[512,256]{1,0:T(8,128)(2,1)}, f32[1,256]{1,0:T(1,128)}) custom-call(f32[512,256]{1,0:T(8,128)S(1)} %get-tuple-element.35.resp_ref, f32[1,256]{1,0:T(1,128)S(1)} %get-tuple-element.42.near_ref, f32[1,256]{1,0:T(1,128)S(1)} %collective-permute-done.11.far_ref), custom_call_target="tpu_custom_call" | custom-call | flops 1000000000 | bytes 1000000 | tf_op jit(solution)/shard_map/scale/pallas_call | solution.py:472
  (23 shorter events, 0.1 us)
Async XLA Ops:
  0.6 1.5 %copy-start.5 = (s32[3,512,2]{1,2,0:T(2,128)S(1)}, s32[3,512,2]{1,2,0:T(2,128)}, u32[]{:S(2)}) copy-start(s32[3,512,2]{1,2,0:T(2,128)} %param.10) | copy-start | bytes 36868
  0.6 14.0 %copy-start.4 = (bf16[512,512]{1,0:T(8,128)(2,1)S(1)}, bf16[512,512]{1,0:T(8,128)(2,1)}, u32[]{:S(2)}) copy-start(bf16[512,512]{1,0:T(8,128)(2,1)} %constant.7.clone.low_ref) | copy-start | bytes 1572868
  2.0 12.6 %copy-start = (bf16[512,512]{1,0:T(8,128)(2,1)S(1)}, bf16[512,512]{1,0:T(8,128)(2,1)}, u32[]{:S(2)}) copy-start(bf16[512,512]{1,0:T(8,128)(2,1)} %constant.6.clone.high_ref.refs_6_) | copy-start | bytes 1572868
  2.0 12.6 %copy-start.2 = (bf16[512,1024]{1,0:T(8,128)(2,1)S(1)}, bf16[512,1024]{1,0:T(8,128)(2,1)}, u32[]{:S(2)}) copy-start(bf16[512,1024]{1,0:T(8,128)(2,1)} %filt_ref.1) | copy-start | bytes 3145732
  2.1 12.6 %copy-start.3 = (bf16[3,512,256]{2,1,0:T(8,128)(2,1)S(1)}, bf16[3,512,256]{2,1,0:T(8,128)(2,1)}, u32[]{:S(2)}) copy-start(bf16[3,512,256]{2,1,0:T(8,128)(2,1)} %proj_ref.1) | copy-start | bytes 2359300
  2.1 12.6 %copy-start.6 = (s32[512]{0:T(512)S(1)}, s32[512]{0:T(512)}, u32[]{:S(2)}) copy-start(s32[512]{0:T(512)} %param.12) | copy-start | bytes 6148
  2.1 12.6 %copy-start.7 = (f32[512]{0:T(512)S(1)}, f32[512]{0:T(512)}, u32[]{:S(2)}) copy-start(f32[512]{0:T(512)} %param.13) | copy-start | bytes 6148
  2.5 10.1 %collective-permute-start.2 = (bf16[512,256]{1,0:T(8,128)(2,1)S(1)}, bf16[512,256]{1,0:T(8,128)(2,1)S(1)}, u32[]{:S(2)}, u32[]{:S(2)}) collective-permute-start(bf16[512,256]{1,0:T(8,128)(2,1)S(1)} %get-tuple-element.30), channel_id=1, source_target_pairs={{0,8},{8,0},{16,24},{24,16},{1,9},{9,1},{17,25},{25,17},{2,10},{10... | collective-permute-start | bytes 786440 | tf_op jit(solution)/shard_map/ppermute | solution.py:380
  5.5 15.5 %collective-permute-start = (bf16[512,256]{1,0:T(8,128)(2,1)S(1)}, bf16[512,256]{1,0:T(8,128)(2,1)S(1)}, u32[]{:S(2)}, u32[]{:S(2)}) collective-permute-start(bf16[512,256]{1,0:T(8,128)(2,1)S(1)} %get-tuple-element.28.main_ref), channel_id=1, source_target_pairs={{0,16},{8,24},{16,0},{24,8},{1,17},{9,25},{17,1},{25,9},{2,18},{10... | collective-permute-start | bytes 786440 | tf_op jit(solution)/shard_map/ppermute | solution.py:380
  7.0 14.0 %collective-permute-start.1 = (bf16[512,256]{1,0:T(8,128)(2,1)S(1)}, bf16[512,256]{1,0:T(8,128)(2,1)S(1)}, u32[]{:S(2)}, u32[]{:S(2)}) collective-permute-start(bf16[512,256]{1,0:T(8,128)(2,1)S(1)} %get-tuple-element.28.main_ref), channel_id=1, source_target_pairs={{0,24},{8,16},{16,8},{24,0},{1,25},{9,17},{17,9},{25,1},{2,26},{10... | collective-permute-start | bytes 786440 | tf_op jit(solution)/shard_map/ppermute | solution.py:380
  7.0 15.3 %collective-permute-start.4 = (bf16[128,256]{1,0:T(8,128)(2,1)S(1)}, bf16[128,256]{1,0:T(8,128)(2,1)S(1)}, u32[]{:S(2)}, u32[]{:S(2)}) collective-permute-start(bf16[128,256]{1,0:T(8,128)(2,1)S(1)} %pick.4), channel_id=1, source_target_pairs={{0,16},{8,24},{16,0},{24,8},{1,17},{9,25},{17,1},{25,9},{2,18},{10... | collective-permute-start | bytes 196616 | tf_op jit(solution)/shard_map/ppermute | solution.py:380
  9.0 12.0 %copy-start.1 = (bf16[512,512]{1,0:T(8,128)(2,1)S(1)}, bf16[512,512]{1,0:T(8,128)(2,1)}, u32[]{:S(2)}) copy-start(bf16[512,512]{1,0:T(8,128)(2,1)} %constant.8.clone.refs_7_.inv_ref) | copy-start | bytes 1572868
  9.0 13.3 %collective-permute-start.5 = (bf16[128,256]{1,0:T(8,128)(2,1)S(1)}, bf16[128,256]{1,0:T(8,128)(2,1)S(1)}, u32[]{:S(2)}, u32[]{:S(2)}) collective-permute-start(bf16[128,256]{1,0:T(8,128)(2,1)S(1)} %pick.5), channel_id=1, source_target_pairs={{0,24},{8,16},{16,8},{24,0},{1,25},{9,17},{17,9},{25,1},{2,26},{10... | collective-permute-start | bytes 196616 | tf_op jit(solution)/shard_map/ppermute | solution.py:380
  12.6 9.7 %collective-permute-start.3 = (bf16[128,256]{1,0:T(8,128)(2,1)S(1)}, bf16[128,256]{1,0:T(8,128)(2,1)S(1)}, u32[]{:S(2)}, u32[]{:S(2)}) collective-permute-start(bf16[128,256]{1,0:T(8,128)(2,1)S(1)} %pick.3), channel_id=1, source_target_pairs={{0,8},{8,0},{16,24},{24,16},{1,9},{9,1},{17,25},{25,17},{2,10},{10... | collective-permute-start | bytes 196616 | tf_op jit(solution)/shard_map/ppermute | solution.py:380
  22.2 9.0 %copy-start.8 = (bf16[512,256]{1,0:T(8,128)(2,1)S(1)}, bf16[512,256]{1,0:T(8,128)(2,1)}, u32[]{:S(2)}) copy-start(bf16[512,256]{1,0:T(8,128)(2,1)} %cot_ref.1) | copy-start | bytes 786436
  22.2 1.2 %collective-permute-start.9 = (f32[1,256]{1,0:T(1,128)S(1)}, f32[1,256]{1,0:T(1,128)S(1)}, u32[]{:S(2)}, u32[]{:S(2)}) collective-permute-start(f32[1,256]{1,0:T(1,128)S(1)} %get-tuple-element.36.refs_6_), channel_id=1, source_target_pairs={{0,1},{1,0},{2,3},{3,2},{4,5},{5,4},{6,7},{7,6},{8,9},{9,8},{10,11... | collective-permute-start | bytes 3080 | tf_op jit(solution)/shard_map/ppermute | solution.py:380
  23.5 5.1 %collective-permute-start.10 = (f32[1,256]{1,0:T(1,128)S(1)}, f32[1,256]{1,0:T(1,128)S(1)}, u32[]{:S(2)}, u32[]{:S(2)}) collective-permute-start(f32[1,256]{1,0:T(1,128)S(1)} %max.6), channel_id=1, source_target_pairs={{0,2},{1,3},{2,0},{3,1},{4,6},{5,7},{6,4},{7,5},{8,10},{9,11},{10,... | collective-permute-start | bytes 3080 | tf_op jit(solution)/shard_map/ppermute | solution.py:380
  25.1 7.3 %collective-permute-start.6 = (bf16[128,256]{1,0:T(8,128)(2,1)S(1)}, bf16[128,256]{1,0:T(8,128)(2,1)S(1)}, u32[]{:S(2)}, u32[]{:S(2)}) collective-permute-start(bf16[128,256]{1,0:T(8,128)(2,1)S(1)} %get-tuple-element.38), channel_id=1, source_target_pairs={{0,8},{8,0},{16,24},{24,16},{1,9},{9,1},{17,25},{25,17},{2,10},{10... | collective-permute-start | bytes 196616 | tf_op jit(solution)/shard_map/ppermute | solution.py:380
  25.4 7.0 %collective-permute-start.7 = (bf16[128,256]{1,0:T(8,128)(2,1)S(1)}, bf16[128,256]{1,0:T(8,128)(2,1)S(1)}, u32[]{:S(2)}, u32[]{:S(2)}) collective-permute-start(bf16[128,256]{1,0:T(8,128)(2,1)S(1)} %get-tuple-element.39), channel_id=1, source_target_pairs={{0,16},{8,24},{16,0},{24,8},{1,17},{9,25},{17,1},{25,9},{2,18},{10... | collective-permute-start | bytes 196616 | tf_op jit(solution)/shard_map/ppermute | solution.py:380
  27.2 5.2 %collective-permute-start.8 = (bf16[128,256]{1,0:T(8,128)(2,1)S(1)}, bf16[128,256]{1,0:T(8,128)(2,1)S(1)}, u32[]{:S(2)}, u32[]{:S(2)}) collective-permute-start(bf16[128,256]{1,0:T(8,128)(2,1)S(1)} %get-tuple-element.40), channel_id=1, source_target_pairs={{0,24},{8,16},{16,8},{24,0},{1,25},{9,17},{17,9},{25,1},{2,26},{10... | collective-permute-start | bytes 196616 | tf_op jit(solution)/shard_map/ppermute | solution.py:380
  28.6 4.6 %collective-permute-start.11 = (f32[1,256]{1,0:T(1,128)S(1)}, f32[1,256]{1,0:T(1,128)S(1)}, u32[]{:S(2)}, u32[]{:S(2)}) collective-permute-start(f32[1,256]{1,0:T(1,128)S(1)} %max.7.refs_4_), channel_id=1, source_target_pairs={{0,4},{1,5},{2,6},{3,7},{4,0},{5,1},{6,2},{7,3},{8,12},{9,13},{10,... | collective-permute-start | bytes 3080 | tf_op jit(solution)/shard_map/ppermute | solution.py:380

commit v5 on v4

--- a/solution.py
+++ b/solution.py
@@ -85,6 +85,14 @@
         lax.fori_loop(0, total // step, one, 0)
 
     return run
+
+
+def early(n):
+    return min(3, n - 1)
+
+
+def others(n):
+    return [k for k in range(1, n) if k != early(n)]
 
 
 def top_bit(n):
@@ -172,9 +180,10 @@
             )
             sign = jnp.where(other < me, 1.0, -1.0).astype(F32)
             wr, wi = win[:, :span], win[:, span:] * sign
-            if k > 1:
-                win_refs[k - 2][block, :span] = wr.astype(BF16)
-                win_refs[k - 2][block, span:] = wi.astype(BF16)
+            if k != early(n):
+                slot = others(n).index(k)
+                win_refs[slot][block, :span] = wr.astype(BF16)
+                win_refs[slot][block, span:] = wi.astype(BF16)
                 continue
             later = jnp.where(other > me, 1, 0)
             start = pl.multiple_of(later * span, span)
@@ -184,39 +193,26 @@
             base_ref[later, block, span:] += xr * wi + xi * wr
 
 
-def conv_kernel(n, seq_len, rows, *refs):
+def conv_kernel(n, seq_len, *refs):
     recv_refs, win_refs, refs = refs[: n - 2], refs[n - 2 : 2 * n - 4], refs[2 * n - 4 :]
-    base_ref, deq_ref, high_ref, inv_ref, back_ref, resp_ref, conv_ref, peak_ref = refs
-    me = lax.axis_index("ctx")
-    channels, span = resp_ref.shape
+    _, deq_ref, high_ref, inv_ref, acc, resp_ref, conv_ref, peak_ref = refs
+    me = lax.axis_index("ctx")
+    span = resp_ref.shape[1]
     fscale = 1.0 / math.sqrt(seq_len)
-    uppers = [lax.rem(lax.div(me, 2**bit), 2) for bit in range((n - 1).bit_length())]
-    starts = [pl.multiple_of((1 - upper) * span, span) for upper in uppers]
-    peaks = []
-    for first in range(0, channels, rows):
-        tile = slice(first, first + rows)
-        fr, fi = base_ref[0, tile, :span], base_ref[0, tile, span:]
-        br, bi = base_ref[1, tile, :span], base_ref[1, tile, span:]
-        for bit in range(1, len(uppers)):
-            real = imag = 0.0
-            for k in range(2**bit, min(2 ** (bit + 1), n)):
-                spec = mm(recv_refs[k - 2][tile], high_ref[pl.ds(starts[bit], span), :])
-                xr, xi = spec[:, :span], spec[:, span:]
-                wr = win_refs[k - 2][tile, :span].astype(F32)
-                wi = win_refs[k - 2][tile, span:].astype(F32)
-                real += xr * wr - xi * wi
-                imag += xr * wi + xi * wr
-            here = uppers[bit] == 1
-            fr, br = jnp.where(here, fr + real, fr), jnp.where(here, br, br + real)
-            fi, bi = jnp.where(here, fi + imag, fi), jnp.where(here, bi, bi + imag)
-        back_ref[tile, :span], back_ref[tile, span:] = br.astype(BF16), bi.astype(BF16)
-        front = jnp.concatenate([fr.astype(BF16), fi.astype(BF16)], axis=1)
-        conv = mm(front, inv_ref[:, span:]) * fscale
-        response = deq_ref[0, tile].astype(F32) * conv
-        resp_ref[tile] = response
-        conv_ref[tile] = conv
-        peaks.append(jnp.max(jnp.abs(response), axis=0, keepdims=True))
-    peak_ref[...] = functools.reduce(jnp.maximum, peaks)
+    for k, recv_ref, win_ref in zip(others(n), recv_refs, win_refs):
+        later = jnp.where(jnp.bitwise_xor(me, k) > me, 1, 0)
+        start = pl.multiple_of(later * span, span)
+        spec = mm(recv_ref[...], high_ref[pl.ds(start, span), :])
+        xr, xi = spec[:, :span], spec[:, span:]
+        wr = win_ref[:, :span].astype(F32)
+        wi = win_ref[:, span:].astype(F32)
+        acc[later, :, :span] += xr * wr - xi * wi
+        acc[later, :, span:] += xr * wi + xi * wr
+    conv = mm(acc[0].astype(BF16), inv_ref[:, span:]) * fscale
+    response = deq_ref[0].astype(F32) * conv
+    resp_ref[...] = response
+    conv_ref[...] = conv
+    peak_ref[...] = jnp.max(jnp.abs(response), axis=0, keepdims=True)
 
 
 def taps_kernel(n, seq_len, main_ref, rest_ref, reach_ref, high_ref, inv_ref, *refs):
@@ -300,7 +296,7 @@
         out_ref[...] = rest_ref[other]
 
 
-def grads_kernel(seq_len, deq_ref, cot_ref, conv_ref, back_ref, inv_ref, grad_hbm, grad, grad_sem):
+def grads_kernel(seq_len, deq_ref, cot_ref, conv_ref, acc_ref, inv_ref, grad_hbm, grad, grad_sem):
     span = cot_ref.shape[1]
     fscale = 1.0 / math.sqrt(seq_len)
     copies = []
@@ -311,7 +307,7 @@
         copies[-1].start()
 
     send(0, cot_ref[...].astype(F32) * conv_ref[...])
-    grad_mixed = mm(back_ref[...], inv_ref[:, :span]) * fscale
+    grad_mixed = mm(acc_ref[1].astype(BF16), inv_ref[:, :span]) * fscale
     send(1, grad_mixed * deq_ref[2].astype(F32))
     send(2, grad_mixed * deq_ref[1].astype(F32))
     for copy in copies:
@@ -419,15 +415,16 @@
             pltpu.VMEM((channels, 1), jnp.int32),
             pltpu.VMEM((channels, 1), F32),
         ],
-    )(proj, exps, filt, reach_row, skip_row, main, rest, high, low, first[0])
-    second[1] = swap(pick(1, first[0]), "ctx", 1)
-
-    back, response, conv, peak = call(
-        functools.partial(conv_kernel, n, seq_len, channels),
+    )(proj, exps, filt, reach_row, skip_row, main, rest, high, low, first[early(n) - 1])
+    second[1] = swap(pick(1, first[early(n) - 1]), "ctx", 1)
+
+    acc, response, conv, peak = call(
+        functools.partial(conv_kernel, n, seq_len),
         "conv",
         [vmem] * (2 * n),
-        [wide] + [shape((channels, span), F32)] * 2 + [line],
-    )(*first[1:], *wins, base, deq, high, inverse)
+        [shape((2, channels, 2 * span), F32)] + [shape((channels, span), F32)] * 2 + [line],
+        input_output_aliases={2 * n - 4: 0},
+    )(*[first[k - 1] for k in others(n)], *wins, base, deq, high, inverse)
 
     far = swap(peak, "ch", 1)
     own_part, *parts_out, peak = call(
@@ -460,7 +457,7 @@
         [shape((3, channels, span), BF16)],
         out_specs=[hbm],
         scratch_shapes=[pltpu.VMEM((3, channels, span), BF16), pltpu.SemaphoreType.DMA((3,))],
-    )(deq, cotangent, conv, back, inverse)
+    )(deq, cotangent, conv, acc, inverse)
     filter_grad, peak = call(
         functools.partial(spread_kernel, n),
         "spread",

time: 34.2 us -> 33.4 us (0.977)
  waiting for transfers between devices: 4.78 us -> 4.22 us
    ppermute x12, waiting for transfers between devices: 4.78 us -> 4.22 us  [swap(): lax.ppermute(value, axis, [(j, j ^ k) for j in range(lax.axis_size(axis))])]
  transfers between devices with their start and end apart: 12 -> 12, of which waited for: 2 -> 5; matrix products, arithmetic and copies ran while one was open for 0% -> 0% of each run, Pallas kernels for 23% -> 24%
where the time goes in v5:
time: 33.4 us; the launch traced here: 33.3 us
  starting transfers between devices  17.8 us (53%)
  Pallas kernels  10.3 us (31%)
  waiting for transfers between devices  4.22 us (13%)
  between operations  0.84 us (3%)
    ppermute x12, starting transfers between devices, swap(): lax.ppermute(value, axis, [(j, j ^ k) for j in range(lax.axis_size(axis))])  17.8 us
    ppermute x12, waiting for transfers between devices, swap(): lax.ppermute(value, axis, [(j, j ^ k) for j in range(lax.axis_size(axis))])  4.22 us
    pallas_call x1, Pallas kernels, body(): call(functools.partial(windows_kernel, n, rows), 'windows', [vmem] * 10,...  3.58 us
    pallas_call x1, Pallas kernels, body(): call(functools.partial(load_kernel, parts), 'load', [hbm] * 2, [flat] * 2...  1.37 us
    pallas_call x1, Pallas kernels, body(): call(functools.partial(grads_kernel, seq_len), 'grads', [vmem] * 5, [shap...  1.18 us
    pallas_call x1, Pallas kernels, body(): call(functools.partial(conv_kernel, n, seq_len), 'conv', [vmem] * (2 * n)...  1.16 us
    pallas_call x1, Pallas kernels, body(): call(functools.partial(taps_kernel, n, seq_len), 'taps', [vmem] * (2 * n...  1.09 us
    pallas_call x1, Pallas kernels, body(): call(functools.partial(spread_kernel, n), 'spread', [vmem] * (n + 1), [sh...  0.84 us
  transfers between devices with their start and end apart: 12, of which 5 were waited for; matrix products, arithmetic and copies ran while one was open for 0% of the time, Pallas kernels for 24%

profile of v5, /device:TPU:0, one launch (start us, length us, event | category | flops | bytes accessed | tf_op | source)
XLA Modules:
  0.0 33.3 jit_solution(4771578889234118720)
XLA Ops:
  0.6 0.0 copy-start.4
  0.7 1.4 %load.1 = (bf16[512,256]{1,0:T(8,128)(2,1)S(1)}, bf16[512,256]{1,0:T(8,128)(2,1)S(1)}) custom-call(bf16[3,512,256]{2,1,0:T(8,128)(2,1)} %proj_ref.1, bf16[512,256]{1,0:T(8,128)(2,1)} %cot_ref.1), custom_call_target="tpu_custom_call" | custom-call | flops 1000000000 | bytes 1000000 | tf_op jit(solution)/shard_map/load/pallas_call | solution.py:381
  2.0 0.0 copy-start.1
  2.0 0.0 copy-start.2
  2.1 0.0 copy-start.3
  2.1 0.0 copy-start.7
  2.1 0.0 copy-start.8
  2.1 0.3 %prep.1 = (bf16[512,256]{1,0:T(8,128)(2,1)S(1)}, bf16[512,256]{1,0:T(8,128)(2,1)S(1)}, bf16[512,256]{1,0:T(8,128)(2,1)S(1)}) custom-call(bf16[512,256]{1,0:T(8,128)(2,1)S(1)} %get-tuple-element.26.key_value_ref, bf16[512,256]{1,0:T(8,128)(2,1)S(1)} %get-tuple-element.27.query_cot_ref, s32[3,2,512]{2,1,0:T(2,128)S(1)} %bitcast.22), custom_call_target="tpu_custom_call" | custom-call | tf_op jit(solution)/shard_map/prep/pallas_call | solution.py:394
  2.5 4.0 %collective-permute-start.2 = (bf16[512,256]{1,0:T(8,128)(2,1)S(1)}, bf16[512,256]{1,0:T(8,128)(2,1)S(1)}, u32[]{:S(2)}, u32[]{:S(2)}) collective-permute-start(bf16[512,256]{1,0:T(8,128)(2,1)S(1)} %get-tuple-element.29.main_ref), channel_id=1, source_target_pairs={{0,24},{8,16},{16,8},{24,0},{1,25},{9,17},{17,9},{25,1},{2,26},{10... | collective-permute-start | bytes 786440 | tf_op jit(solution)/shard_map/ppermute | solution.py:376
  6.4 0.5 %collective-permute-start.1 = (bf16[512,256]{1,0:T(8,128)(2,1)S(1)}, bf16[512,256]{1,0:T(8,128)(2,1)S(1)}, u32[]{:S(2)}, u32[]{:S(2)}) collective-permute-start(bf16[512,256]{1,0:T(8,128)(2,1)S(1)} %get-tuple-element.29.main_ref), channel_id=1, source_target_pairs={{0,16},{8,24},{16,0},{24,8},{1,17},{9,25},{17,1},{25,9},{2,18},{10... | collective-permute-start | bytes 786440 | tf_op jit(solution)/shard_map/ppermute | solution.py:376
  6.9 0.1 collective-permute-start
  7.1 1.9 %collective-permute-start.4 = (bf16[128,256]{1,0:T(8,128)(2,1)S(1)}, bf16[128,256]{1,0:T(8,128)(2,1)S(1)}, u32[]{:S(2)}, u32[]{:S(2)}) collective-permute-start(bf16[128,256]{1,0:T(8,128)(2,1)S(1)} %pick.4), channel_id=1, source_target_pairs={{0,16},{8,24},{16,0},{24,8},{1,17},{9,25},{17,1},{25,9},{2,18},{10... | collective-permute-start | bytes 196616 | tf_op jit(solution)/shard_map/ppermute | solution.py:376
  9.0 1.5 %collective-permute-start.5 = (bf16[128,256]{1,0:T(8,128)(2,1)S(1)}, bf16[128,256]{1,0:T(8,128)(2,1)S(1)}, u32[]{:S(2)}, u32[]{:S(2)}) collective-permute-start(bf16[128,256]{1,0:T(8,128)(2,1)S(1)} %pick.5), channel_id=1, source_target_pairs={{0,24},{8,16},{16,8},{24,0},{1,25},{9,17},{17,9},{25,1},{2,26},{10... | collective-permute-start | bytes 196616 | tf_op jit(solution)/shard_map/ppermute | solution.py:376
  10.5 3.1 %collective-permute-done.2.recv_ref.refs_0_ = bf16[512,256]{1,0:T(8,128)(2,1)S(1)} collective-permute-done((bf16[512,256]{1,0:T(8,128)(2,1)S(1)}, bf16[512,256]{1,0:T(8,128)(2,1)S(1)}, u32[]{:S(2)}, u32[]{:S(2)}) %collective-permute-start.2) | collective-permute-done | bytes 262176 | tf_op jit(solution)/shard_map/ppermute | solution.py:376
  13.6 2.0 %collective-permute-start.3 = (bf16[128,256]{1,0:T(8,128)(2,1)S(1)}, bf16[128,256]{1,0:T(8,128)(2,1)S(1)}, u32[]{:S(2)}, u32[]{:S(2)}) collective-permute-start(bf16[128,256]{1,0:T(8,128)(2,1)S(1)} %pick.3), channel_id=1, source_target_pairs={{0,8},{8,0},{16,24},{24,16},{1,9},{9,1},{17,25},{25,17},{2,10},{10... | collective-permute-start | bytes 196616 | tf_op jit(solution)/shard_map/ppermute | solution.py:376
  15.6 3.6 %windows.1 = (bf16[3,512,256]{2,1,0:T(8,128)(2,1)S(1)}, f32[2,512,512]{2,1,0:T(8,128)S(1)}, bf16[512,512]{1,0:T(8,128)(2,1)S(1)}, bf16[512,512]{1,0:T(8,128)(2,1)S(1)}) custom-call(bf16[3,512,256]{2,1,0:T(8,128)(2,1)S(1)} %copy-done.3, s32[3,2,512]{2,1,0:T(2,128)S(1)} %bitcast.23, bf16[512,1024]{1,0:T(8,128)(2,1)S(1)} %copy-done.2, s32[1,512]{1,0:T(1,128)S(1)} %bitcast.24, ...), custom_call_target="tpu_custom_call" | custom-call | tf_op jit(solution)/shard_map/windows/pallas_call | solution.py:408
  19.2 0.5 %collective-permute-done.refs_0_ = bf16[512,256]{1,0:T(8,128)(2,1)S(1)} collective-permute-done((bf16[512,256]{1,0:T(8,128)(2,1)S(1)}, bf16[512,256]{1,0:T(8,128)(2,1)S(1)}, u32[]{:S(2)}, u32[]{:S(2)}) %collective-permute-start) | collective-permute-done | bytes 262176 | tf_op jit(solution)/shard_map/ppermute | solution.py:376
  19.8 1.2 %conv.1 = (f32[2,512,512]{2,1,0:T(8,128)S(1)}, f32[512,256]{1,0:T(8,128)S(1)}, f32[512,256]{1,0:T(8,128)S(1)}, f32[1,256]{1,0:T(1,128)S(1)}) custom-call(bf16[512,256]{1,0:T(8,128)(2,1)S(1)} %collective-permute-done.refs_0_, bf16[512,256]{1,0:T(8,128)(2,1)S(1)} %collective-permute-done.1.refs_1_, ...), custom_call_target="tpu_custom_call", output_to_operand_aliasing={{0}: (4, {})} | custom-call | tf_op jit(solution)/shard_map/conv/pallas_call | solution.py:421
  21.0 0.0 copy-start.5
  21.0 0.1 collective-permute-start.9
  21.0 0.1 collective-permute-done.4.refs_4_
  21.2 0.3 collective-permute-done.3.refs_3_
  21.4 1.1 %taps.1 = (bf16[128,256]{1,0:T(8,128)(2,1)S(1)}, bf16[128,256]{1,0:T(8,128)(2,1)S(1)}, bf16[128,256]{1,0:T(8,128)(2,1)S(1)}, bf16[128,256]{1,0:T(8,128)(2,1)S(1)}, f32[1,256]{1,0:T(1,128)S(1)}) custom-call(bf16[4,128,256]{2,1,0:T(8,128)(2,1)S(1)} %bitcast.14, bf16[4,128,256]{2,1,0:T(8,128)(2,1)S(1)} %bitcast.18, s32[4,1,128]{2,1,0:T(1,128)S(1)} %bitcast.25, ...), custom_call_target="tpu_custom_call" | custom-call | tf_op jit(solution)/shard_map/taps/pallas_call | solution.py:430
  22.6 1.6 %collective-permute-start.10 = (f32[1,256]{1,0:T(1,128)S(1)}, f32[1,256]{1,0:T(1,128)S(1)}, u32[]{:S(2)}, u32[]{:S(2)}) collective-permute-start(f32[1,256]{1,0:T(1,128)S(1)} %max.6), channel_id=1, source_target_pairs={{0,2},{1,3},{2,0},{3,1},{4,6},{5,7},{6,4},{7,5},{8,10},{9,11},{10,... | collective-permute-start | bytes 3080 | tf_op jit(solution)/shard_map/ppermute | solution.py:376
  24.2 1.5 %collective-permute-start.6 = (bf16[128,256]{1,0:T(8,128)(2,1)S(1)}, bf16[128,256]{1,0:T(8,128)(2,1)S(1)}, u32[]{:S(2)}, u32[]{:S(2)}) collective-permute-start(bf16[128,256]{1,0:T(8,128)(2,1)S(1)} %get-tuple-element.38), channel_id=1, source_target_pairs={{0,8},{8,0},{16,24},{24,16},{1,9},{9,1},{17,25},{25,17},{2,10},{10... | collective-permute-start | bytes 196616 | tf_op jit(solution)/shard_map/ppermute | solution.py:376
  25.7 0.8 %collective-permute-start.7 = (bf16[128,256]{1,0:T(8,128)(2,1)S(1)}, bf16[128,256]{1,0:T(8,128)(2,1)S(1)}, u32[]{:S(2)}, u32[]{:S(2)}) collective-permute-start(bf16[128,256]{1,0:T(8,128)(2,1)S(1)} %get-tuple-element.39), channel_id=1, source_target_pairs={{0,16},{8,24},{16,0},{24,8},{1,17},{9,25},{17,1},{25,9},{2,18},{10... | collective-permute-start | bytes 196616 | tf_op jit(solution)/shard_map/ppermute | solution.py:376
  26.5 1.2 %collective-permute-start.8 = (bf16[128,256]{1,0:T(8,128)(2,1)S(1)}, bf16[128,256]{1,0:T(8,128)(2,1)S(1)}, u32[]{:S(2)}, u32[]{:S(2)}) collective-permute-start(bf16[128,256]{1,0:T(8,128)(2,1)S(1)} %get-tuple-element.40), channel_id=1, source_target_pairs={{0,24},{8,16},{16,8},{24,0},{1,25},{9,17},{17,9},{25,1},{2,26},{10... | collective-permute-start | bytes 196616 | tf_op jit(solution)/shard_map/ppermute | solution.py:376
  27.7 2.6 %collective-permute-start.11 = (f32[1,256]{1,0:T(1,128)S(1)}, f32[1,256]{1,0:T(1,128)S(1)}, u32[]{:S(2)}, u32[]{:S(2)}) collective-permute-start(f32[1,256]{1,0:T(1,128)S(1)} %max.7.refs_4_), channel_id=1, source_target_pairs={{0,4},{1,5},{2,6},{3,7},{4,0},{5,1},{6,2},{7,3},{8,12},{9,13},{10,... | collective-permute-start | bytes 3080 | tf_op jit(solution)/shard_map/ppermute | solution.py:376
  30.3 1.2 %grads.1 = bf16[3,512,256]{2,1,0:T(8,128)(2,1)} custom-call(bf16[3,512,256]{2,1,0:T(8,128)(2,1)S(1)} %get-tuple-element.34.refs_5_.deq_ref, bf16[512,256]{1,0:T(8,128)(2,1)S(1)} %copy-done.5, f32[512,256]{1,0:T(8,128)S(1)} %get-tuple-element.45.conv_ref, f32[2,512,512]{2,1,0:T(8,128)S(1)} %get-tuple-element.46.acc_ref, bf16[512,512]{1,0:T(8,128)(2,1)S(1)} %copy-done), custom_call_target="tpu_custom_call" | custom-call | flops 1000000000 | bytes 1000000 | tf_op jit(solution)/shard_map/grads/pallas_call | solution.py:453
  31.5 0.1 collective-permute-done.8.refs_3_
  31.7 0.8 %spread.1 = (f32[4,128,256]{2,1,0:T(8,128)}, f32[1,256]{1,0:T(1,128)S(1)}) custom-call(bf16[128,256]{1,0:T(8,128)(2,1)S(1)} %get-tuple-element.37.refs_0_, bf16[128,256]{1,0:T(8,128)(2,1)S(1)} %collective-permute-done.6.refs_1_, bf16[128,256]{1,0:T(8,128)(2,1)S(1)} %collective-permute-done.7.refs_2_, bf16[128,256]{1,0:T(8,128)(2,1)S(1)} %collective-permute-done.8.refs_3_, ...), custom_call_target="tpu_custom_call" | custom-call | tf_op jit(solution)/shard_map/spread/pallas_call | solution.py:461
  32.5 0.7 %scale.1 = (bf16[512,256]{1,0:T(8,128)(2,1)}, f32[1,256]{1,0:T(1,128)}) custom-call(f32[512,256]{1,0:T(8,128)S(1)} %get-tuple-element.35.resp_ref, f32[1,256]{1,0:T(1,128)S(1)} %get-tuple-element.42.near_ref, f32[1,256]{1,0:T(1,128)S(1)} %collective-permute-done.11.far_ref), custom_call_target="tpu_custom_call" | custom-call | flops 1000000000 | bytes 1000000 | tf_op jit(solution)/shard_map/scale/pallas_call | solution.py:469
  (23 shorter events, 0.1 us)
Async XLA Ops:
  0.6 1.5 %copy-start.6 = (s32[3,512,2]{1,2,0:T(2,128)S(1)}, s32[3,512,2]{1,2,0:T(2,128)}, u32[]{:S(2)}) copy-start(s32[3,512,2]{1,2,0:T(2,128)} %param.10) | copy-start | bytes 36868
  0.6 15.0 %copy-start.4 = (bf16[512,512]{1,0:T(8,128)(2,1)S(1)}, bf16[512,512]{1,0:T(8,128)(2,1)}, u32[]{:S(2)}) copy-start(bf16[512,512]{1,0:T(8,128)(2,1)} %constant.7.clone.low_ref) | copy-start | bytes 1572868
  2.0 13.6 %copy-start.1 = (bf16[512,512]{1,0:T(8,128)(2,1)S(1)}, bf16[512,512]{1,0:T(8,128)(2,1)}, u32[]{:S(2)}) copy-start(bf16[512,512]{1,0:T(8,128)(2,1)} %constant.6.clone.high_ref.refs_6_) | copy-start | bytes 1572868
  2.0 13.6 %copy-start.2 = (bf16[512,1024]{1,0:T(8,128)(2,1)S(1)}, bf16[512,1024]{1,0:T(8,128)(2,1)}, u32[]{:S(2)}) copy-start(bf16[512,1024]{1,0:T(8,128)(2,1)} %filt_ref.1) | copy-start | bytes 3145732
  2.1 13.6 %copy-start.3 = (bf16[3,512,256]{2,1,0:T(8,128)(2,1)S(1)}, bf16[3,512,256]{2,1,0:T(8,128)(2,1)}, u32[]{:S(2)}) copy-start(bf16[3,512,256]{2,1,0:T(8,128)(2,1)} %proj_ref.1) | copy-start | bytes 2359300
  2.1 13.5 %copy-start.7 = (s32[512]{0:T(512)S(1)}, s32[512]{0:T(512)}, u32[]{:S(2)}) copy-start(s32[512]{0:T(512)} %param.12) | copy-start | bytes 6148
  2.1 13.5 %copy-start.8 = (f32[512]{0:T(512)S(1)}, f32[512]{0:T(512)}, u32[]{:S(2)}) copy-start(f32[512]{0:T(512)} %param.13) | copy-start | bytes 6148
  2.5 11.1 %collective-permute-start.2 = (bf16[512,256]{1,0:T(8,128)(2,1)S(1)}, bf16[512,256]{1,0:T(8,128)(2,1)S(1)}, u32[]{:S(2)}, u32[]{:S(2)}) collective-permute-start(bf16[512,256]{1,0:T(8,128)(2,1)S(1)} %get-tuple-element.29.main_ref), channel_id=1, source_target_pairs={{0,24},{8,16},{16,8},{24,0},{1,25},{9,17},{17,9},{25,1},{2,26},{10... | collective-permute-start | bytes 786440 | tf_op jit(solution)/shard_map/ppermute | solution.py:376
  6.4 12.8 %collective-permute-start.1 = (bf16[512,256]{1,0:T(8,128)(2,1)S(1)}, bf16[512,256]{1,0:T(8,128)(2,1)S(1)}, u32[]{:S(2)}, u32[]{:S(2)}) collective-permute-start(bf16[512,256]{1,0:T(8,128)(2,1)S(1)} %get-tuple-element.29.main_ref), channel_id=1, source_target_pairs={{0,16},{8,24},{16,0},{24,8},{1,17},{9,25},{17,1},{25,9},{2,18},{10... | collective-permute-start | bytes 786440 | tf_op jit(solution)/shard_map/ppermute | solution.py:376
  6.9 12.9 %collective-permute-start = (bf16[512,256]{1,0:T(8,128)(2,1)S(1)}, bf16[512,256]{1,0:T(8,128)(2,1)S(1)}, u32[]{:S(2)}, u32[]{:S(2)}) collective-permute-start(bf16[512,256]{1,0:T(8,128)(2,1)S(1)} %get-tuple-element.28), channel_id=1, source_target_pairs={{0,8},{8,0},{16,24},{24,16},{1,9},{9,1},{17,25},{25,17},{2,10},{10... | collective-permute-start | bytes 786440 | tf_op jit(solution)/shard_map/ppermute | solution.py:376
  7.1 14.1 %collective-permute-start.4 = (bf16[128,256]{1,0:T(8,128)(2,1)S(1)}, bf16[128,256]{1,0:T(8,128)(2,1)S(1)}, u32[]{:S(2)}, u32[]{:S(2)}) collective-permute-start(bf16[128,256]{1,0:T(8,128)(2,1)S(1)} %pick.4), channel_id=1, source_target_pairs={{0,16},{8,24},{16,0},{24,8},{1,17},{9,25},{17,1},{25,9},{2,18},{10... | collective-permute-start | bytes 196616 | tf_op jit(solution)/shard_map/ppermute | solution.py:376
  9.0 10.8 %copy-start = (bf16[512,512]{1,0:T(8,128)(2,1)S(1)}, bf16[512,512]{1,0:T(8,128)(2,1)}, u32[]{:S(2)}) copy-start(bf16[512,512]{1,0:T(8,128)(2,1)} %constant.8.clone.refs_7_.inv_ref) | copy-start | bytes 1572868
  9.0 12.2 %collective-permute-start.5 = (bf16[128,256]{1,0:T(8,128)(2,1)S(1)}, bf16[128,256]{1,0:T(8,128)(2,1)S(1)}, u32[]{:S(2)}, u32[]{:S(2)}) collective-permute-start(bf16[128,256]{1,0:T(8,128)(2,1)S(1)} %pick.5), channel_id=1, source_target_pairs={{0,24},{8,16},{16,8},{24,0},{1,25},{9,17},{17,9},{25,1},{2,26},{10... | collective-permute-start | bytes 196616 | tf_op jit(solution)/shard_map/ppermute | solution.py:376
  13.6 7.8 %collective-permute-start.3 = (bf16[128,256]{1,0:T(8,128)(2,1)S(1)}, bf16[128,256]{1,0:T(8,128)(2,1)S(1)}, u32[]{:S(2)}, u32[]{:S(2)}) collective-permute-start(bf16[128,256]{1,0:T(8,128)(2,1)S(1)} %pick.3), channel_id=1, source_target_pairs={{0,8},{8,0},{16,24},{24,16},{1,9},{9,1},{17,25},{25,17},{2,10},{10... | collective-permute-start | bytes 196616 | tf_op jit(solution)/shard_map/ppermute | solution.py:376
  21.0 9.3 %copy-start.5 = (bf16[512,256]{1,0:T(8,128)(2,1)S(1)}, bf16[512,256]{1,0:T(8,128)(2,1)}, u32[]{:S(2)}) copy-start(bf16[512,256]{1,0:T(8,128)(2,1)} %cot_ref.1) | copy-start | bytes 786436
  21.0 1.6 %collective-permute-start.9 = (f32[1,256]{1,0:T(1,128)S(1)}, f32[1,256]{1,0:T(1,128)S(1)}, u32[]{:S(2)}, u32[]{:S(2)}) collective-permute-start(f32[1,256]{1,0:T(1,128)S(1)} %get-tuple-element.36.refs_6_), channel_id=1, source_target_pairs={{0,1},{1,0},{2,3},{3,2},{4,5},{5,4},{6,7},{7,6},{8,9},{9,8},{10,11... | collective-permute-start | bytes 3080 | tf_op jit(solution)/shard_map/ppermute | solution.py:376
  22.6 5.1 %collective-permute-start.10 = (f32[1,256]{1,0:T(1,128)S(1)}, f32[1,256]{1,0:T(1,128)S(1)}, u32[]{:S(2)}, u32[]{:S(2)}) collective-permute-start(f32[1,256]{1,0:T(1,128)S(1)} %max.6), channel_id=1, source_target_pairs={{0,2},{1,3},{2,0},{3,1},{4,6},{5,7},{6,4},{7,5},{8,10},{9,11},{10,... | collective-permute-start | bytes 3080 | tf_op jit(solution)/shard_map/ppermute | solution.py:376
  24.2 7.3 %collective-permute-start.6 = (bf16[128,256]{1,0:T(8,128)(2,1)S(1)}, bf16[128,256]{1,0:T(8,128)(2,1)S(1)}, u32[]{:S(2)}, u32[]{:S(2)}) collective-permute-start(bf16[128,256]{1,0:T(8,128)(2,1)S(1)} %get-tuple-element.38), channel_id=1, source_target_pairs={{0,8},{8,0},{16,24},{24,16},{1,9},{9,1},{17,25},{25,17},{2,10},{10... | collective-permute-start | bytes 196616 | tf_op jit(solution)/shard_map/ppermute | solution.py:376
  25.7 5.8 %collective-permute-start.7 = (bf16[128,256]{1,0:T(8,128)(2,1)S(1)}, bf16[128,256]{1,0:T(8,128)(2,1)S(1)}, u32[]{:S(2)}, u32[]{:S(2)}) collective-permute-start(bf16[128,256]{1,0:T(8,128)(2,1)S(1)} %get-tuple-element.39), channel_id=1, source_target_pairs={{0,16},{8,24},{16,0},{24,8},{1,17},{9,25},{17,1},{25,9},{2,18},{10... | collective-permute-start | bytes 196616 | tf_op jit(solution)/shard_map/ppermute | solution.py:376
  26.5 5.2 %collective-permute-start.8 = (bf16[128,256]{1,0:T(8,128)(2,1)S(1)}, bf16[128,256]{1,0:T(8,128)(2,1)S(1)}, u32[]{:S(2)}, u32[]{:S(2)}) collective-permute-start(bf16[128,256]{1,0:T(8,128)(2,1)S(1)} %get-tuple-element.40), channel_id=1, source_target_pairs={{0,24},{8,16},{16,8},{24,0},{1,25},{9,17},{17,9},{25,1},{2,26},{10... | collective-permute-start | bytes 196616 | tf_op jit(solution)/shard_map/ppermute | solution.py:376
  27.7 4.8 %collective-permute-start.11 = (f32[1,256]{1,0:T(1,128)S(1)}, f32[1,256]{1,0:T(1,128)S(1)}, u32[]{:S(2)}, u32[]{:S(2)}) collective-permute-start(f32[1,256]{1,0:T(1,128)S(1)} %max.7.refs_4_), channel_id=1, source_target_pairs={{0,4},{1,5},{2,6},{3,7},{4,0},{5,1},{6,2},{7,3},{8,12},{9,13},{10,... | collective-permute-start | bytes 3080 | tf_op jit(solution)/shard_map/ppermute | solution.py:376

commit v6 on v5

--- a/solution.py
+++ b/solution.py
@@ -11,7 +11,7 @@
 from jax.sharding import PartitionSpec as P
 
 REACH_DIVISORS = (64, 32, 16, 4, 1)
-LOAD_MIB = 53.3
+LOAD_MIB = 53.5
 
 
 def cost(flops):
@@ -99,43 +99,63 @@
     return lax.div(lax.axis_index("ctx"), (n + 1) // 2)
 
 
-def load_kernel(parts, proj_hbm, cot_hbm, key_value_ref, query_cot_ref, proj, cot, key_sem, query_sem):
-    channels, span = cot.shape
-    rows = channels // parts
-    copies = []
-    for part in range(parts):
-        block = pl.ds(part * rows, rows)
-        copies.append(
-            (
-                pltpu.make_async_copy(proj_hbm.at[pl.ds(1, 2), block], proj.at[pl.ds(1, 2), block], key_sem.at[part]),
-                pltpu.make_async_copy(proj_hbm.at[0, block], proj.at[0, block], query_sem.at[part, 0]),
-                pltpu.make_async_copy(cot_hbm.at[block], cot.at[block], query_sem.at[part, 1]),
-            )
-        )
-        for copy in copies[-1]:
+def load_kernel(n, proj_hbm, cot_hbm, raw_ref, left, right, sems):
+    upper = top_bit(n)
+
+    def pair(first, second):
+        copies = [
+            pltpu.make_async_copy(first, left, sems.at[0]),
+            pltpu.make_async_copy(second, right, sems.at[1]),
+        ]
+        for copy in copies:
             copy.start()
-    for part in range(parts):
-        block = pl.ds(part * rows, rows)
-        copies[part][0].wait()
-        key_value_ref[block] = (proj[1, block].astype(F32) * proj[2, block].astype(F32)).astype(BF16)
-        copies[part][1].wait()
-        copies[part][2].wait()
-        query_cot_ref[block] = (cot[block].astype(F32) * proj[0, block].astype(F32)).astype(BF16)
-
-
-def prep_kernel(n, rows, key_value_ref, query_cot_ref, exp_ref, main_ref, rest_ref, *send_refs):
+        for copy in copies:
+            copy.wait()
+
+    @pl.when(upper == 0)
+    def _():
+        pair(proj_hbm.at[1], proj_hbm.at[2])
+
+    @pl.when(upper == 1)
+    def _():
+        pair(proj_hbm.at[0], cot_hbm)
+
+    raw_ref[...] = (left[...].astype(F32) * right[...].astype(F32)).astype(BF16)
+
+
+def exponents(exp_ref, pulled):
+    return jnp.where(pulled == 1, exp_ref[0], exp_ref[1] + exp_ref[2])
+
+
+def main_kernel(n, raw_ref, exp_ref, main_ref):
+    span = main_ref.shape[1]
+    main_ref[...] = (raw_ref[...].astype(F32) * block_scale(exponents(exp_ref, top_bit(n)), span)).astype(BF16)
+
+
+def rest_kernel(n, proj_ref, cot_ref, exp_ref, main_ref, rest_ref, *send_refs):
     me = lax.axis_index("ctx")
     upper = top_bit(n)
-    channels, span = main_ref.shape
-    lows = [lax.rem(lax.div(me, 2**bit), 2) for bit in range(len(send_refs))]
-    for first in range(0, channels, rows):
-        block = slice(first, first + rows)
-        mixed = (
-            key_value_ref[block].astype(F32) * block_scale(exp_ref[1, :, block] + exp_ref[2, :, block], span)
-        ).astype(BF16)
-        pulled = (query_cot_ref[block].astype(F32) * block_scale(exp_ref[0, :, block], span)).astype(BF16)
-        for ref, later in [(main_ref, upper), (rest_ref, 1 - upper), *zip(send_refs, lows)]:
-            ref[block] = jnp.where(later == 1, pulled, mixed)
+    span = main_ref.shape[1]
+    scale = block_scale(exponents(exp_ref, 1 - upper), span)
+
+    @pl.when(upper == 1)
+    def _():
+        rest_ref[...] = (proj_ref[1].astype(F32) * proj_ref[2].astype(F32) * scale).astype(BF16)
+
+    @pl.when(upper == 0)
+    def _():
+        rest_ref[...] = (cot_ref[...].astype(F32) * proj_ref[0].astype(F32) * scale).astype(BF16)
+
+    for bit, ref in enumerate(send_refs):
+        low = lax.rem(lax.div(me, 2**bit), 2)
+
+        @pl.when(low == upper)
+        def _():
+            ref[...] = main_ref[...]
+
+        @pl.when(low != upper)
+        def _():
+            ref[...] = rest_ref[...]
 
 
 def windows_kernel(
@@ -314,15 +334,15 @@
         copy.wait()
 
 
-def spread_kernel(n, *refs):
-    part_refs, (near_ref, taps_hbm, peak_ref, taps, taps_sem) = refs[:n], refs[n:]
+def spread_kernel(ks, *refs):
+    part_refs, (near_ref, taps_hbm, peak_ref, taps, taps_sem) = refs[: len(ks)], refs[len(ks) :]
     me = lax.axis_index("ctx")
     peak_ref[...] = near_ref[...]
     copies = []
-    for k in range(n):
+    for slot, k in enumerate(ks):
         block = jnp.bitwise_xor(me, k)
-        taps[block] = part_refs[k][...].astype(F32)
-        copies.append(pltpu.make_async_copy(taps.at[block], taps_hbm.at[block], taps_sem.at[k]))
+        taps[block] = part_refs[slot][...].astype(F32)
+        copies.append(pltpu.make_async_copy(taps.at[block], taps_hbm.at[block], taps_sem.at[slot]))
         copies[-1].start()
     for copy in copies:
         copy.wait()
@@ -346,7 +366,6 @@
     blocks = scale_exp.shape[2]
     bits = max(1, (n - 1).bit_length())
     rows = channels
-    parts = 2 if channels % 256 == 0 else 1
     share = channels // n
     shares = (n, share, span)
     high, low, inverse = (jnp.asarray(t) for t in fourier_tables(span))
@@ -378,22 +397,22 @@
     flat = shape((channels, span), BF16)
     part = shape((share, span), BF16)
     line = shape((1, span), F32)
-    raw = call(
-        functools.partial(load_kernel, parts),
+    (raw,) = call(
+        functools.partial(load_kernel, n),
         "load",
         [hbm] * 2,
-        [flat] * 2,
+        [flat],
         mib=LOAD_MIB,
         scratch_shapes=[
-            pltpu.VMEM((3, channels, span), BF16),
             pltpu.VMEM((channels, span), BF16),
-            pltpu.SemaphoreType.DMA((parts,)),
-            pltpu.SemaphoreType.DMA((parts, 2)),
+            pltpu.VMEM((channels, span), BF16),
+            pltpu.SemaphoreType.DMA((2,)),
         ],
     )(proj, cotangent)
-    main, rest, *sends = call(
-        functools.partial(prep_kernel, n, rows), "prep", [vmem] * 3, [flat] * (1 + bits)
-    )(*raw, exps)
+    (main,) = call(functools.partial(main_kernel, n), "main", [vmem] * 2, [flat])(raw, exps)
+    rest, *sends = call(functools.partial(rest_kernel, n), "rest", [vmem] * 4, [flat] * bits)(
+        proj, cotangent, exps, main
+    )
     sends.append(main)
     first = [swap(sends[k.bit_length() - 1], "ctx", k) for k in range(1, n)]
 
@@ -449,6 +468,7 @@
         peak = jnp.maximum(peak, far)
         far = swap(peak, "ch", hop)
         hop *= 2
+    order = [*range(2, n), 1]
     parts_out = [swap(x, "ctx", k + 1) for k, x in enumerate(parts_out)]
     (gradients,) = call(
         functools.partial(grads_kernel, seq_len),
@@ -459,13 +479,13 @@
         scratch_shapes=[pltpu.VMEM((3, channels, span), BF16), pltpu.SemaphoreType.DMA((3,))],
     )(deq, cotangent, conv, acc, inverse)
     filter_grad, peak = call(
-        functools.partial(spread_kernel, n),
+        functools.partial(spread_kernel, (0, *order)),
         "spread",
         [vmem] * (n + 1),
         [shape(shares, F32), line],
         out_specs=[hbm, vmem],
         scratch_shapes=[pltpu.VMEM(shares, F32), pltpu.SemaphoreType.DMA((n,))],
-    )(own_part, *parts_out, peak)
+    )(own_part, *[parts_out[k - 1] for k in order], peak)
     scaled_out, peak = call(scale_kernel, "scale", [vmem] * 3, [flat, line])(response, peak, far)
     return (scaled_out, peak.reshape(span), gradients, filter_grad.reshape(channels, span))
 

time: 33.4 us -> 33 us (0.988)
  waiting for transfers between devices: 4.22 us -> 3.63 us
    ppermute x12, waiting for transfers between devices: 4.22 us -> 3.63 us  [swap(): lax.ppermute(value, axis, [(j, j ^ k) for j in range(lax.axis_size(axis))])]
    pallas_call x3 -> x4, Pallas kernels: 2.55 us -> 2.7 us  [the longest x1 1.2 us: body(): call(functools.partial(load_kernel, n), 'load', [hbm] * 2, [flat], mib=LO...]
  transfers between devices with their start and end apart: 12 -> 12, of which waited for: 5 -> 4; matrix products, arithmetic and copies ran while one was open for 0% -> 0% of each run, Pallas kernels for 24% -> 25%
where the time goes in v6:
time: 33 us; the launch traced here: 32.9 us
  starting transfers between devices  17.9 us (54%)
  Pallas kernels  10.5 us (32%)
  waiting for transfers between devices  3.63 us (11%)
  between operations  0.84 us (3%)
    ppermute x12, starting transfers between devices, swap(): lax.ppermute(value, axis, [(j, j ^ k) for j in range(lax.axis_size(axis))])  17.9 us
    ppermute x12, waiting for transfers between devices, swap(): lax.ppermute(value, axis, [(j, j ^ k) for j in range(lax.axis_size(axis))])  3.63 us
    pallas_call x1, Pallas kernels, body(): call(functools.partial(windows_kernel, n, rows), 'windows', [vmem] * 10,...  3.58 us
    pallas_call x1, Pallas kernels, body(): call(functools.partial(load_kernel, n), 'load', [hbm] * 2, [flat], mib=LO...  1.2 us
    pallas_call x1, Pallas kernels, body(): call(functools.partial(grads_kernel, seq_len), 'grads', [vmem] * 5, [shap...  1.18 us
    pallas_call x1, Pallas kernels, body(): call(functools.partial(conv_kernel, n, seq_len), 'conv', [vmem] * (2 * n)...  1.17 us
    pallas_call x1, Pallas kernels, body(): call(functools.partial(taps_kernel, n, seq_len), 'taps', [vmem] * (2 * n...  1.09 us
    pallas_call x1, Pallas kernels, body(): call(functools.partial(spread_kernel, (0, *order)), 'spread', [vmem] * (n...  0.84 us
  transfers between devices with their start and end apart: 12, of which 4 were waited for; matrix products, arithmetic and copies ran while one was open for 0% of the time, Pallas kernels for 25%

profile of v6, /device:TPU:0, one launch (start us, length us, event | category | flops | bytes accessed | tf_op | source)
XLA Modules:
  0.0 32.9 jit_solution(16574193827212176100)
XLA Ops:
  0.7 1.2 %load.1.raw_ref = bf16[512,256]{1,0:T(8,128)(2,1)S(1)} custom-call(bf16[3,512,256]{2,1,0:T(8,128)(2,1)} %proj_ref.3, bf16[512,256]{1,0:T(8,128)(2,1)} %cot_ref.3), custom_call_target="tpu_custom_call" | custom-call | flops 1000000000 | bytes 1000000 | tf_op jit(solution)/shard_map/load/pallas_call | solution.py:400
  1.9 0.0 copy-start.1
  1.9 0.0 copy-start.3
  1.9 0.0 copy-start.5
  1.9 0.0 copy-start.7
  1.9 0.0 copy-start.8
  1.9 0.3 main.1.main_ref
  2.2 4.0 %collective-permute-start.2 = (bf16[512,256]{1,0:T(8,128)(2,1)S(1)}, bf16[512,256]{1,0:T(8,128)(2,1)S(1)}, u32[]{:S(2)}, u32[]{:S(2)}) collective-permute-start(bf16[512,256]{1,0:T(8,128)(2,1)S(1)} %main.1.main_ref), channel_id=1, source_target_pairs={{0,24},{8,16},{16,8},{24,0},{1,25},{9,17},{17,9},{25,1},{2,26},{10... | collective-permute-start | bytes 786440 | tf_op jit(solution)/shard_map/ppermute | solution.py:395
  6.2 0.4 %rest.1 = (bf16[512,256]{1,0:T(8,128)(2,1)S(1)}, bf16[512,256]{1,0:T(8,128)(2,1)S(1)}) custom-call(bf16[3,512,256]{2,1,0:T(8,128)(2,1)S(1)} %copy-done.2, bf16[512,256]{1,0:T(8,128)(2,1)S(1)} %copy-done.4, s32[3,2,512]{2,1,0:T(2,128)S(1)} %bitcast.23, bf16[512,256]{1,0:T(8,128)(2,1)S(1)} %main.1.main_ref), custom_call_target="tpu_custom_call" | custom-call | tf_op jit(solution)/shard_map/rest/pallas_call | solution.py:413
  6.6 0.6 %collective-permute-start = (bf16[512,256]{1,0:T(8,128)(2,1)S(1)}, bf16[512,256]{1,0:T(8,128)(2,1)S(1)}, u32[]{:S(2)}, u32[]{:S(2)}) collective-permute-start(bf16[512,256]{1,0:T(8,128)(2,1)S(1)} %get-tuple-element.23), channel_id=1, source_target_pairs={{0,8},{8,0},{16,24},{24,16},{1,9},{9,1},{17,25},{25,17},{2,10},{10... | collective-permute-start | bytes 786440 | tf_op jit(solution)/shard_map/ppermute | solution.py:395
  7.2 0.1 collective-permute-start.1
  7.3 2.0 %collective-permute-start.4 = (bf16[128,256]{1,0:T(8,128)(2,1)S(1)}, bf16[128,256]{1,0:T(8,128)(2,1)S(1)}, u32[]{:S(2)}, u32[]{:S(2)}) collective-permute-start(bf16[128,256]{1,0:T(8,128)(2,1)S(1)} %pick.4), channel_id=1, source_target_pairs={{0,16},{8,24},{16,0},{24,8},{1,17},{9,25},{17,1},{25,9},{2,18},{10... | collective-permute-start | bytes 196616 | tf_op jit(solution)/shard_map/ppermute | solution.py:395
  9.2 1.5 %collective-permute-start.5 = (bf16[128,256]{1,0:T(8,128)(2,1)S(1)}, bf16[128,256]{1,0:T(8,128)(2,1)S(1)}, u32[]{:S(2)}, u32[]{:S(2)}) collective-permute-start(bf16[128,256]{1,0:T(8,128)(2,1)S(1)} %pick.5), channel_id=1, source_target_pairs={{0,24},{8,16},{16,8},{24,0},{1,25},{9,17},{17,9},{25,1},{2,26},{10... | collective-permute-start | bytes 196616 | tf_op jit(solution)/shard_map/ppermute | solution.py:395
  10.7 2.6 %collective-permute-done.2.recv_ref.refs_0_ = bf16[512,256]{1,0:T(8,128)(2,1)S(1)} collective-permute-done((bf16[512,256]{1,0:T(8,128)(2,1)S(1)}, bf16[512,256]{1,0:T(8,128)(2,1)S(1)}, u32[]{:S(2)}, u32[]{:S(2)}) %collective-permute-start.2) | collective-permute-done | bytes 262176 | tf_op jit(solution)/shard_map/ppermute | solution.py:395
  13.4 2.0 %collective-permute-start.3 = (bf16[128,256]{1,0:T(8,128)(2,1)S(1)}, bf16[128,256]{1,0:T(8,128)(2,1)S(1)}, u32[]{:S(2)}, u32[]{:S(2)}) collective-permute-start(bf16[128,256]{1,0:T(8,128)(2,1)S(1)} %pick.3), channel_id=1, source_target_pairs={{0,8},{8,0},{16,24},{24,16},{1,9},{9,1},{17,25},{25,17},{2,10},{10... | collective-permute-start | bytes 196616 | tf_op jit(solution)/shard_map/ppermute | solution.py:395
  15.4 3.6 %windows.1 = (bf16[3,512,256]{2,1,0:T(8,128)(2,1)S(1)}, f32[2,512,512]{2,1,0:T(8,128)S(1)}, bf16[512,512]{1,0:T(8,128)(2,1)S(1)}, bf16[512,512]{1,0:T(8,128)(2,1)S(1)}) custom-call(bf16[3,512,256]{2,1,0:T(8,128)(2,1)S(1)} %copy-done.2, s32[3,2,512]{2,1,0:T(2,128)S(1)} %bitcast.24, bf16[512,1024]{1,0:T(8,128)(2,1)S(1)} %copy-done.3, s32[1,512]{1,0:T(1,128)S(1)} %bitcast.25, ...), custom_call_target="tpu_custom_call" | custom-call | tf_op jit(solution)/shard_map/windows/pallas_call | solution.py:427
  19.0 0.6 %collective-permute-done.refs_0_ = bf16[512,256]{1,0:T(8,128)(2,1)S(1)} collective-permute-done((bf16[512,256]{1,0:T(8,128)(2,1)S(1)}, bf16[512,256]{1,0:T(8,128)(2,1)S(1)}, u32[]{:S(2)}, u32[]{:S(2)}) %collective-permute-start) | collective-permute-done | bytes 262176 | tf_op jit(solution)/shard_map/ppermute | solution.py:395
  19.6 1.2 %conv.1 = (f32[2,512,512]{2,1,0:T(8,128)S(1)}, f32[512,256]{1,0:T(8,128)S(1)}, f32[512,256]{1,0:T(8,128)S(1)}, f32[1,256]{1,0:T(1,128)S(1)}) custom-call(bf16[512,256]{1,0:T(8,128)(2,1)S(1)} %collective-permute-done.refs_0_, bf16[512,256]{1,0:T(8,128)(2,1)S(1)} %collective-permute-done.1.refs_1_, ...), custom_call_target="tpu_custom_call", output_to_operand_aliasing={{0}: (4, {})} | custom-call | tf_op jit(solution)/shard_map/conv/pallas_call | solution.py:440
  20.7 0.1 collective-permute-start.9
  20.8 0.1 collective-permute-done.4.refs_4_
  20.9 0.3 collective-permute-done.3.refs_3_
  21.2 1.1 %taps.1 = (bf16[128,256]{1,0:T(8,128)(2,1)S(1)}, bf16[128,256]{1,0:T(8,128)(2,1)S(1)}, bf16[128,256]{1,0:T(8,128)(2,1)S(1)}, bf16[128,256]{1,0:T(8,128)(2,1)S(1)}, f32[1,256]{1,0:T(1,128)S(1)}) custom-call(bf16[4,128,256]{2,1,0:T(8,128)(2,1)S(1)} %bitcast.14, bf16[4,128,256]{2,1,0:T(8,128)(2,1)S(1)} %bitcast.18, s32[4,1,128]{2,1,0:T(1,128)S(1)} %bitcast.26, ...), custom_call_target="tpu_custom_call" | custom-call | tf_op jit(solution)/shard_map/taps/pallas_call | solution.py:449
  22.3 1.6 %collective-permute-start.10 = (f32[1,256]{1,0:T(1,128)S(1)}, f32[1,256]{1,0:T(1,128)S(1)}, u32[]{:S(2)}, u32[]{:S(2)}) collective-permute-start(f32[1,256]{1,0:T(1,128)S(1)} %max.6), channel_id=1, source_target_pairs={{0,2},{1,3},{2,0},{3,1},{4,6},{5,7},{6,4},{7,5},{8,10},{9,11},{10,... | collective-permute-start | bytes 3080 | tf_op jit(solution)/shard_map/ppermute | solution.py:395
  24.0 1.4 %collective-permute-start.6 = (bf16[128,256]{1,0:T(8,128)(2,1)S(1)}, bf16[128,256]{1,0:T(8,128)(2,1)S(1)}, u32[]{:S(2)}, u32[]{:S(2)}) collective-permute-start(bf16[128,256]{1,0:T(8,128)(2,1)S(1)} %get-tuple-element.32), channel_id=1, source_target_pairs={{0,16},{8,24},{16,0},{24,8},{1,17},{9,25},{17,1},{25,9},{2,18},{10... | collective-permute-start | bytes 196616 | tf_op jit(solution)/shard_map/ppermute | solution.py:395
  25.4 1.5 %collective-permute-start.7 = (bf16[128,256]{1,0:T(8,128)(2,1)S(1)}, bf16[128,256]{1,0:T(8,128)(2,1)S(1)}, u32[]{:S(2)}, u32[]{:S(2)}) collective-permute-start(bf16[128,256]{1,0:T(8,128)(2,1)S(1)} %get-tuple-element.33), channel_id=1, source_target_pairs={{0,24},{8,16},{16,8},{24,0},{1,25},{9,17},{17,9},{25,1},{2,26},{10... | collective-permute-start | bytes 196616 | tf_op jit(solution)/shard_map/ppermute | solution.py:395
  26.9 0.5 %collective-permute-start.8 = (bf16[128,256]{1,0:T(8,128)(2,1)S(1)}, bf16[128,256]{1,0:T(8,128)(2,1)S(1)}, u32[]{:S(2)}, u32[]{:S(2)}) collective-permute-start(bf16[128,256]{1,0:T(8,128)(2,1)S(1)} %get-tuple-element.34), channel_id=1, source_target_pairs={{0,8},{8,0},{16,24},{24,16},{1,9},{9,1},{17,25},{25,17},{2,10},{10... | collective-permute-start | bytes 196616 | tf_op jit(solution)/shard_map/ppermute | solution.py:395
  27.5 2.6 %collective-permute-start.11 = (f32[1,256]{1,0:T(1,128)S(1)}, f32[1,256]{1,0:T(1,128)S(1)}, u32[]{:S(2)}, u32[]{:S(2)}) collective-permute-start(f32[1,256]{1,0:T(1,128)S(1)} %max.7.refs_4_), channel_id=1, source_target_pairs={{0,4},{1,5},{2,6},{3,7},{4,0},{5,1},{6,2},{7,3},{8,12},{9,13},{10,... | collective-permute-start | bytes 3080 | tf_op jit(solution)/shard_map/ppermute | solution.py:395
  30.1 1.2 %grads.1 = bf16[3,512,256]{2,1,0:T(8,128)(2,1)} custom-call(bf16[3,512,256]{2,1,0:T(8,128)(2,1)S(1)} %get-tuple-element.28.refs_5_.deq_ref, bf16[512,256]{1,0:T(8,128)(2,1)S(1)} %copy-done.4, f32[512,256]{1,0:T(8,128)S(1)} %get-tuple-element.39.conv_ref, f32[2,512,512]{2,1,0:T(8,128)S(1)} %get-tuple-element.40.acc_ref, bf16[512,512]{1,0:T(8,128)(2,1)S(1)} %copy-done), custom_call_target="tpu_custom_call" | custom-call | flops 1000000000 | bytes 1000000 | tf_op jit(solution)/shard_map/grads/pallas_call | solution.py:473
  31.3 0.0 collective-permute-done.7.refs_2_
  31.3 0.0 collective-permute-done.8.refs_3_
  31.3 0.8 %spread.1 = (f32[4,128,256]{2,1,0:T(8,128)}, f32[1,256]{1,0:T(1,128)S(1)}) custom-call(bf16[128,256]{1,0:T(8,128)(2,1)S(1)} %get-tuple-element.31.refs_0_, bf16[128,256]{1,0:T(8,128)(2,1)S(1)} %collective-permute-done.6.refs_1_, bf16[128,256]{1,0:T(8,128)(2,1)S(1)} %collective-permute-done.7.refs_2_, bf16[128,256]{1,0:T(8,128)(2,1)S(1)} %collective-permute-done.8.refs_3_, ...), custom_call_target="tpu_custom_call" | custom-call | tf_op jit(solution)/shard_map/spread/pallas_call | solution.py:481
  32.1 0.7 %scale.1 = (bf16[512,256]{1,0:T(8,128)(2,1)}, f32[1,256]{1,0:T(1,128)}) custom-call(f32[512,256]{1,0:T(8,128)S(1)} %get-tuple-element.29.resp_ref, f32[1,256]{1,0:T(1,128)S(1)} %get-tuple-element.36.near_ref, f32[1,256]{1,0:T(1,128)S(1)} %collective-permute-done.11.far_ref), custom_call_target="tpu_custom_call" | custom-call | flops 1000000000 | bytes 1000000 | tf_op jit(solution)/shard_map/scale/pallas_call | solution.py:489
  (24 shorter events, 0.1 us)
Async XLA Ops:
  0.6 5.6 %copy-start.4 = (bf16[512,256]{1,0:T(8,128)(2,1)S(1)}, bf16[512,256]{1,0:T(8,128)(2,1)}, u32[]{:S(2)}) copy-start(bf16[512,256]{1,0:T(8,128)(2,1)} %cot_ref.3) | copy-start | bytes 786436
  0.6 5.6 %copy-start.2 = (bf16[3,512,256]{2,1,0:T(8,128)(2,1)S(1)}, bf16[3,512,256]{2,1,0:T(8,128)(2,1)}, u32[]{:S(2)}) copy-start(bf16[3,512,256]{2,1,0:T(8,128)(2,1)} %proj_ref.3) | copy-start | bytes 2359300
  0.7 1.3 %copy-start.6 = (s32[3,512,2]{1,2,0:T(2,128)S(1)}, s32[3,512,2]{1,2,0:T(2,128)}, u32[]{:S(2)}) copy-start(s32[3,512,2]{1,2,0:T(2,128)} %param.10) | copy-start | bytes 36868
  1.9 13.5 %copy-start.1 = (bf16[512,512]{1,0:T(8,128)(2,1)S(1)}, bf16[512,512]{1,0:T(8,128)(2,1)}, u32[]{:S(2)}) copy-start(bf16[512,512]{1,0:T(8,128)(2,1)} %constant.6.clone.high_ref.refs_6_) | copy-start | bytes 1572868
  1.9 13.5 %copy-start.3 = (bf16[512,1024]{1,0:T(8,128)(2,1)S(1)}, bf16[512,1024]{1,0:T(8,128)(2,1)}, u32[]{:S(2)}) copy-start(bf16[512,1024]{1,0:T(8,128)(2,1)} %filt_ref.1) | copy-start | bytes 3145732
  1.9 13.5 %copy-start.5 = (bf16[512,512]{1,0:T(8,128)(2,1)S(1)}, bf16[512,512]{1,0:T(8,128)(2,1)}, u32[]{:S(2)}) copy-start(bf16[512,512]{1,0:T(8,128)(2,1)} %constant.7.clone.low_ref) | copy-start | bytes 1572868
  1.9 13.5 %copy-start.7 = (s32[512]{0:T(512)S(1)}, s32[512]{0:T(512)}, u32[]{:S(2)}) copy-start(s32[512]{0:T(512)} %param.12) | copy-start | bytes 6148
  1.9 13.5 %copy-start.8 = (f32[512]{0:T(512)S(1)}, f32[512]{0:T(512)}, u32[]{:S(2)}) copy-start(f32[512]{0:T(512)} %param.13) | copy-start | bytes 6148
  2.2 11.1 %collective-permute-start.2 = (bf16[512,256]{1,0:T(8,128)(2,1)S(1)}, bf16[512,256]{1,0:T(8,128)(2,1)S(1)}, u32[]{:S(2)}, u32[]{:S(2)}) collective-permute-start(bf16[512,256]{1,0:T(8,128)(2,1)S(1)} %main.1.main_ref), channel_id=1, source_target_pairs={{0,24},{8,16},{16,8},{24,0},{1,25},{9,17},{17,9},{25,1},{2,26},{10... | collective-permute-start | bytes 786440 | tf_op jit(solution)/shard_map/ppermute | solution.py:395
  6.6 13.0 %collective-permute-start = (bf16[512,256]{1,0:T(8,128)(2,1)S(1)}, bf16[512,256]{1,0:T(8,128)(2,1)S(1)}, u32[]{:S(2)}, u32[]{:S(2)}) collective-permute-start(bf16[512,256]{1,0:T(8,128)(2,1)S(1)} %get-tuple-element.23), channel_id=1, source_target_pairs={{0,8},{8,0},{16,24},{24,16},{1,9},{9,1},{17,25},{25,17},{2,10},{10... | collective-permute-start | bytes 786440 | tf_op jit(solution)/shard_map/ppermute | solution.py:395
  7.2 12.4 %collective-permute-start.1 = (bf16[512,256]{1,0:T(8,128)(2,1)S(1)}, bf16[512,256]{1,0:T(8,128)(2,1)S(1)}, u32[]{:S(2)}, u32[]{:S(2)}) collective-permute-start(bf16[512,256]{1,0:T(8,128)(2,1)S(1)} %main.1.main_ref), channel_id=1, source_target_pairs={{0,16},{8,24},{16,0},{24,8},{1,17},{9,25},{17,1},{25,9},{2,18},{10... | collective-permute-start | bytes 786440 | tf_op jit(solution)/shard_map/ppermute | solution.py:395
  7.3 13.7 %collective-permute-start.4 = (bf16[128,256]{1,0:T(8,128)(2,1)S(1)}, bf16[128,256]{1,0:T(8,128)(2,1)S(1)}, u32[]{:S(2)}, u32[]{:S(2)}) collective-permute-start(bf16[128,256]{1,0:T(8,128)(2,1)S(1)} %pick.4), channel_id=1, source_target_pairs={{0,16},{8,24},{16,0},{24,8},{1,17},{9,25},{17,1},{25,9},{2,18},{10... | collective-permute-start | bytes 196616 | tf_op jit(solution)/shard_map/ppermute | solution.py:395
  9.2 10.3 %copy-start = (bf16[512,512]{1,0:T(8,128)(2,1)S(1)}, bf16[512,512]{1,0:T(8,128)(2,1)}, u32[]{:S(2)}) copy-start(bf16[512,512]{1,0:T(8,128)(2,1)} %constant.8.clone.refs_7_.inv_ref) | copy-start | bytes 1572868
  9.2 11.7 %collective-permute-start.5 = (bf16[128,256]{1,0:T(8,128)(2,1)S(1)}, bf16[128,256]{1,0:T(8,128)(2,1)S(1)}, u32[]{:S(2)}, u32[]{:S(2)}) collective-permute-start(bf16[128,256]{1,0:T(8,128)(2,1)S(1)} %pick.5), channel_id=1, source_target_pairs={{0,24},{8,16},{16,8},{24,0},{1,25},{9,17},{17,9},{25,1},{2,26},{10... | collective-permute-start | bytes 196616 | tf_op jit(solution)/shard_map/ppermute | solution.py:395
  13.4 7.8 %collective-permute-start.3 = (bf16[128,256]{1,0:T(8,128)(2,1)S(1)}, bf16[128,256]{1,0:T(8,128)(2,1)S(1)}, u32[]{:S(2)}, u32[]{:S(2)}) collective-permute-start(bf16[128,256]{1,0:T(8,128)(2,1)S(1)} %pick.3), channel_id=1, source_target_pairs={{0,8},{8,0},{16,24},{24,16},{1,9},{9,1},{17,25},{25,17},{2,10},{10... | collective-permute-start | bytes 196616 | tf_op jit(solution)/shard_map/ppermute | solution.py:395
  20.7 1.6 %collective-permute-start.9 = (f32[1,256]{1,0:T(1,128)S(1)}, f32[1,256]{1,0:T(1,128)S(1)}, u32[]{:S(2)}, u32[]{:S(2)}) collective-permute-start(f32[1,256]{1,0:T(1,128)S(1)} %get-tuple-element.30.refs_6_), channel_id=1, source_target_pairs={{0,1},{1,0},{2,3},{3,2},{4,5},{5,4},{6,7},{7,6},{8,9},{9,8},{10,11... | collective-permute-start | bytes 3080 | tf_op jit(solution)/shard_map/ppermute | solution.py:395
  22.3 5.1 %collective-permute-start.10 = (f32[1,256]{1,0:T(1,128)S(1)}, f32[1,256]{1,0:T(1,128)S(1)}, u32[]{:S(2)}, u32[]{:S(2)}) collective-permute-start(f32[1,256]{1,0:T(1,128)S(1)} %max.6), channel_id=1, source_target_pairs={{0,2},{1,3},{2,0},{3,1},{4,6},{5,7},{6,4},{7,5},{8,10},{9,11},{10,... | collective-permute-start | bytes 3080 | tf_op jit(solution)/shard_map/ppermute | solution.py:395
  24.0 7.3 %collective-permute-start.6 = (bf16[128,256]{1,0:T(8,128)(2,1)S(1)}, bf16[128,256]{1,0:T(8,128)(2,1)S(1)}, u32[]{:S(2)}, u32[]{:S(2)}) collective-permute-start(bf16[128,256]{1,0:T(8,128)(2,1)S(1)} %get-tuple-element.32), channel_id=1, source_target_pairs={{0,16},{8,24},{16,0},{24,8},{1,17},{9,25},{17,1},{25,9},{2,18},{10... | collective-permute-start | bytes 196616 | tf_op jit(solution)/shard_map/ppermute | solution.py:395
  25.4 5.8 %collective-permute-start.7 = (bf16[128,256]{1,0:T(8,128)(2,1)S(1)}, bf16[128,256]{1,0:T(8,128)(2,1)S(1)}, u32[]{:S(2)}, u32[]{:S(2)}) collective-permute-start(bf16[128,256]{1,0:T(8,128)(2,1)S(1)} %get-tuple-element.33), channel_id=1, source_target_pairs={{0,24},{8,16},{16,8},{24,0},{1,25},{9,17},{17,9},{25,1},{2,26},{10... | collective-permute-start | bytes 196616 | tf_op jit(solution)/shard_map/ppermute | solution.py:395
  26.9 4.3 %collective-permute-start.8 = (bf16[128,256]{1,0:T(8,128)(2,1)S(1)}, bf16[128,256]{1,0:T(8,128)(2,1)S(1)}, u32[]{:S(2)}, u32[]{:S(2)}) collective-permute-start(bf16[128,256]{1,0:T(8,128)(2,1)S(1)} %get-tuple-element.34), channel_id=1, source_target_pairs={{0,8},{8,0},{16,24},{24,16},{1,9},{9,1},{17,25},{25,17},{2,10},{10... | collective-permute-start | bytes 196616 | tf_op jit(solution)/shard_map/ppermute | solution.py:395
  27.5 4.7 %collective-permute-start.11 = (f32[1,256]{1,0:T(1,128)S(1)}, f32[1,256]{1,0:T(1,128)S(1)}, u32[]{:S(2)}, u32[]{:S(2)}) collective-permute-start(f32[1,256]{1,0:T(1,128)S(1)} %max.7.refs_4_), channel_id=1, source_target_pairs={{0,4},{1,5},{2,6},{3,7},{4,0},{5,1},{6,2},{7,3},{8,12},{9,13},{10,... | collective-permute-start | bytes 3080 | tf_op jit(solution)/shard_map/ppermute | solution.py:395

commit v7 on v6

--- a/solution.py
+++ b/solution.py
@@ -316,9 +316,13 @@
         out_ref[...] = rest_ref[other]
 
 
-def grads_kernel(seq_len, deq_ref, cot_ref, conv_ref, acc_ref, inv_ref, grad_hbm, grad, grad_sem):
-    span = cot_ref.shape[1]
-    fscale = 1.0 / math.sqrt(seq_len)
+def back_kernel(seq_len, acc_ref, inv_ref, near_ref, out_ref, peak_ref):
+    peak_ref[...] = near_ref[...]
+    span = out_ref.shape[1]
+    out_ref[...] = mm(acc_ref[1].astype(BF16), inv_ref[:, :span]) * (1.0 / math.sqrt(seq_len))
+
+
+def grads_kernel(deq_ref, cot_ref, conv_ref, back_ref, grad_hbm, grad, grad_sem):
     copies = []
 
     def send(slot, value):
@@ -327,7 +331,7 @@
         copies[-1].start()
 
     send(0, cot_ref[...].astype(F32) * conv_ref[...])
-    grad_mixed = mm(acc_ref[1].astype(BF16), inv_ref[:, :span]) * fscale
+    grad_mixed = back_ref[...]
     send(1, grad_mixed * deq_ref[2].astype(F32))
     send(2, grad_mixed * deq_ref[1].astype(F32))
     for copy in copies:
@@ -446,6 +450,12 @@
     )(*[first[k - 1] for k in others(n)], *wins, base, deq, high, inverse)
 
     far = swap(peak, "ch", 1)
+    back, peak = call(
+        functools.partial(back_kernel, seq_len),
+        "back",
+        [vmem] * 3,
+        [shape((channels, span), F32), line],
+    )(acc, inverse, peak)
     own_part, *parts_out, peak = call(
         functools.partial(taps_kernel, n, seq_len),
         "taps",
@@ -471,13 +481,13 @@
     order = [*range(2, n), 1]
     parts_out = [swap(x, "ctx", k + 1) for k, x in enumerate(parts_out)]
     (gradients,) = call(
-        functools.partial(grads_kernel, seq_len),
+        grads_kernel,
         "grads",
-        [vmem] * 5,
+        [vmem] * 4,
         [shape((3, channels, span), BF16)],
         out_specs=[hbm],
         scratch_shapes=[pltpu.VMEM((3, channels, span), BF16), pltpu.SemaphoreType.DMA((3,))],
-    )(deq, cotangent, conv, acc, inverse)
+    )(deq, cotangent, conv, back)
     filter_grad, peak = call(
         functools.partial(spread_kernel, (0, *order)),
         "spread",

time: 33 us -> 33 us (level)
    pallas_call x1 -> x2, Pallas kernels: 1.18 us -> 1.25 us  [the longest x1 0.95 us: body(): call(grads_kernel, 'grads', [vmem] * 4, [shape((3, channels, span), BF16)...]
where the time goes in v7:
time: 33 us; the launch traced here: 32.8 us
  starting transfers between devices  17.9 us (54%)
  Pallas kernels  10.6 us (32%)
  waiting for transfers between devices  3.47 us (11%)
  between operations  0.85 us (3%)
    ppermute x12, starting transfers between devices, swap(): lax.ppermute(value, axis, [(j, j ^ k) for j in range(lax.axis_size(axis))])  17.9 us
    pallas_call x1, Pallas kernels, body(): call(functools.partial(windows_kernel, n, rows), 'windows', [vmem] * 10,...  3.58 us
    ppermute x12, waiting for transfers between devices, swap(): lax.ppermute(value, axis, [(j, j ^ k) for j in range(lax.axis_size(axis))])  3.47 us
    pallas_call x1, Pallas kernels, body(): call(functools.partial(load_kernel, n), 'load', [hbm] * 2, [flat], mib=LO...  1.2 us
    pallas_call x1, Pallas kernels, body(): call(functools.partial(conv_kernel, n, seq_len), 'conv', [vmem] * (2 * n)...  1.17 us
    pallas_call x1, Pallas kernels, body(): call(functools.partial(taps_kernel, n, seq_len), 'taps', [vmem] * (2 * n...  1.09 us
    pallas_call x1, Pallas kernels, body(): call(grads_kernel, 'grads', [vmem] * 4, [shape((3, channels, span), BF16)...  0.95 us
    pallas_call x1, Pallas kernels, body(): call(functools.partial(spread_kernel, (0, *order)), 'spread', [vmem] * (n...  0.84 us
  transfers between devices with their start and end apart: 12, of which 4 were waited for; matrix products, arithmetic and copies ran while one was open for 0% of the time, Pallas kernels for 25%

profile of v7, /device:TPU:0, one launch (start us, length us, event | category | flops | bytes accessed | tf_op | source)
XLA Modules:
  0.0 32.8 jit_solution(16569412544651822734)
XLA Ops:
  0.7 1.2 %load.1.raw_ref = bf16[512,256]{1,0:T(8,128)(2,1)S(1)} custom-call(bf16[3,512,256]{2,1,0:T(8,128)(2,1)} %proj_ref.3, bf16[512,256]{1,0:T(8,128)(2,1)} %cot_ref.3), custom_call_target="tpu_custom_call" | custom-call | flops 1000000000 | bytes 1000000 | tf_op jit(solution)/shard_map/load/pallas_call | solution.py:404
  1.9 0.0 copy-start
  1.9 0.0 copy-start.3
  1.9 0.0 copy-start.4
  1.9 0.0 copy-start.7
  1.9 0.0 copy-start.8
  1.9 0.3 main.1.main_ref
  2.2 4.0 %collective-permute-start.2 = (bf16[512,256]{1,0:T(8,128)(2,1)S(1)}, bf16[512,256]{1,0:T(8,128)(2,1)S(1)}, u32[]{:S(2)}, u32[]{:S(2)}) collective-permute-start(bf16[512,256]{1,0:T(8,128)(2,1)S(1)} %main.1.main_ref), channel_id=1, source_target_pairs={{0,24},{8,16},{16,8},{24,0},{1,25},{9,17},{17,9},{25,1},{2,26},{10... | collective-permute-start | bytes 786440 | tf_op jit(solution)/shard_map/ppermute | solution.py:399
  6.2 0.4 %rest.1 = (bf16[512,256]{1,0:T(8,128)(2,1)S(1)}, bf16[512,256]{1,0:T(8,128)(2,1)S(1)}) custom-call(bf16[3,512,256]{2,1,0:T(8,128)(2,1)S(1)} %copy-done.2, bf16[512,256]{1,0:T(8,128)(2,1)S(1)} %copy-done.5, s32[3,2,512]{2,1,0:T(2,128)S(1)} %bitcast.23, bf16[512,256]{1,0:T(8,128)(2,1)S(1)} %main.1.main_ref), custom_call_target="tpu_custom_call" | custom-call | tf_op jit(solution)/shard_map/rest/pallas_call | solution.py:417
  6.6 0.6 %collective-permute-start = (bf16[512,256]{1,0:T(8,128)(2,1)S(1)}, bf16[512,256]{1,0:T(8,128)(2,1)S(1)}, u32[]{:S(2)}, u32[]{:S(2)}) collective-permute-start(bf16[512,256]{1,0:T(8,128)(2,1)S(1)} %get-tuple-element.25), channel_id=1, source_target_pairs={{0,8},{8,0},{16,24},{24,16},{1,9},{9,1},{17,25},{25,17},{2,10},{10... | collective-permute-start | bytes 786440 | tf_op jit(solution)/shard_map/ppermute | solution.py:399
  7.2 0.1 collective-permute-start.1
  7.3 2.0 %collective-permute-start.4 = (bf16[128,256]{1,0:T(8,128)(2,1)S(1)}, bf16[128,256]{1,0:T(8,128)(2,1)S(1)}, u32[]{:S(2)}, u32[]{:S(2)}) collective-permute-start(bf16[128,256]{1,0:T(8,128)(2,1)S(1)} %pick.4), channel_id=1, source_target_pairs={{0,16},{8,24},{16,0},{24,8},{1,17},{9,25},{17,1},{25,9},{2,18},{10... | collective-permute-start | bytes 196616 | tf_op jit(solution)/shard_map/ppermute | solution.py:399
  9.2 1.5 %collective-permute-start.5 = (bf16[128,256]{1,0:T(8,128)(2,1)S(1)}, bf16[128,256]{1,0:T(8,128)(2,1)S(1)}, u32[]{:S(2)}, u32[]{:S(2)}) collective-permute-start(bf16[128,256]{1,0:T(8,128)(2,1)S(1)} %pick.5), channel_id=1, source_target_pairs={{0,24},{8,16},{16,8},{24,0},{1,25},{9,17},{17,9},{25,1},{2,26},{10... | collective-permute-start | bytes 196616 | tf_op jit(solution)/shard_map/ppermute | solution.py:399
  10.7 2.6 %collective-permute-done.2.recv_ref.refs_0_ = bf16[512,256]{1,0:T(8,128)(2,1)S(1)} collective-permute-done((bf16[512,256]{1,0:T(8,128)(2,1)S(1)}, bf16[512,256]{1,0:T(8,128)(2,1)S(1)}, u32[]{:S(2)}, u32[]{:S(2)}) %collective-permute-start.2) | collective-permute-done | bytes 262176 | tf_op jit(solution)/shard_map/ppermute | solution.py:399
  13.4 2.0 %collective-permute-start.3 = (bf16[128,256]{1,0:T(8,128)(2,1)S(1)}, bf16[128,256]{1,0:T(8,128)(2,1)S(1)}, u32[]{:S(2)}, u32[]{:S(2)}) collective-permute-start(bf16[128,256]{1,0:T(8,128)(2,1)S(1)} %pick.3), channel_id=1, source_target_pairs={{0,8},{8,0},{16,24},{24,16},{1,9},{9,1},{17,25},{25,17},{2,10},{10... | collective-permute-start | bytes 196616 | tf_op jit(solution)/shard_map/ppermute | solution.py:399
  15.4 3.6 %windows.1 = (bf16[3,512,256]{2,1,0:T(8,128)(2,1)S(1)}, f32[2,512,512]{2,1,0:T(8,128)S(1)}, bf16[512,512]{1,0:T(8,128)(2,1)S(1)}, bf16[512,512]{1,0:T(8,128)(2,1)S(1)}) custom-call(bf16[3,512,256]{2,1,0:T(8,128)(2,1)S(1)} %copy-done.2, s32[3,2,512]{2,1,0:T(2,128)S(1)} %bitcast.24, bf16[512,1024]{1,0:T(8,128)(2,1)S(1)} %copy-done.3, s32[1,512]{1,0:T(1,128)S(1)} %bitcast.25, ...), custom_call_target="tpu_custom_call" | custom-call | tf_op jit(solution)/shard_map/windows/pallas_call | solution.py:431
  19.0 0.6 %collective-permute-done.refs_0_ = bf16[512,256]{1,0:T(8,128)(2,1)S(1)} collective-permute-done((bf16[512,256]{1,0:T(8,128)(2,1)S(1)}, bf16[512,256]{1,0:T(8,128)(2,1)S(1)}, u32[]{:S(2)}, u32[]{:S(2)}) %collective-permute-start) | collective-permute-done | bytes 262176 | tf_op jit(solution)/shard_map/ppermute | solution.py:399
  19.6 1.2 %conv.1 = (f32[2,512,512]{2,1,0:T(8,128)S(1)}, f32[512,256]{1,0:T(8,128)S(1)}, f32[512,256]{1,0:T(8,128)S(1)}, f32[1,256]{1,0:T(1,128)S(1)}) custom-call(bf16[512,256]{1,0:T(8,128)(2,1)S(1)} %collective-permute-done.refs_0_, bf16[512,256]{1,0:T(8,128)(2,1)S(1)} %collective-permute-done.1.refs_1_, ...), custom_call_target="tpu_custom_call", output_to_operand_aliasing={{0}: (4, {})} | custom-call | tf_op jit(solution)/shard_map/conv/pallas_call | solution.py:444
  20.7 0.1 collective-permute-start.9
  20.8 0.3 back.1
  21.2 0.1 collective-permute-done.3.refs_3_
  21.2 1.1 %taps.1 = (bf16[128,256]{1,0:T(8,128)(2,1)S(1)}, bf16[128,256]{1,0:T(8,128)(2,1)S(1)}, bf16[128,256]{1,0:T(8,128)(2,1)S(1)}, bf16[128,256]{1,0:T(8,128)(2,1)S(1)}, f32[1,256]{1,0:T(1,128)S(1)}) custom-call(bf16[4,128,256]{2,1,0:T(8,128)(2,1)S(1)} %bitcast.14, bf16[4,128,256]{2,1,0:T(8,128)(2,1)S(1)} %bitcast.18, s32[4,1,128]{2,1,0:T(1,128)S(1)} %bitcast.26, ...), custom_call_target="tpu_custom_call" | custom-call | tf_op jit(solution)/shard_map/taps/pallas_call | solution.py:459
  22.3 1.6 %collective-permute-start.10 = (f32[1,256]{1,0:T(1,128)S(1)}, f32[1,256]{1,0:T(1,128)S(1)}, u32[]{:S(2)}, u32[]{:S(2)}) collective-permute-start(f32[1,256]{1,0:T(1,128)S(1)} %max.6), channel_id=1, source_target_pairs={{0,2},{1,3},{2,0},{3,1},{4,6},{5,7},{6,4},{7,5},{8,10},{9,11},{10,... | collective-permute-start | bytes 3080 | tf_op jit(solution)/shard_map/ppermute | solution.py:399
  24.0 1.4 %collective-permute-start.6 = (bf16[128,256]{1,0:T(8,128)(2,1)S(1)}, bf16[128,256]{1,0:T(8,128)(2,1)S(1)}, u32[]{:S(2)}, u32[]{:S(2)}) collective-permute-start(bf16[128,256]{1,0:T(8,128)(2,1)S(1)} %get-tuple-element.36), channel_id=1, source_target_pairs={{0,16},{8,24},{16,0},{24,8},{1,17},{9,25},{17,1},{25,9},{2,18},{10... | collective-permute-start | bytes 196616 | tf_op jit(solution)/shard_map/ppermute | solution.py:399
  25.4 1.5 %collective-permute-start.7 = (bf16[128,256]{1,0:T(8,128)(2,1)S(1)}, bf16[128,256]{1,0:T(8,128)(2,1)S(1)}, u32[]{:S(2)}, u32[]{:S(2)}) collective-permute-start(bf16[128,256]{1,0:T(8,128)(2,1)S(1)} %get-tuple-element.37), channel_id=1, source_target_pairs={{0,24},{8,16},{16,8},{24,0},{1,25},{9,17},{17,9},{25,1},{2,26},{10... | collective-permute-start | bytes 196616 | tf_op jit(solution)/shard_map/ppermute | solution.py:399
  26.9 0.5 %collective-permute-start.8 = (bf16[128,256]{1,0:T(8,128)(2,1)S(1)}, bf16[128,256]{1,0:T(8,128)(2,1)S(1)}, u32[]{:S(2)}, u32[]{:S(2)}) collective-permute-start(bf16[128,256]{1,0:T(8,128)(2,1)S(1)} %get-tuple-element.38), channel_id=1, source_target_pairs={{0,8},{8,0},{16,24},{24,16},{1,9},{9,1},{17,25},{25,17},{2,10},{10... | collective-permute-start | bytes 196616 | tf_op jit(solution)/shard_map/ppermute | solution.py:399
  27.5 2.6 %collective-permute-start.11 = (f32[1,256]{1,0:T(1,128)S(1)}, f32[1,256]{1,0:T(1,128)S(1)}, u32[]{:S(2)}, u32[]{:S(2)}) collective-permute-start(f32[1,256]{1,0:T(1,128)S(1)} %max.7.refs_4_), channel_id=1, source_target_pairs={{0,4},{1,5},{2,6},{3,7},{4,0},{5,1},{6,2},{7,3},{8,12},{9,13},{10,... | collective-permute-start | bytes 3080 | tf_op jit(solution)/shard_map/ppermute | solution.py:399
  30.1 0.9 %grads.1 = bf16[3,512,256]{2,1,0:T(8,128)(2,1)} custom-call(bf16[3,512,256]{2,1,0:T(8,128)(2,1)S(1)} %get-tuple-element.30.refs_5_.deq_ref, bf16[512,256]{1,0:T(8,128)(2,1)S(1)} %copy-done.5, f32[512,256]{1,0:T(8,128)S(1)} %get-tuple-element.43.conv_ref, f32[512,256]{1,0:T(8,128)S(1)} %get-tuple-element.44.back_ref), custom_call_target="tpu_custom_call" | custom-call | flops 1000000000 | bytes 1000000 | tf_op jit(solution)/shard_map/grads/pallas_call | solution.py:483
  31.0 0.0 collective-permute-done.7.refs_2_
  31.1 0.1 collective-permute-done.8.refs_3_
  31.2 0.8 %spread.1 = (f32[4,128,256]{2,1,0:T(8,128)}, f32[1,256]{1,0:T(1,128)S(1)}) custom-call(bf16[128,256]{1,0:T(8,128)(2,1)S(1)} %get-tuple-element.35.refs_0_, bf16[128,256]{1,0:T(8,128)(2,1)S(1)} %collective-permute-done.6.refs_1_, bf16[128,256]{1,0:T(8,128)(2,1)S(1)} %collective-permute-done.7.refs_2_, bf16[128,256]{1,0:T(8,128)(2,1)S(1)} %collective-permute-done.8.refs_3_, ...), custom_call_target="tpu_custom_call" | custom-call | tf_op jit(solution)/shard_map/spread/pallas_call | solution.py:491
  32.1 0.7 %scale.1 = (bf16[512,256]{1,0:T(8,128)(2,1)}, f32[1,256]{1,0:T(1,128)}) custom-call(f32[512,256]{1,0:T(8,128)S(1)} %get-tuple-element.31.resp_ref, f32[1,256]{1,0:T(1,128)S(1)} %get-tuple-element.40.near_ref, f32[1,256]{1,0:T(1,128)S(1)} %collective-permute-done.11.far_ref), custom_call_target="tpu_custom_call" | custom-call | flops 1000000000 | bytes 1000000 | tf_op jit(solution)/shard_map/scale/pallas_call | solution.py:499
  (25 shorter events, 0.1 us)
Async XLA Ops:
  0.6 5.6 %copy-start.5 = (bf16[512,256]{1,0:T(8,128)(2,1)S(1)}, bf16[512,256]{1,0:T(8,128)(2,1)}, u32[]{:S(2)}) copy-start(bf16[512,256]{1,0:T(8,128)(2,1)} %cot_ref.3) | copy-start | bytes 786436
  0.6 5.6 %copy-start.2 = (bf16[3,512,256]{2,1,0:T(8,128)(2,1)S(1)}, bf16[3,512,256]{2,1,0:T(8,128)(2,1)}, u32[]{:S(2)}) copy-start(bf16[3,512,256]{2,1,0:T(8,128)(2,1)} %proj_ref.3) | copy-start | bytes 2359300
  0.7 1.3 %copy-start.6 = (s32[3,512,2]{1,2,0:T(2,128)S(1)}, s32[3,512,2]{1,2,0:T(2,128)}, u32[]{:S(2)}) copy-start(s32[3,512,2]{1,2,0:T(2,128)} %param.10) | copy-start | bytes 36868
  1.9 13.5 %copy-start = (bf16[512,512]{1,0:T(8,128)(2,1)S(1)}, bf16[512,512]{1,0:T(8,128)(2,1)}, u32[]{:S(2)}) copy-start(bf16[512,512]{1,0:T(8,128)(2,1)} %constant.6.clone.high_ref.refs_6_) | copy-start | bytes 1572868
  1.9 13.5 %copy-start.3 = (bf16[512,1024]{1,0:T(8,128)(2,1)S(1)}, bf16[512,1024]{1,0:T(8,128)(2,1)}, u32[]{:S(2)}) copy-start(bf16[512,1024]{1,0:T(8,128)(2,1)} %filt_ref.1) | copy-start | bytes 3145732
  1.9 13.5 %copy-start.4 = (bf16[512,512]{1,0:T(8,128)(2,1)S(1)}, bf16[512,512]{1,0:T(8,128)(2,1)}, u32[]{:S(2)}) copy-start(bf16[512,512]{1,0:T(8,128)(2,1)} %constant.7.clone.low_ref) | copy-start | bytes 1572868
  1.9 13.5 %copy-start.7 = (s32[512]{0:T(512)S(1)}, s32[512]{0:T(512)}, u32[]{:S(2)}) copy-start(s32[512]{0:T(512)} %param.12) | copy-start | bytes 6148
  1.9 13.5 %copy-start.8 = (f32[512]{0:T(512)S(1)}, f32[512]{0:T(512)}, u32[]{:S(2)}) copy-start(f32[512]{0:T(512)} %param.13) | copy-start | bytes 6148
  2.2 11.1 %collective-permute-start.2 = (bf16[512,256]{1,0:T(8,128)(2,1)S(1)}, bf16[512,256]{1,0:T(8,128)(2,1)S(1)}, u32[]{:S(2)}, u32[]{:S(2)}) collective-permute-start(bf16[512,256]{1,0:T(8,128)(2,1)S(1)} %main.1.main_ref), channel_id=1, source_target_pairs={{0,24},{8,16},{16,8},{24,0},{1,25},{9,17},{17,9},{25,1},{2,26},{10... | collective-permute-start | bytes 786440 | tf_op jit(solution)/shard_map/ppermute | solution.py:399
  6.6 13.0 %collective-permute-start = (bf16[512,256]{1,0:T(8,128)(2,1)S(1)}, bf16[512,256]{1,0:T(8,128)(2,1)S(1)}, u32[]{:S(2)}, u32[]{:S(2)}) collective-permute-start(bf16[512,256]{1,0:T(8,128)(2,1)S(1)} %get-tuple-element.25), channel_id=1, source_target_pairs={{0,8},{8,0},{16,24},{24,16},{1,9},{9,1},{17,25},{25,17},{2,10},{10... | collective-permute-start | bytes 786440 | tf_op jit(solution)/shard_map/ppermute | solution.py:399
  7.2 12.4 %collective-permute-start.1 = (bf16[512,256]{1,0:T(8,128)(2,1)S(1)}, bf16[512,256]{1,0:T(8,128)(2,1)S(1)}, u32[]{:S(2)}, u32[]{:S(2)}) collective-permute-start(bf16[512,256]{1,0:T(8,128)(2,1)S(1)} %main.1.main_ref), channel_id=1, source_target_pairs={{0,16},{8,24},{16,0},{24,8},{1,17},{9,25},{17,1},{25,9},{2,18},{10... | collective-permute-start | bytes 786440 | tf_op jit(solution)/shard_map/ppermute | solution.py:399
  7.3 13.9 %collective-permute-start.4 = (bf16[128,256]{1,0:T(8,128)(2,1)S(1)}, bf16[128,256]{1,0:T(8,128)(2,1)S(1)}, u32[]{:S(2)}, u32[]{:S(2)}) collective-permute-start(bf16[128,256]{1,0:T(8,128)(2,1)S(1)} %pick.4), channel_id=1, source_target_pairs={{0,16},{8,24},{16,0},{24,8},{1,17},{9,25},{17,1},{25,9},{2,18},{10... | collective-permute-start | bytes 196616 | tf_op jit(solution)/shard_map/ppermute | solution.py:399
  9.2 10.3 %copy-start.1 = (bf16[512,512]{1,0:T(8,128)(2,1)S(1)}, bf16[512,512]{1,0:T(8,128)(2,1)}, u32[]{:S(2)}) copy-start(bf16[512,512]{1,0:T(8,128)(2,1)} %constant.8.clone.refs_7_.inv_ref) | copy-start | bytes 1572868
  9.2 11.9 %collective-permute-start.5 = (bf16[128,256]{1,0:T(8,128)(2,1)S(1)}, bf16[128,256]{1,0:T(8,128)(2,1)S(1)}, u32[]{:S(2)}, u32[]{:S(2)}) collective-permute-start(bf16[128,256]{1,0:T(8,128)(2,1)S(1)} %pick.5), channel_id=1, source_target_pairs={{0,24},{8,16},{16,8},{24,0},{1,25},{9,17},{17,9},{25,1},{2,26},{10... | collective-permute-start | bytes 196616 | tf_op jit(solution)/shard_map/ppermute | solution.py:399
  13.4 7.8 %collective-permute-start.3 = (bf16[128,256]{1,0:T(8,128)(2,1)S(1)}, bf16[128,256]{1,0:T(8,128)(2,1)S(1)}, u32[]{:S(2)}, u32[]{:S(2)}) collective-permute-start(bf16[128,256]{1,0:T(8,128)(2,1)S(1)} %pick.3), channel_id=1, source_target_pairs={{0,8},{8,0},{16,24},{24,16},{1,9},{9,1},{17,25},{25,17},{2,10},{10... | collective-permute-start | bytes 196616 | tf_op jit(solution)/shard_map/ppermute | solution.py:399
  20.7 1.6 %collective-permute-start.9 = (f32[1,256]{1,0:T(1,128)S(1)}, f32[1,256]{1,0:T(1,128)S(1)}, u32[]{:S(2)}, u32[]{:S(2)}) collective-permute-start(f32[1,256]{1,0:T(1,128)S(1)} %get-tuple-element.33.near_ref), channel_id=1, source_target_pairs={{0,1},{1,0},{2,3},{3,2},{4,5},{5,4},{6,7},{7,6},{8,9},{9,8},{10,11... | collective-permute-start | bytes 3080 | tf_op jit(solution)/shard_map/ppermute | solution.py:399
  22.3 5.1 %collective-permute-start.10 = (f32[1,256]{1,0:T(1,128)S(1)}, f32[1,256]{1,0:T(1,128)S(1)}, u32[]{:S(2)}, u32[]{:S(2)}) collective-permute-start(f32[1,256]{1,0:T(1,128)S(1)} %max.6), channel_id=1, source_target_pairs={{0,2},{1,3},{2,0},{3,1},{4,6},{5,7},{6,4},{7,5},{8,10},{9,11},{10,... | collective-permute-start | bytes 3080 | tf_op jit(solution)/shard_map/ppermute | solution.py:399
  24.0 7.0 %collective-permute-start.6 = (bf16[128,256]{1,0:T(8,128)(2,1)S(1)}, bf16[128,256]{1,0:T(8,128)(2,1)S(1)}, u32[]{:S(2)}, u32[]{:S(2)}) collective-permute-start(bf16[128,256]{1,0:T(8,128)(2,1)S(1)} %get-tuple-element.36), channel_id=1, source_target_pairs={{0,16},{8,24},{16,0},{24,8},{1,17},{9,25},{17,1},{25,9},{2,18},{10... | collective-permute-start | bytes 196616 | tf_op jit(solution)/shard_map/ppermute | solution.py:399
  25.4 5.6 %collective-permute-start.7 = (bf16[128,256]{1,0:T(8,128)(2,1)S(1)}, bf16[128,256]{1,0:T(8,128)(2,1)S(1)}, u32[]{:S(2)}, u32[]{:S(2)}) collective-permute-start(bf16[128,256]{1,0:T(8,128)(2,1)S(1)} %get-tuple-element.37), channel_id=1, source_target_pairs={{0,24},{8,16},{16,8},{24,0},{1,25},{9,17},{17,9},{25,1},{2,26},{10... | collective-permute-start | bytes 196616 | tf_op jit(solution)/shard_map/ppermute | solution.py:399
  26.9 4.3 %collective-permute-start.8 = (bf16[128,256]{1,0:T(8,128)(2,1)S(1)}, bf16[128,256]{1,0:T(8,128)(2,1)S(1)}, u32[]{:S(2)}, u32[]{:S(2)}) collective-permute-start(bf16[128,256]{1,0:T(8,128)(2,1)S(1)} %get-tuple-element.38), channel_id=1, source_target_pairs={{0,8},{8,0},{16,24},{24,16},{1,9},{9,1},{17,25},{25,17},{2,10},{10... | collective-permute-start | bytes 196616 | tf_op jit(solution)/shard_map/ppermute | solution.py:399
  27.5 4.6 %collective-permute-start.11 = (f32[1,256]{1,0:T(1,128)S(1)}, f32[1,256]{1,0:T(1,128)S(1)}, u32[]{:S(2)}, u32[]{:S(2)}) collective-permute-start(f32[1,256]{1,0:T(1,128)S(1)} %max.7.refs_4_), channel_id=1, source_target_pairs={{0,4},{1,5},{2,6},{3,7},{4,0},{5,1},{6,2},{7,3},{8,12},{9,13},{10,... | collective-permute-start | bytes 3080 | tf_op jit(solution)/shard_map/ppermute | solution.py:399

commit v8 on v7

--- a/solution.py
+++ b/solution.py
@@ -478,7 +478,7 @@
         peak = jnp.maximum(peak, far)
         far = swap(peak, "ch", hop)
         hop *= 2
-    order = [*range(2, n), 1]
+    order = [*range(n - 1, 0, -1)]
     parts_out = [swap(x, "ctx", k + 1) for k, x in enumerate(parts_out)]
     (gradients,) = call(
         grads_kernel,

time: 33 us -> 33 us (level)
  no operation moved by 1% of the time
where the time goes in v8:
time: 33 us; the launch traced here: 32.8 us
  starting transfers between devices  17.9 us (54%)
  Pallas kernels  10.6 us (32%)
  waiting for transfers between devices  3.46 us (10%)
  between operations  0.86 us (3%)
    ppermute x12, starting transfers between devices, swap(): lax.ppermute(value, axis, [(j, j ^ k) for j in range(lax.axis_size(axis))])  17.9 us
    pallas_call x1, Pallas kernels, body(): call(functools.partial(windows_kernel, n, rows), 'windows', [vmem] * 10,...  3.58 us
    ppermute x12, waiting for transfers between devices, swap(): lax.ppermute(value, axis, [(j, j ^ k) for j in range(lax.axis_size(axis))])  3.46 us
    pallas_call x1, Pallas kernels, body(): call(functools.partial(load_kernel, n), 'load', [hbm] * 2, [flat], mib=LO...  1.2 us
    pallas_call x1, Pallas kernels, body(): call(functools.partial(conv_kernel, n, seq_len), 'conv', [vmem] * (2 * n)...  1.17 us
    pallas_call x1, Pallas kernels, body(): call(functools.partial(taps_kernel, n, seq_len), 'taps', [vmem] * (2 * n...  1.09 us
    pallas_call x1, Pallas kernels, body(): call(grads_kernel, 'grads', [vmem] * 4, [shape((3, channels, span), BF16)...  0.95 us
    pallas_call x1, Pallas kernels, body(): call(functools.partial(spread_kernel, (0, *order)), 'spread', [vmem] * (n...  0.84 us
  transfers between devices with their start and end apart: 12, of which 4 were waited for; matrix products, arithmetic and copies ran while one was open for 0% of the time, Pallas kernels for 25%

profile of v8, /device:TPU:0, one launch (start us, length us, event | category | flops | bytes accessed | tf_op | source)
XLA Modules:
  0.0 32.8 jit_solution(3816074102347781227)
XLA Ops:
  0.7 1.2 %load.1.raw_ref = bf16[512,256]{1,0:T(8,128)(2,1)S(1)} custom-call(bf16[3,512,256]{2,1,0:T(8,128)(2,1)} %proj_ref.3, bf16[512,256]{1,0:T(8,128)(2,1)} %cot_ref.3), custom_call_target="tpu_custom_call" | custom-call | flops 1000000000 | bytes 1000000 | tf_op jit(solution)/shard_map/load/pallas_call | solution.py:404
  1.9 0.0 copy-start
  1.9 0.0 copy-start.3
  1.9 0.0 copy-start.4
  1.9 0.0 copy-start.7
  1.9 0.0 copy-start.8
  1.9 0.3 main.1.main_ref
  2.2 4.0 %collective-permute-start.2 = (bf16[512,256]{1,0:T(8,128)(2,1)S(1)}, bf16[512,256]{1,0:T(8,128)(2,1)S(1)}, u32[]{:S(2)}, u32[]{:S(2)}) collective-permute-start(bf16[512,256]{1,0:T(8,128)(2,1)S(1)} %main.1.main_ref), channel_id=1, source_target_pairs={{0,24},{8,16},{16,8},{24,0},{1,25},{9,17},{17,9},{25,1},{2,26},{10... | collective-permute-start | bytes 786440 | tf_op jit(solution)/shard_map/ppermute | solution.py:399
  6.2 0.4 %rest.1 = (bf16[512,256]{1,0:T(8,128)(2,1)S(1)}, bf16[512,256]{1,0:T(8,128)(2,1)S(1)}) custom-call(bf16[3,512,256]{2,1,0:T(8,128)(2,1)S(1)} %copy-done.2, bf16[512,256]{1,0:T(8,128)(2,1)S(1)} %copy-done.5, s32[3,2,512]{2,1,0:T(2,128)S(1)} %bitcast.23, bf16[512,256]{1,0:T(8,128)(2,1)S(1)} %main.1.main_ref), custom_call_target="tpu_custom_call" | custom-call | tf_op jit(solution)/shard_map/rest/pallas_call | solution.py:417
  6.6 0.6 %collective-permute-start = (bf16[512,256]{1,0:T(8,128)(2,1)S(1)}, bf16[512,256]{1,0:T(8,128)(2,1)S(1)}, u32[]{:S(2)}, u32[]{:S(2)}) collective-permute-start(bf16[512,256]{1,0:T(8,128)(2,1)S(1)} %get-tuple-element.25), channel_id=1, source_target_pairs={{0,8},{8,0},{16,24},{24,16},{1,9},{9,1},{17,25},{25,17},{2,10},{10... | collective-permute-start | bytes 786440 | tf_op jit(solution)/shard_map/ppermute | solution.py:399
  7.2 0.1 collective-permute-start.1
  7.3 2.0 %collective-permute-start.4 = (bf16[128,256]{1,0:T(8,128)(2,1)S(1)}, bf16[128,256]{1,0:T(8,128)(2,1)S(1)}, u32[]{:S(2)}, u32[]{:S(2)}) collective-permute-start(bf16[128,256]{1,0:T(8,128)(2,1)S(1)} %pick.4), channel_id=1, source_target_pairs={{0,16},{8,24},{16,0},{24,8},{1,17},{9,25},{17,1},{25,9},{2,18},{10... | collective-permute-start | bytes 196616 | tf_op jit(solution)/shard_map/ppermute | solution.py:399
  9.2 1.5 %collective-permute-start.5 = (bf16[128,256]{1,0:T(8,128)(2,1)S(1)}, bf16[128,256]{1,0:T(8,128)(2,1)S(1)}, u32[]{:S(2)}, u32[]{:S(2)}) collective-permute-start(bf16[128,256]{1,0:T(8,128)(2,1)S(1)} %pick.5), channel_id=1, source_target_pairs={{0,24},{8,16},{16,8},{24,0},{1,25},{9,17},{17,9},{25,1},{2,26},{10... | collective-permute-start | bytes 196616 | tf_op jit(solution)/shard_map/ppermute | solution.py:399
  10.7 2.6 %collective-permute-done.2.recv_ref.refs_0_ = bf16[512,256]{1,0:T(8,128)(2,1)S(1)} collective-permute-done((bf16[512,256]{1,0:T(8,128)(2,1)S(1)}, bf16[512,256]{1,0:T(8,128)(2,1)S(1)}, u32[]{:S(2)}, u32[]{:S(2)}) %collective-permute-start.2) | collective-permute-done | bytes 262176 | tf_op jit(solution)/shard_map/ppermute | solution.py:399
  13.4 2.0 %collective-permute-start.3 = (bf16[128,256]{1,0:T(8,128)(2,1)S(1)}, bf16[128,256]{1,0:T(8,128)(2,1)S(1)}, u32[]{:S(2)}, u32[]{:S(2)}) collective-permute-start(bf16[128,256]{1,0:T(8,128)(2,1)S(1)} %pick.3), channel_id=1, source_target_pairs={{0,8},{8,0},{16,24},{24,16},{1,9},{9,1},{17,25},{25,17},{2,10},{10... | collective-permute-start | bytes 196616 | tf_op jit(solution)/shard_map/ppermute | solution.py:399
  15.4 3.6 %windows.1 = (bf16[3,512,256]{2,1,0:T(8,128)(2,1)S(1)}, f32[2,512,512]{2,1,0:T(8,128)S(1)}, bf16[512,512]{1,0:T(8,128)(2,1)S(1)}, bf16[512,512]{1,0:T(8,128)(2,1)S(1)}) custom-call(bf16[3,512,256]{2,1,0:T(8,128)(2,1)S(1)} %copy-done.2, s32[3,2,512]{2,1,0:T(2,128)S(1)} %bitcast.24, bf16[512,1024]{1,0:T(8,128)(2,1)S(1)} %copy-done.3, s32[1,512]{1,0:T(1,128)S(1)} %bitcast.25, ...), custom_call_target="tpu_custom_call" | custom-call | tf_op jit(solution)/shard_map/windows/pallas_call | solution.py:431
  19.0 0.6 %collective-permute-done.refs_0_ = bf16[512,256]{1,0:T(8,128)(2,1)S(1)} collective-permute-done((bf16[512,256]{1,0:T(8,128)(2,1)S(1)}, bf16[512,256]{1,0:T(8,128)(2,1)S(1)}, u32[]{:S(2)}, u32[]{:S(2)}) %collective-permute-start) | collective-permute-done | bytes 262176 | tf_op jit(solution)/shard_map/ppermute | solution.py:399
  19.6 1.2 %conv.1 = (f32[2,512,512]{2,1,0:T(8,128)S(1)}, f32[512,256]{1,0:T(8,128)S(1)}, f32[512,256]{1,0:T(8,128)S(1)}, f32[1,256]{1,0:T(1,128)S(1)}) custom-call(bf16[512,256]{1,0:T(8,128)(2,1)S(1)} %collective-permute-done.refs_0_, bf16[512,256]{1,0:T(8,128)(2,1)S(1)} %collective-permute-done.1.refs_1_, ...), custom_call_target="tpu_custom_call", output_to_operand_aliasing={{0}: (4, {})} | custom-call | tf_op jit(solution)/shard_map/conv/pallas_call | solution.py:444
  20.7 0.1 collective-permute-start.9
  20.8 0.3 back.1
  21.1 0.0 collective-permute-done.5.refs_5_
  21.2 0.1 collective-permute-done.3.refs_3_
  21.2 1.1 %taps.1 = (bf16[128,256]{1,0:T(8,128)(2,1)S(1)}, bf16[128,256]{1,0:T(8,128)(2,1)S(1)}, bf16[128,256]{1,0:T(8,128)(2,1)S(1)}, bf16[128,256]{1,0:T(8,128)(2,1)S(1)}, f32[1,256]{1,0:T(1,128)S(1)}) custom-call(bf16[4,128,256]{2,1,0:T(8,128)(2,1)S(1)} %bitcast.14, bf16[4,128,256]{2,1,0:T(8,128)(2,1)S(1)} %bitcast.18, s32[4,1,128]{2,1,0:T(1,128)S(1)} %bitcast.26, ...), custom_call_target="tpu_custom_call" | custom-call | tf_op jit(solution)/shard_map/taps/pallas_call | solution.py:459
  22.3 1.6 %collective-permute-start.10 = (f32[1,256]{1,0:T(1,128)S(1)}, f32[1,256]{1,0:T(1,128)S(1)}, u32[]{:S(2)}, u32[]{:S(2)}) collective-permute-start(f32[1,256]{1,0:T(1,128)S(1)} %max.6), channel_id=1, source_target_pairs={{0,2},{1,3},{2,0},{3,1},{4,6},{5,7},{6,4},{7,5},{8,10},{9,11},{10,... | collective-permute-start | bytes 3080 | tf_op jit(solution)/shard_map/ppermute | solution.py:399
  24.0 2.4 %collective-permute-start.6 = (bf16[128,256]{1,0:T(8,128)(2,1)S(1)}, bf16[128,256]{1,0:T(8,128)(2,1)S(1)}, u32[]{:S(2)}, u32[]{:S(2)}) collective-permute-start(bf16[128,256]{1,0:T(8,128)(2,1)S(1)} %get-tuple-element.36), channel_id=1, source_target_pairs={{0,24},{8,16},{16,8},{24,0},{1,25},{9,17},{17,9},{25,1},{2,26},{10... | collective-permute-start | bytes 196616 | tf_op jit(solution)/shard_map/ppermute | solution.py:399
  26.4 0.6 %collective-permute-start.7 = (bf16[128,256]{1,0:T(8,128)(2,1)S(1)}, bf16[128,256]{1,0:T(8,128)(2,1)S(1)}, u32[]{:S(2)}, u32[]{:S(2)}) collective-permute-start(bf16[128,256]{1,0:T(8,128)(2,1)S(1)} %get-tuple-element.37), channel_id=1, source_target_pairs={{0,16},{8,24},{16,0},{24,8},{1,17},{9,25},{17,1},{25,9},{2,18},{10... | collective-permute-start | bytes 196616 | tf_op jit(solution)/shard_map/ppermute | solution.py:399
  26.9 0.5 %collective-permute-start.8 = (bf16[128,256]{1,0:T(8,128)(2,1)S(1)}, bf16[128,256]{1,0:T(8,128)(2,1)S(1)}, u32[]{:S(2)}, u32[]{:S(2)}) collective-permute-start(bf16[128,256]{1,0:T(8,128)(2,1)S(1)} %get-tuple-element.38), channel_id=1, source_target_pairs={{0,8},{8,0},{16,24},{24,16},{1,9},{9,1},{17,25},{25,17},{2,10},{10... | collective-permute-start | bytes 196616 | tf_op jit(solution)/shard_map/ppermute | solution.py:399
  27.5 2.6 %collective-permute-start.11 = (f32[1,256]{1,0:T(1,128)S(1)}, f32[1,256]{1,0:T(1,128)S(1)}, u32[]{:S(2)}, u32[]{:S(2)}) collective-permute-start(f32[1,256]{1,0:T(1,128)S(1)} %max.7.refs_4_), channel_id=1, source_target_pairs={{0,4},{1,5},{2,6},{3,7},{4,0},{5,1},{6,2},{7,3},{8,12},{9,13},{10,... | collective-permute-start | bytes 3080 | tf_op jit(solution)/shard_map/ppermute | solution.py:399
  30.1 0.9 %grads.1 = bf16[3,512,256]{2,1,0:T(8,128)(2,1)} custom-call(bf16[3,512,256]{2,1,0:T(8,128)(2,1)S(1)} %get-tuple-element.30.refs_5_.deq_ref, bf16[512,256]{1,0:T(8,128)(2,1)S(1)} %copy-done.5, f32[512,256]{1,0:T(8,128)S(1)} %get-tuple-element.43.conv_ref, f32[512,256]{1,0:T(8,128)S(1)} %get-tuple-element.44.back_ref), custom_call_target="tpu_custom_call" | custom-call | flops 1000000000 | bytes 1000000 | tf_op jit(solution)/shard_map/grads/pallas_call | solution.py:483
  31.0 0.2 collective-permute-done.8.refs_3_
  31.2 0.8 %spread.1 = (f32[4,128,256]{2,1,0:T(8,128)}, f32[1,256]{1,0:T(1,128)S(1)}) custom-call(bf16[128,256]{1,0:T(8,128)(2,1)S(1)} %get-tuple-element.35.refs_0_, bf16[128,256]{1,0:T(8,128)(2,1)S(1)} %collective-permute-done.6.refs_1_, bf16[128,256]{1,0:T(8,128)(2,1)S(1)} %collective-permute-done.7.refs_2_, bf16[128,256]{1,0:T(8,128)(2,1)S(1)} %collective-permute-done.8.refs_3_, ...), custom_call_target="tpu_custom_call" | custom-call | tf_op jit(solution)/shard_map/spread/pallas_call | solution.py:491
  32.1 0.7 %scale.1 = (bf16[512,256]{1,0:T(8,128)(2,1)}, f32[1,256]{1,0:T(1,128)}) custom-call(f32[512,256]{1,0:T(8,128)S(1)} %get-tuple-element.31.resp_ref, f32[1,256]{1,0:T(1,128)S(1)} %get-tuple-element.40.near_ref, f32[1,256]{1,0:T(1,128)S(1)} %collective-permute-done.11.far_ref), custom_call_target="tpu_custom_call" | custom-call | flops 1000000000 | bytes 1000000 | tf_op jit(solution)/shard_map/scale/pallas_call | solution.py:499
  (25 shorter events, 0.1 us)
Async XLA Ops:
  0.6 5.6 %copy-start.5 = (bf16[512,256]{1,0:T(8,128)(2,1)S(1)}, bf16[512,256]{1,0:T(8,128)(2,1)}, u32[]{:S(2)}) copy-start(bf16[512,256]{1,0:T(8,128)(2,1)} %cot_ref.3) | copy-start | bytes 786436
  0.6 5.6 %copy-start.2 = (bf16[3,512,256]{2,1,0:T(8,128)(2,1)S(1)}, bf16[3,512,256]{2,1,0:T(8,128)(2,1)}, u32[]{:S(2)}) copy-start(bf16[3,512,256]{2,1,0:T(8,128)(2,1)} %proj_ref.3) | copy-start | bytes 2359300
  0.7 1.3 %copy-start.6 = (s32[3,512,2]{1,2,0:T(2,128)S(1)}, s32[3,512,2]{1,2,0:T(2,128)}, u32[]{:S(2)}) copy-start(s32[3,512,2]{1,2,0:T(2,128)} %param.10) | copy-start | bytes 36868
  1.9 13.5 %copy-start = (bf16[512,512]{1,0:T(8,128)(2,1)S(1)}, bf16[512,512]{1,0:T(8,128)(2,1)}, u32[]{:S(2)}) copy-start(bf16[512,512]{1,0:T(8,128)(2,1)} %constant.6.clone.high_ref.refs_6_) | copy-start | bytes 1572868
  1.9 13.5 %copy-start.3 = (bf16[512,1024]{1,0:T(8,128)(2,1)S(1)}, bf16[512,1024]{1,0:T(8,128)(2,1)}, u32[]{:S(2)}) copy-start(bf16[512,1024]{1,0:T(8,128)(2,1)} %filt_ref.1) | copy-start | bytes 3145732
  1.9 13.5 %copy-start.4 = (bf16[512,512]{1,0:T(8,128)(2,1)S(1)}, bf16[512,512]{1,0:T(8,128)(2,1)}, u32[]{:S(2)}) copy-start(bf16[512,512]{1,0:T(8,128)(2,1)} %constant.7.clone.low_ref) | copy-start | bytes 1572868
  1.9 13.5 %copy-start.7 = (s32[512]{0:T(512)S(1)}, s32[512]{0:T(512)}, u32[]{:S(2)}) copy-start(s32[512]{0:T(512)} %param.12) | copy-start | bytes 6148
  1.9 13.5 %copy-start.8 = (f32[512]{0:T(512)S(1)}, f32[512]{0:T(512)}, u32[]{:S(2)}) copy-start(f32[512]{0:T(512)} %param.13) | copy-start | bytes 6148
  2.2 11.1 %collective-permute-start.2 = (bf16[512,256]{1,0:T(8,128)(2,1)S(1)}, bf16[512,256]{1,0:T(8,128)(2,1)S(1)}, u32[]{:S(2)}, u32[]{:S(2)}) collective-permute-start(bf16[512,256]{1,0:T(8,128)(2,1)S(1)} %main.1.main_ref), channel_id=1, source_target_pairs={{0,24},{8,16},{16,8},{24,0},{1,25},{9,17},{17,9},{25,1},{2,26},{10... | collective-permute-start | bytes 786440 | tf_op jit(solution)/shard_map/ppermute | solution.py:399
  6.6 13.0 %collective-permute-start = (bf16[512,256]{1,0:T(8,128)(2,1)S(1)}, bf16[512,256]{1,0:T(8,128)(2,1)S(1)}, u32[]{:S(2)}, u32[]{:S(2)}) collective-permute-start(bf16[512,256]{1,0:T(8,128)(2,1)S(1)} %get-tuple-element.25), channel_id=1, source_target_pairs={{0,8},{8,0},{16,24},{24,16},{1,9},{9,1},{17,25},{25,17},{2,10},{10... | collective-permute-start | bytes 786440 | tf_op jit(solution)/shard_map/ppermute | solution.py:399
  7.2 12.4 %collective-permute-start.1 = (bf16[512,256]{1,0:T(8,128)(2,1)S(1)}, bf16[512,256]{1,0:T(8,128)(2,1)S(1)}, u32[]{:S(2)}, u32[]{:S(2)}) collective-permute-start(bf16[512,256]{1,0:T(8,128)(2,1)S(1)} %main.1.main_ref), channel_id=1, source_target_pairs={{0,16},{8,24},{16,0},{24,8},{1,17},{9,25},{17,1},{25,9},{2,18},{10... | collective-permute-start | bytes 786440 | tf_op jit(solution)/shard_map/ppermute | solution.py:399
  7.3 13.9 %collective-permute-start.4 = (bf16[128,256]{1,0:T(8,128)(2,1)S(1)}, bf16[128,256]{1,0:T(8,128)(2,1)S(1)}, u32[]{:S(2)}, u32[]{:S(2)}) collective-permute-start(bf16[128,256]{1,0:T(8,128)(2,1)S(1)} %pick.4), channel_id=1, source_target_pairs={{0,16},{8,24},{16,0},{24,8},{1,17},{9,25},{17,1},{25,9},{2,18},{10... | collective-permute-start | bytes 196616 | tf_op jit(solution)/shard_map/ppermute | solution.py:399
  9.2 10.3 %copy-start.1 = (bf16[512,512]{1,0:T(8,128)(2,1)S(1)}, bf16[512,512]{1,0:T(8,128)(2,1)}, u32[]{:S(2)}) copy-start(bf16[512,512]{1,0:T(8,128)(2,1)} %constant.8.clone.refs_7_.inv_ref) | copy-start | bytes 1572868
  9.2 11.9 %collective-permute-start.5 = (bf16[128,256]{1,0:T(8,128)(2,1)S(1)}, bf16[128,256]{1,0:T(8,128)(2,1)S(1)}, u32[]{:S(2)}, u32[]{:S(2)}) collective-permute-start(bf16[128,256]{1,0:T(8,128)(2,1)S(1)} %pick.5), channel_id=1, source_target_pairs={{0,24},{8,16},{16,8},{24,0},{1,25},{9,17},{17,9},{25,1},{2,26},{10... | collective-permute-start | bytes 196616 | tf_op jit(solution)/shard_map/ppermute | solution.py:399
  13.4 7.8 %collective-permute-start.3 = (bf16[128,256]{1,0:T(8,128)(2,1)S(1)}, bf16[128,256]{1,0:T(8,128)(2,1)S(1)}, u32[]{:S(2)}, u32[]{:S(2)}) collective-permute-start(bf16[128,256]{1,0:T(8,128)(2,1)S(1)} %pick.3), channel_id=1, source_target_pairs={{0,8},{8,0},{16,24},{24,16},{1,9},{9,1},{17,25},{25,17},{2,10},{10... | collective-permute-start | bytes 196616 | tf_op jit(solution)/shard_map/ppermute | solution.py:399
  20.7 1.6 %collective-permute-start.9 = (f32[1,256]{1,0:T(1,128)S(1)}, f32[1,256]{1,0:T(1,128)S(1)}, u32[]{:S(2)}, u32[]{:S(2)}) collective-permute-start(f32[1,256]{1,0:T(1,128)S(1)} %get-tuple-element.33.near_ref), channel_id=1, source_target_pairs={{0,1},{1,0},{2,3},{3,2},{4,5},{5,4},{6,7},{7,6},{8,9},{9,8},{10,11... | collective-permute-start | bytes 3080 | tf_op jit(solution)/shard_map/ppermute | solution.py:399
  22.3 5.1 %collective-permute-start.10 = (f32[1,256]{1,0:T(1,128)S(1)}, f32[1,256]{1,0:T(1,128)S(1)}, u32[]{:S(2)}, u32[]{:S(2)}) collective-permute-start(f32[1,256]{1,0:T(1,128)S(1)} %max.6), channel_id=1, source_target_pairs={{0,2},{1,3},{2,0},{3,1},{4,6},{5,7},{6,4},{7,5},{8,10},{9,11},{10,... | collective-permute-start | bytes 3080 | tf_op jit(solution)/shard_map/ppermute | solution.py:399
  24.0 7.0 %collective-permute-start.6 = (bf16[128,256]{1,0:T(8,128)(2,1)S(1)}, bf16[128,256]{1,0:T(8,128)(2,1)S(1)}, u32[]{:S(2)}, u32[]{:S(2)}) collective-permute-start(bf16[128,256]{1,0:T(8,128)(2,1)S(1)} %get-tuple-element.36), channel_id=1, source_target_pairs={{0,24},{8,16},{16,8},{24,0},{1,25},{9,17},{17,9},{25,1},{2,26},{10... | collective-permute-start | bytes 196616 | tf_op jit(solution)/shard_map/ppermute | solution.py:399
  26.4 4.7 %collective-permute-start.7 = (bf16[128,256]{1,0:T(8,128)(2,1)S(1)}, bf16[128,256]{1,0:T(8,128)(2,1)S(1)}, u32[]{:S(2)}, u32[]{:S(2)}) collective-permute-start(bf16[128,256]{1,0:T(8,128)(2,1)S(1)} %get-tuple-element.37), channel_id=1, source_target_pairs={{0,16},{8,24},{16,0},{24,8},{1,17},{9,25},{17,1},{25,9},{2,18},{10... | collective-permute-start | bytes 196616 | tf_op jit(solution)/shard_map/ppermute | solution.py:399
  26.9 4.3 %collective-permute-start.8 = (bf16[128,256]{1,0:T(8,128)(2,1)S(1)}, bf16[128,256]{1,0:T(8,128)(2,1)S(1)}, u32[]{:S(2)}, u32[]{:S(2)}) collective-permute-start(bf16[128,256]{1,0:T(8,128)(2,1)S(1)} %get-tuple-element.38), channel_id=1, source_target_pairs={{0,8},{8,0},{16,24},{24,16},{1,9},{9,1},{17,25},{25,17},{2,10},{10... | collective-permute-start | bytes 196616 | tf_op jit(solution)/shard_map/ppermute | solution.py:399
  27.5 4.6 %collective-permute-start.11 = (f32[1,256]{1,0:T(1,128)S(1)}, f32[1,256]{1,0:T(1,128)S(1)}, u32[]{:S(2)}, u32[]{:S(2)}) collective-permute-start(f32[1,256]{1,0:T(1,128)S(1)} %max.7.refs_4_), channel_id=1, source_target_pairs={{0,4},{1,5},{2,6},{3,7},{4,0},{5,1},{6,2},{7,3},{8,12},{9,13},{10,... | collective-permute-start | bytes 3080 | tf_op jit(solution)/shard_map/ppermute | solution.py:399
